TPU v7x, 32 devices: a whole 2x2x4 slice. The times are simulated.
32 devices in a mesh: dp: 4 (over z), row: 4 (over x, core), col: 2 (over y).
Axes of the slice: x: 2, y: 2, z: 4, core: 2. Of those that a mesh axis runs over, the one named last changes fastest.
Arguments:
- residual_in: bfloat16 [4096, 2048], P(('dp', 'col'), 'row'), may hold values from -6 to 6
- attention_gain: bfloat16 [2048], P('row'), may hold values from 0.099609375 to 1.8984375
- query_weight: bfloat16 [2048, 2048], P('row', 'col'), may hold values from -0.125 to 0.125
- key_weight: bfloat16 [2048, 2048], P('row', 'col'), may hold values from -0.125 to 0.125
- value_weight: bfloat16 [2048, 2048], P('row', 'col'), may hold values from -0.125 to 0.125
- query_gain: bfloat16 [2048], P('col'), may hold values from 0.099609375 to 1.8984375
- key_gain: bfloat16 [2048], P('col'), may hold values from 0.099609375 to 1.8984375
- output_weight: bfloat16 [2048, 2048], P('col', 'row'), may hold values from -0.5 to 0.5
- expert_gain: bfloat16 [2048], P('row'), may hold values from 0.099609375 to 1.8984375
- router_weight: bfloat16 [2048, 32], P('row'), may hold values from -0.0625 to 0.0625
- gate_weight: bfloat16 [32, 2048, 1024], P(None, 'row', 'col'), may hold values from -0.125 to 0.125
- up_weight: bfloat16 [32, 2048, 1024], P(None, 'row', 'col'), may hold values from -0.125 to 0.125
- down_weight: bfloat16 [32, 1024, 2048], P(None, 'col', 'row'), may hold values from -2.5 to 2.5
- segments: int32 [4096], P('dp'), may hold values from 0 to 2, as said below
- routes: int32 [4096, 8], P('dp'), may hold values from 0 to 31, all different within a row; in each aligned block of 1024 rows (0 to 1023, 1024 to 2047, ...) at most 384 rows name the same one
- cotangent: bfloat16 [4096, 2048], P(('dp', 'col'), 'row'), may hold values from -6 to 6
Outputs:
- residual_out: bfloat16 [4096, 2048], P(('dp', 'col'), 'row')
- input_gradient: float32 [4096, 2048], P(('dp', 'col'), 'row')
- attention_gain_gradient: float32 [2048], P('row')
- query_weight_gradient: float32 [2048, 2048], P('row', 'col')
- key_weight_gradient: float32 [2048, 2048], P('row', 'col')
- value_weight_gradient: float32 [2048, 2048], P('row', 'col')
- query_gain_gradient: float32 [2048], P('col')
- key_gain_gradient: float32 [2048], P('col')
- output_weight_gradient: float32 [2048, 2048], P('col', 'row')
- expert_gain_gradient: float32 [2048], P('row')
- router_weight_gradient: float32 [2048, 32], P('row')
- gate_weight_gradient: float32 [32, 2048, 1024], P(None, 'row', 'col')
- up_weight_gradient: float32 [32, 2048, 1024], P(None, 'row', 'col')
- down_weight_gradient: float32 [32, 1024, 2048], P(None, 'col', 'row')
Inputs may be any that keep to these rules, and one draw needn't show every extreme that they name: `segments`: within each sequence the numbers never fall and start at 1; each sequence holds exactly 2 documents of 60 to 800 tokens, followed by a tail of 1 to 59 padding tokens that carry 0. In each data group's 1024 tokens (aligned blocks of rows) no expert is named by more than 384 routes, and in every draw some expert is named by exactly 384 of them.
All inputs are finite; a program needn't handle non-finite values.
Results may differ from a plain program's by a relative error of at most 0.018.
Values may be sent and summed in bfloat16 or wider, within the bound.
No kernel may reach another device: no remote copies, remote signals or barrier semaphores. Data moves between devices by JAX's collectives and lax.ppermute only.
A program may use at most 640 MiB of HBM per device.

v0:
```python
import jax
import jax.numpy as jnp
from jax import lax
from jax.sharding import PartitionSpec as P

D = 2048
HEAD_DIM = 128
MAX_LEN = 2048


EPSILON = 1e-05
NEGATIVE = -1e30


def total_rows(value):
    return lax.psum(value, "row")


def total_columns(value):
    return lax.psum(value, "col")


def gather_columns(value):
    return lax.all_gather(value, "col", axis=0, tiled=True)


def reduce_rows(value):
    return lax.psum_scatter(value, "row", scatter_dimension=1, tiled=True)


def gather_rows(value):
    return lax.all_gather(value, "row", axis=1, tiled=True)


def reduce_columns(value):
    return lax.psum_scatter(value, "col", scatter_dimension=0, tiled=True)


def expert_slots(routes, experts, capacity):
    flat_routes = routes.reshape(-1)
    route_count = flat_routes.shape[0]
    member = (flat_routes[:, None] == jnp.arange(experts, dtype=jnp.int32)[None, :]).astype(
        jnp.int32
    )
    before = jnp.cumsum(member, axis=0) - member
    slot_index = jnp.sum(before * member, axis=1)
    slot_table = jnp.full((experts, capacity), route_count, jnp.int32)
    slot_table = slot_table.at[flat_routes, slot_index].set(
        jnp.arange(route_count, dtype=jnp.int32)
    )
    filled = slot_table < route_count
    source = jnp.where(filled, slot_table, 0)
    position = flat_routes * capacity + slot_index
    return (source, filled, position)


def to_routes(expert_rows, position):
    flat_rows = expert_rows.reshape(
        expert_rows.shape[0] * expert_rows.shape[1], expert_rows.shape[2]
    )
    return jnp.take(flat_rows, position, axis=0)


def allowed_keys(query_segments, key_segments, query_places):
    key_places = jnp.arange(key_segments.shape[0], dtype=jnp.int32)
    return (query_segments[:, None] == key_segments[None, :]) & (
        key_places[None, :] <= query_places[:, None]
    )


def on_device(
    residual_in,
    attention_gain,
    query_weight,
    key_weight,
    value_weight,
    query_gain,
    key_gain,
    output_weight,
    expert_gain,
    router_weight,
    gate_weight,
    up_weight,
    down_weight,
    segments,
    routes,
    cotangent,
):
    row_count = lax.axis_size("row")
    row_index = lax.axis_index("row")
    column_count = lax.axis_size("col")
    column_index = lax.axis_index("col")
    local_tokens, width_part = residual_in.shape
    group_tokens = local_tokens * column_count
    shared = group_tokens // row_count
    head_part = query_weight.shape[1]
    heads_here = head_part // HEAD_DIM
    experts = gate_weight.shape[0]
    hidden_part = gate_weight.shape[2]
    top_count = routes.shape[1]
    sequence_length = min(MAX_LEN, group_tokens)
    sequence_count = group_tokens // sequence_length
    sequence_share = sequence_length // row_count
    capacity = group_tokens * top_count * 3 // (2 * experts)
    score_scale = HEAD_DIM ** (-0.5)
    empty_value = jnp.zeros((), jnp.bfloat16)
    residual = residual_in.astype(jnp.float32)
    first_scale = attention_gain.astype(jnp.float32)
    first_inverse = lax.rsqrt(total_rows(jnp.sum(residual * residual, axis=1)) / D + EPSILON)
    first_normed = (residual * first_inverse[:, None] * first_scale).astype(jnp.bfloat16)
    normed_group = gather_columns(first_normed)
    joint_weight = jnp.concatenate([query_weight, key_weight, value_weight], axis=1)
    joint_part = jnp.dot(normed_group, joint_weight, preferred_element_type=jnp.float32)
    joint_local = reduce_rows(joint_part.reshape(shared, row_count, 3 * head_part)).reshape(
        shared, 3 * head_part
    )
    query_raw = joint_local[:, :head_part]
    key_raw = joint_local[:, head_part : 2 * head_part]
    value_raw = joint_local[:, 2 * head_part :]
    square_sums = total_columns(
        jnp.stack([jnp.sum(query_raw * query_raw, axis=1), jnp.sum(key_raw * key_raw, axis=1)])
    )
    query_inverse = lax.rsqrt(square_sums[0] / D + EPSILON)
    key_inverse = lax.rsqrt(square_sums[1] / D + EPSILON)
    query_scale = query_gain.astype(jnp.float32)
    key_scale = key_gain.astype(jnp.float32)
    query_round = (query_raw * query_inverse[:, None] * query_scale).astype(jnp.bfloat16)
    key_round = (key_raw * key_inverse[:, None] * key_scale).astype(jnp.bfloat16)
    value_round = value_raw.astype(jnp.bfloat16)
    pair_local = jnp.concatenate([key_round, value_round], axis=1)
    pair_group = gather_rows(pair_local.reshape(shared, 1, 2 * head_part)).reshape(
        group_tokens, 2 * head_part
    )
    query_places = jnp.arange(sequence_share, dtype=jnp.int32) * row_count + row_index
    key_segments = segments.reshape(sequence_count, sequence_length)
    query_segments = lax.dynamic_index_in_dim(
        segments.reshape(shared, row_count), row_index, axis=1, keepdims=False
    ).reshape(sequence_count, sequence_share)

    def attend(pieces):
        query_block, key_block, value_block, query_marks, key_marks = pieces
        scores = (
            jnp.einsum("qhd,khd->hqk", query_block, key_block, preferred_element_type=jnp.float32)
            * score_scale
        )
        allowed = allowed_keys(query_marks, key_marks, query_places)
        masked = jnp.where(allowed[None], scores, NEGATIVE)
        largest = jnp.max(masked, axis=2, keepdims=True)
        raised = jnp.exp(masked - largest)
        summed = jnp.sum(raised, axis=2, keepdims=True)
        weights = (raised / summed).astype(jnp.bfloat16)
        mixed = jnp.einsum("hqk,khd->qhd", weights, value_block, preferred_element_type=jnp.float32)
        return (mixed.astype(jnp.bfloat16), (largest + jnp.log(summed))[..., 0])

    query_blocks = query_round.reshape(sequence_count, sequence_share, heads_here, HEAD_DIM)
    key_blocks = pair_group[:, :head_part].reshape(
        sequence_count, sequence_length, heads_here, HEAD_DIM
    )
    value_blocks = pair_group[:, head_part:].reshape(
        sequence_count, sequence_length, heads_here, HEAD_DIM
    )
    key_blocks, value_blocks = (key_blocks, value_blocks)
    mixed_blocks, log_sums = lax.map(
        attend, (query_blocks, key_blocks, value_blocks, query_segments, key_segments)
    )
    mixed_local = mixed_blocks.reshape(shared, head_part)
    mixed_group = gather_rows(mixed_local.reshape(shared, 1, head_part)).reshape(
        group_tokens, head_part
    )
    attention_out = reduce_columns(
        jnp.dot(mixed_group, output_weight, preferred_element_type=jnp.float32)
    )
    middle = residual + attention_out
    second_scale = expert_gain.astype(jnp.float32)
    second_inverse = lax.rsqrt(total_rows(jnp.sum(middle * middle, axis=1)) / D + EPSILON)
    second_normed = (middle * second_inverse[:, None] * second_scale).astype(jnp.bfloat16)
    second_group = gather_columns(second_normed)
    logits_part = jnp.dot(second_group, router_weight, preferred_element_type=jnp.float32)
    source, filled, position = expert_slots(routes, experts, capacity)
    second_buffer = jnp.take(second_group, source // top_count, axis=0)
    gate_up_weight = jnp.concatenate([gate_weight, up_weight], axis=2)
    gate_up_buffer_forward = jnp.einsum(
        "ecd,edf->ecf", second_buffer, gate_up_weight, preferred_element_type=jnp.float32
    )
    gate_up_part = to_routes(gate_up_buffer_forward, position)
    logits_local, gate_up_local = (
        lax.psum_scatter(
            logits_part.reshape(shared, row_count, experts), "row", scatter_dimension=1, tiled=True
        ),
        lax.psum_scatter(
            gate_up_part.reshape(shared, row_count, top_count * 2 * hidden_part),
            "row",
            scatter_dimension=1,
            tiled=True,
        ),
    )
    logits_local = logits_local.reshape(shared, experts)
    gate_up_local = gate_up_local.reshape(shared, top_count, 2 * hidden_part)
    gate_local = gate_up_local[..., :hidden_part]
    up_local = gate_up_local[..., hidden_part:]
    own_routes = lax.dynamic_index_in_dim(
        routes.reshape(shared, row_count, top_count), row_index, axis=1, keepdims=False
    )
    largest_logit = jnp.max(logits_local, axis=1, keepdims=True)
    raised_logits = jnp.exp(logits_local - largest_logit)
    router_probs = raised_logits / jnp.sum(raised_logits, axis=1, keepdims=True)
    route_match = (
        own_routes[..., None] == jnp.arange(experts, dtype=jnp.int32)[None, None, :]
    ).astype(jnp.float32)
    picked = jnp.sum(route_match * router_probs[:, None, :], axis=2)
    sigmoid_gate = jax.nn.sigmoid(gate_local)
    silu_gate = gate_local * sigmoid_gate
    hidden_local = (picked[..., None] * silu_gate * up_local).astype(jnp.bfloat16)
    hidden_group = gather_rows(hidden_local.reshape(shared, 1, top_count * hidden_part)).reshape(
        group_tokens * top_count, hidden_part
    )
    hidden_buffer = jnp.take(hidden_group, source, axis=0)
    down_buffer = jnp.einsum(
        "ecf,efd->ecd", hidden_buffer, down_weight, preferred_element_type=jnp.float32
    )
    expert_part = jnp.sum(
        to_routes(down_buffer, position).reshape(group_tokens, top_count, width_part), axis=1
    )
    expert_out = reduce_columns(expert_part)
    residual_out = (middle + expert_out).astype(jnp.bfloat16)
    output_delta = cotangent.astype(jnp.float32)
    delta_group = gather_columns(cotangent)
    delta_buffer = jnp.where(
        filled[..., None], jnp.take(delta_group, source // top_count, axis=0), empty_value
    )
    down_gradient = jnp.einsum(
        "ecf,ecd->efd", hidden_buffer, delta_buffer, preferred_element_type=jnp.float32
    )
    hidden_delta_buffer = jnp.einsum(
        "ecd,efd->ecf", delta_buffer, down_weight, preferred_element_type=jnp.float32
    )
    hidden_delta = reduce_rows(
        to_routes(hidden_delta_buffer, position).reshape(shared, row_count, top_count * hidden_part)
    ).reshape(shared, top_count, hidden_part)
    picked_delta = total_columns(jnp.sum(hidden_delta * silu_gate * up_local, axis=2))
    through = hidden_delta * picked[..., None]
    gate_delta = through * up_local * sigmoid_gate * (1.0 + gate_local * (1.0 - sigmoid_gate))
    up_delta = through * silu_gate
    probs_delta = jnp.sum(route_match * picked_delta[..., None], axis=1)
    logits_delta = router_probs * (
        probs_delta - jnp.sum(router_probs * probs_delta, axis=1, keepdims=True)
    )
    gate_up_round = (
        jnp.concatenate([gate_delta, up_delta], axis=2)
        .astype(jnp.bfloat16)
        .reshape(shared, 1, top_count * 2 * hidden_part)
    )
    logits_round = logits_delta.astype(jnp.bfloat16).reshape(shared, 1, experts)
    logits_group, gate_up_group = (
        lax.all_gather(logits_round, "row", axis=1, tiled=True),
        lax.all_gather(gate_up_round, "row", axis=1, tiled=True),
    )
    logits_group = logits_group.reshape(group_tokens, experts)
    gate_up_group = gate_up_group.reshape(group_tokens * top_count, 2 * hidden_part)
    gate_up_buffer = jnp.where(
        filled[..., None], jnp.take(gate_up_group, source, axis=0), empty_value
    )
    gate_up_gradient = jnp.einsum(
        "ecd,ecf->edf", second_buffer, gate_up_buffer, preferred_element_type=jnp.float32
    )
    gate_gradient = gate_up_gradient[..., :hidden_part]
    up_gradient = gate_up_gradient[..., hidden_part:]
    router_gradient = jnp.einsum(
        "td,te->de", second_group, logits_group, preferred_element_type=jnp.float32
    )
    input_buffer = jnp.einsum(
        "ecf,edf->ecd", gate_up_buffer, gate_up_weight, preferred_element_type=jnp.float32
    )
    expert_back = jnp.sum(
        to_routes(input_buffer, position).reshape(group_tokens, top_count, width_part), axis=1
    )
    logits_own = lax.dynamic_slice_in_dim(
        logits_group, column_index * local_tokens, local_tokens, 0
    )
    second_delta = reduce_columns(expert_back) + jnp.dot(
        logits_own, router_weight.T, preferred_element_type=jnp.float32
    )
    second_inner = total_rows(jnp.sum(second_delta * second_scale * middle, axis=1))
    middle_delta = (
        output_delta
        + second_inverse[:, None] * second_scale * second_delta
        - middle * (second_inverse**3 * second_inner / D)[:, None]
    )
    second_gain_part = jnp.sum(second_delta * middle * second_inverse[:, None], axis=0)
    attention_round = middle_delta.astype(jnp.bfloat16)
    attention_group = gather_columns(attention_round)
    output_gradient = jnp.einsum(
        "th,td->hd", mixed_group, attention_group, preferred_element_type=jnp.float32
    )
    mixed_delta = (
        reduce_rows(
            jnp.dot(attention_group, output_weight.T, preferred_element_type=jnp.float32).reshape(
                shared, row_count, head_part
            )
        )
        .reshape(shared, head_part)
        .astype(jnp.bfloat16)
    )
    mixed_delta_blocks = mixed_delta.reshape(sequence_count, sequence_share, heads_here, HEAD_DIM)

    def attend_back(pieces):
        query_block, key_block, value_block, query_marks, key_marks, log_block, delta_block = pieces
        scores = (
            jnp.einsum("qhd,khd->hqk", query_block, key_block, preferred_element_type=jnp.float32)
            * score_scale
        )
        allowed = allowed_keys(query_marks, key_marks, query_places)
        probs = jnp.where(allowed[None], jnp.exp(scores - log_block[..., None]), 0.0)
        weights = probs.astype(jnp.bfloat16)
        weights_delta = jnp.einsum(
            "qhd,khd->hqk", delta_block, value_block, preferred_element_type=jnp.float32
        )
        centre = jnp.sum(probs * weights_delta, axis=2, keepdims=True)
        score_delta = (probs * (weights_delta - centre)).astype(jnp.bfloat16)
        query_delta = (
            jnp.einsum("hqk,khd->qhd", score_delta, key_block, preferred_element_type=jnp.float32)
            * score_scale
        )
        key_delta = (
            jnp.einsum("hqk,qhd->khd", score_delta, query_block, preferred_element_type=jnp.float32)
            * score_scale
        )
        value_delta = jnp.einsum(
            "hqk,qhd->khd", weights, delta_block, preferred_element_type=jnp.float32
        )
        pair_delta = jnp.concatenate(
            [
                key_delta.reshape(sequence_length, head_part),
                value_delta.reshape(sequence_length, head_part),
            ],
            axis=1,
        )
        return (query_delta.reshape(sequence_share, head_part), pair_delta)

    query_deltas, pair_deltas = lax.map(
        attend_back,
        (
            query_blocks,
            key_blocks,
            value_blocks,
            query_segments,
            key_segments,
            log_sums,
            mixed_delta_blocks,
        ),
    )
    query_delta = query_deltas.reshape(shared, head_part)
    pair_delta = reduce_rows(pair_deltas.reshape(shared, row_count, 2 * head_part)).reshape(
        shared, 2 * head_part
    )
    key_delta = pair_delta[:, :head_part]
    value_delta = pair_delta[:, head_part:]
    inner_sums = total_columns(
        jnp.stack(
            [
                jnp.sum(query_delta * query_scale * query_raw, axis=1),
                jnp.sum(key_delta * key_scale * key_raw, axis=1),
            ]
        )
    )
    query_raw_delta = (
        query_inverse[:, None] * query_scale * query_delta
        - query_raw * (query_inverse**3 * inner_sums[0] / D)[:, None]
    )
    key_raw_delta = (
        key_inverse[:, None] * key_scale * key_delta
        - key_raw * (key_inverse**3 * inner_sums[1] / D)[:, None]
    )
    query_gain_part = jnp.sum(query_delta * query_raw * query_inverse[:, None], axis=0)
    key_gain_part = jnp.sum(key_delta * key_raw * key_inverse[:, None], axis=0)
    joint_delta = jnp.concatenate([query_raw_delta, key_raw_delta, value_delta], axis=1).astype(
        jnp.bfloat16
    )
    joint_group = gather_rows(joint_delta.reshape(shared, 1, 3 * head_part)).reshape(
        group_tokens, 3 * head_part
    )
    joint_gradient = jnp.einsum(
        "td,th->dh", normed_group, joint_group, preferred_element_type=jnp.float32
    )
    query_gradient = joint_gradient[:, :head_part]
    key_gradient = joint_gradient[:, head_part : 2 * head_part]
    value_gradient = joint_gradient[:, 2 * head_part :]
    first_delta = reduce_columns(
        jnp.dot(joint_group, joint_weight.T, preferred_element_type=jnp.float32)
    )
    first_inner = total_rows(jnp.sum(first_delta * first_scale * residual, axis=1))
    input_gradient = (
        middle_delta
        + first_inverse[:, None] * first_scale * first_delta
        - residual * (first_inverse**3 * first_inner / D)[:, None]
    )
    first_gain_part = jnp.sum(first_delta * residual * first_inverse[:, None], axis=0)
    (
        query_gradient,
        key_gradient,
        value_gradient,
        output_gradient,
        router_gradient,
        gate_gradient,
        up_gradient,
        down_gradient,
    ) = (
        lax.psum(query_gradient.astype(jnp.bfloat16), "dp").astype(jnp.float32),
        lax.psum(key_gradient.astype(jnp.bfloat16), "dp").astype(jnp.float32),
        lax.psum(value_gradient.astype(jnp.bfloat16), "dp").astype(jnp.float32),
        lax.psum(output_gradient.astype(jnp.bfloat16), "dp").astype(jnp.float32),
        lax.psum(router_gradient.astype(jnp.bfloat16), "dp").astype(jnp.float32),
        lax.psum(gate_gradient.astype(jnp.bfloat16), "dp").astype(jnp.float32),
        lax.psum(up_gradient.astype(jnp.bfloat16), "dp").astype(jnp.float32),
        lax.psum(down_gradient.astype(jnp.bfloat16), "dp").astype(jnp.float32),
    )
    zero_index = jnp.zeros((), jnp.int32)
    gain_table = jnp.zeros((4, D), jnp.float32)
    gain_table = lax.dynamic_update_slice(
        gain_table, first_gain_part[None], (zero_index, row_index * width_part)
    )
    gain_table = lax.dynamic_update_slice(
        gain_table, second_gain_part[None], (zero_index + 1, row_index * width_part)
    )
    gain_table = lax.dynamic_update_slice(
        gain_table, query_gain_part[None], (zero_index + 2, column_index * head_part)
    )
    gain_table = lax.dynamic_update_slice(
        gain_table, key_gain_part[None], (zero_index + 3, column_index * head_part)
    )
    gain_table = lax.psum(gain_table, ("dp", "row", "col"))
    first_gain_gradient = lax.dynamic_slice(gain_table[0], (row_index * width_part,), (width_part,))
    second_gain_gradient = lax.dynamic_slice(
        gain_table[1], (row_index * width_part,), (width_part,)
    )
    query_gain_gradient = lax.dynamic_slice(
        gain_table[2], (column_index * head_part,), (head_part,)
    )
    key_gain_gradient = lax.dynamic_slice(gain_table[3], (column_index * head_part,), (head_part,))
    return (
        residual_out,
        input_gradient,
        first_gain_gradient,
        query_gradient,
        key_gradient,
        value_gradient,
        query_gain_gradient,
        key_gain_gradient,
        output_gradient,
        second_gain_gradient,
        router_gradient,
        gate_gradient,
        up_gradient,
        down_gradient,
    )


def solution(mesh):
    placed = (
        P(("dp", "col"), "row"),
        P("row"),
        P("row", "col"),
        P("row", "col"),
        P("row", "col"),
        P("col"),
        P("col"),
        P("col", "row"),
        P("row"),
        P("row", None),
        P(None, "row", "col"),
        P(None, "row", "col"),
        P(None, "col", "row"),
        P("dp"),
        P("dp", None),
        P(("dp", "col"), "row"),
    )
    return jax.shard_map(
        on_device,
        mesh=mesh,
        in_specs=placed,
        out_specs=(
            P(("dp", "col"), "row"),
            P(("dp", "col"), "row"),
            P("row"),
            P("row", "col"),
            P("row", "col"),
            P("row", "col"),
            P("col"),
            P("col"),
            P("col", "row"),
            P("row"),
            P("row", None),
            P(None, "row", "col"),
            P(None, "row", "col"),
            P(None, "col", "row"),
        ),
        check_vma=False,
    )
```

profile of v0, /device:TPU:0, one launch (start us, length us, event | category | flops | bytes accessed | tf_op | source)
XLA Modules:
  0.0 3791.0 jit_solution(12874688109838540582)
XLA Ops:
  84.4 98.5 %reduce-scatter.11.cloned.1.call-done = f32[256,1,3072]{2,0,1:T(8,128)} async-done(((f32[256,4,3072]{2,0,1:T(8,128)}), f32[256,1,3072]{2,0,1:T(8,128)}) %reduce-scatter.11.cloned.1.call-update) | async-done | bytes 3145744 | tf_op jit(solution)/shard_map/reduce_scatter | solution.py:28
  196.5 32.5 all-gather.27.cloned.1.call-done
  292.5 30.5 scatter_custom_fusion
  323.9 51.7 %gather_fusion.5 = bf16[12288,512]{1,0:T(8,128)(2,1)} fusion(bf16[1024,512]{1,0:T(8,128)(2,1)} %all-gather.19.cloned.1.call-done, s32[12288]{0:T(1024)S(1)} %broadcast_clamp_fusion.1), kind=kCustom, calls=%fused_computation.2.clone | custom fusion | bytes 25214976 | tf_op jit(solution)/shard_map/jit(_take)/gather | solution.py:229
  394.9 43.0 %gather_fusion.6 = f32[8192,512]{1,0:T(8,128)} fusion(f32[12288,512]{1,0:T(8,128)} %bitcast.133, s32[8192]{0:T(1024)S(1)} %broadcast_clamp_fusion.2), kind=kCustom, calls=%fused_computation.3.clone | custom fusion | bytes 33587200 | tf_op jit(solution)/shard_map/jit(_take)/gather | solution.py:61
  554.6 51.7 %gather_fusion.3 = bf16[12288,512]{1,0:T(8,128)(2,1)} fusion(bf16[1024,512]{1,0:T(8,128)(2,1)} %all-gather.15.cloned.1.call-done, s32[12288]{0:T(1024)S(1)} %broadcast_clamp_fusion.1), kind=kCustom, calls=%fused_computation.clone | custom fusion | bytes 25214976 | tf_op jit(solution)/shard_map/jit(_take)/gather | solution.py:180
  622.0 32.2 fusion.7
  654.2 58.6 %gather_fusion = f32[8192,1024]{1,0:T(8,128)} fusion(f32[12288,1024]{1,0:T(8,128)} %bitcast.130, s32[8192]{0:T(1024)S(1)} %broadcast_clamp_fusion.3), kind=kCustom, calls=%fused_computation.5 | custom fusion | bytes 67141632 | tf_op jit(solution)/shard_map/jit(_take)/gather | solution.py:61
  712.8 39.6 %gather.21 = f32[256,4,8192]{2,1,0:T(4,128)} reshape(f32[8192,1024]{1,0:T(8,128)} %gather_fusion) | data formatting | bytes 67108864 | tf_op jit(solution)/shard_map/jit(_take)/gather | solution.py:61
  753.8 33.7 copy_select_fusion
  797.2 226.3 %reduce-scatter.17.cloned.1.call-done = f32[256,1,8192]{2,0,1:T(8,128)} async-done(((f32[256,4,8192]{2,0,1:T(8,128)}), f32[256,1,8192]{2,0,1:T(8,128)}) %reduce-scatter.17.cloned.1.call-update) | async-done | bytes 8388624 | tf_op jit(solution)/shard_map/reduce_scatter | solution.py:190
  1064.9 47.2 %all-gather.17.cloned.1.call-done = bf16[256,4,4096]{2,0,1:T(8,128)(2,1)} async-done(((bf16[256,1,4096]{2,0,1:T(8,128)(2,1)}), bf16[256,4,4096]{2,0,1:T(8,128)(2,1)}) %all-gather.17.cloned.1.call-update) | async-done | bytes 8388624 | tf_op jit(solution)/shard_map/all_gather | solution.py:32
  1139.0 55.0 %gather_fusion.1 = bf16[12288,512]{1,0:T(8,128)(2,1)} fusion(bf16[8192,512]{1,0:T(8,128)(2,1)} %reshape.504, s32[12288]{0:T(1024)S(1)} %broadcast_clamp_fusion), kind=kCustom, calls=%fused_computation.6 | custom fusion | bytes 25214976 | tf_op jit(solution)/shard_map/jit(_take)/gather | solution.py:217
  1231.9 43.3 %gather_fusion.4 = f32[8192,512]{1,0:T(8,128)} fusion(f32[12288,512]{1,0:T(8,128)} %bitcast.131, s32[8192]{0:T(1024)S(1)} %copy-done.25), kind=kCustom, calls=%fused_computation.1.clone | custom fusion | bytes 33587200 | tf_op jit(solution)/shard_map/jit(_take)/gather | solution.py:61
  1297.3 27.6 reshape.510
  1324.8 68.1 %gather_fusion.2 = bf16[12288,1024]{1,0:T(8,128)(2,1)} fusion(bf16[8192,1024]{1,0:T(8,128)(2,1)} %reshape.510, s32[12288]{0:T(1024)S(1)} %broadcast_clamp_fusion), kind=kCustom, calls=%fused_computation.7 | custom fusion | bytes 50380800 | tf_op jit(solution)/shard_map/jit(_take)/gather | solution.py:261
  1392.9 30.7 fusion
  1423.7 42.9 %gather_fusion.7 = f32[8192,512]{1,0:T(8,128)} fusion(f32[12288,512]{1,0:T(8,128)} %bitcast.132, s32[8192]{0:T(1024)S(1)} %copy-done.25), kind=kCustom, calls=%fused_computation.4.clone | custom fusion | bytes 33587200 | tf_op jit(solution)/shard_map/jit(_take)/gather | solution.py:61
  1564.1 44.4 %reduce-scatter.25.cloned.1.call-done = f32[256,1,1024]{2,0,1:T(8,128)} async-done(((f32[256,4,1024]{2,0,1:T(8,128)}), f32[256,1,1024]{2,0,1:T(8,128)}) %reduce-scatter.25.cloned.1.call-update) | async-done | bytes 1048592 | tf_op jit(solution)/shard_map/reduce_scatter | solution.py:28
  1691.5 64.1 %reduce-scatter.27.cloned.1.call-done = f32[256,1,2048]{2,0,1:T(8,128)} async-done(((f32[256,4,2048]{2,0,1:T(8,128)}), f32[256,1,2048]{2,0,1:T(8,128)}) %reduce-scatter.27.cloned.1.call-update) | async-done | bytes 2097168 | tf_op jit(solution)/shard_map/reduce_scatter | solution.py:28
  1768.1 46.3 %all-gather.25.cloned.1.call-done = bf16[256,4,3072]{2,0,1:T(8,128)(2,1)} async-done(((bf16[256,1,3072]{2,0,1:T(8,128)(2,1)}), bf16[256,4,3072]{2,0,1:T(8,128)(2,1)}) %all-gather.25.cloned.1.call-update) | async-done | bytes 6291472 | tf_op jit(solution)/shard_map/all_gather | solution.py:32
  1862.4 30.9 convolution_convert_fusion
  1961.4 51.1 %psum.119 = f32[4,2048]{1,0:T(4,128)S(1)} all-reduce(f32[4,2048]{1,0:T(4,128)S(1)} %dynamic_update_slice.27), channel_id=1, replica_groups=mesh['dp'=4,'row'=4,'col'=2] {'dp','row','col'}, use_global_device_ids=true, to_apply=%region_44.47 | all-reduce | flops 8192 | bytes 65536 | tf_op jit(solution)/shard_map/psum | solution.py:431
  2018.8 1705.2 %all-reduce.3.cloned.1.call-done = (bf16[512,1024]{1,0:T(8,128)(2,1)}, bf16[512,1024]{1,0:T(8,128)(2,1)}, bf16[512,1024]{1,0:T(8,128)(2,1)}, bf16[1024,512]{1,0:...) async-done(((bf16[512,1024]{1,0:T(8,128)(2,1)}, bf16[512,1024]{1,0:T(8,128)(2,1)}, ...) | async-done | bytes 54525968 | tf_op jit(solution)/shard_map/psum | solution.py:408
  (398 shorter events, 820.0 us)
Async XLA Ops:
  7.2 280.5 %copy-start = (bf16[1024,512]{1,0:T(8,128)(2,1)S(1)}, bf16[1024,512]{1,0:T(8,128)(2,1)}, u32[]{:S(2)}) copy-start(bf16[1024,512]{1,0:T(8,128)(2,1)} %param.27) | copy-start | bytes 3145732
  7.2 34.8 all-gather.11.cloned.1.call-start
  20.2 162.7 %reduce-scatter.11.cloned.1.call-start = ((), (), s32[]{:S(2)}) async-start(), calls=%async_computation.11 | async-start | bytes 15728640 | tf_op jit(solution)/shard_map/reduce_scatter | solution.py:28
  83.7 145.3 %all-gather.27.cloned.1.call-start = ((), (), s32[]{:S(2)}) async-start(), calls=%async_computation.28 | async-start | bytes 5242880 | tf_op jit(solution)/shard_map/all_gather | solution.py:32
  194.4 84.7 %all-gather.13.cloned.1.call-start = ((), (), s32[]{:S(2)}) async-start(), calls=%async_computation.12 | async-start | bytes 2621440 | tf_op jit(solution)/shard_map/all_gather | solution.py:32
  256.3 67.5 %all-gather.19.cloned.1.call-start = ((), (), s32[]{:S(2)}) async-start(), calls=%async_computation.19 | async-start | bytes 1572864 | tf_op jit(solution)/shard_map/all_gather | solution.py:24
  256.9 181.0 %reduce-scatter.13.cloned.1.call-start = ((), (), s32[]{:S(2)}) async-start(), calls=%async_computation.13 | async-start | bytes 3145728 | tf_op jit(solution)/shard_map/reduce_scatter | solution.py:36
  257.2 240.0 %copy-start.10 = (s32[1024,8]{1,0:T(8,128)}, s32[1024,8]{1,0:T(8,128)S(1)}, u32[]{:S(2)}) copy-start(s32[1024,8]{1,0:T(8,128)S(1)} %copy.203) | copy-start | bytes 98308
  292.0 262.6 %all-gather.15.cloned.1.call-start = ((), (), s32[]{:S(2)}) async-start(), calls=%async_computation.14 | async-start | bytes 1572864 | tf_op jit(solution)/shard_map/all_gather | solution.py:24
  323.7 298.3 %copy-start.31 = (pred[32,384]{1,0:T(8,128)(4,1)}, pred[32,384]{1,0:T(8,128)(4,1)S(1)}, u32[]{:S(2)}) copy-start(pred[32,384]{1,0:T(8,128)(4,1)S(1)} %get-tuple-element.121) | copy-start | bytes 36868
  446.2 342.9 %reduce-scatter.21.cloned.1.call-start = ((), (), s32[]{:S(2)}) async-start(), calls=%async_computation.20 | async-start | bytes 20971520 | tf_op jit(solution)/shard_map/reduce_scatter | solution.py:28
  496.1 298.7 %reduce-scatter.15.cloned.1.call-start = ((), (), s32[]{:S(2)}) async-start(), calls=%async_computation.15 | async-start | bytes 163840 | tf_op jit(solution)/shard_map/reduce_scatter | solution.py:187
  753.7 269.8 %reduce-scatter.17.cloned.1.call-start = ((), (), s32[]{:S(2)}) async-start(), calls=%async_computation.16 | async-start | bytes 41943040 | tf_op jit(solution)/shard_map/reduce_scatter | solution.py:190
  787.5 324.6 %all-gather.17.cloned.1.call-start = ((), (), s32[]{:S(2)}) async-start(), calls=%async_computation.17 | async-start | bytes 10485760 | tf_op jit(solution)/shard_map/all_gather | solution.py:32
  795.6 236.9 %copy-start.55 = (f32[256]{0:T(256)}, f32[256]{0:T(256)S(1)}, u32[]{:S(2)}) copy-start(f32[256]{0:T(256)S(1)} %reduce_max.20) | copy-start | bytes 3076
  1053.6 221.5 %all-gather.21.cloned.1.call-start = ((), (), s32[]{:S(2)}) async-start(), calls=%async_computation.21 | async-start | bytes 20971520 | tf_op jit(solution)/shard_map/all_gather | solution.py:256
  1064.8 450.8 %reduce-scatter.23.cloned.1.call-start = ((), (), s32[]{:S(2)}) async-start(), calls=%async_computation.22 | async-start | bytes 3145728 | tf_op jit(solution)/shard_map/reduce_scatter | solution.py:36
  1483.4 64.0 %all-gather.23.cloned.1.call-start = ((), (), s32[]{:S(2)}) async-start(), calls=%async_computation.23 | async-start | bytes 1572864 | tf_op jit(solution)/shard_map/all_gather | solution.py:24
  1526.8 81.6 %reduce-scatter.25.cloned.1.call-start = ((), (), s32[]{:S(2)}) async-start(), calls=%async_computation.24 | async-start | bytes 5242880 | tf_op jit(solution)/shard_map/reduce_scatter | solution.py:28
  1563.8 191.8 %reduce-scatter.27.cloned.1.call-start = ((), (), s32[]{:S(2)}) async-start(), calls=%async_computation.25 | async-start | bytes 10485760 | tf_op jit(solution)/shard_map/reduce_scatter | solution.py:28
  1683.7 130.7 %all-gather.25.cloned.1.call-start = ((), (), s32[]{:S(2)}) async-start(), calls=%async_computation.26 | async-start | bytes 7864320 | tf_op jit(solution)/shard_map/all_gather | solution.py:32
  1767.9 183.7 %reduce-scatter.29.cloned.1.call-start = ((), (), s32[]{:S(2)}) async-start(), calls=%async_computation.27 | async-start | bytes 3145728 | tf_op jit(solution)/shard_map/reduce_scatter | solution.py:36
  1843.9 171.0 %reduce-scatter.19.cloned.1.call-start = ((), (), s32[]{:S(2)}) async-start(), calls=%async_computation.18 | async-start | bytes 3145728 | tf_op jit(solution)/shard_map/reduce_scatter | solution.py:36
  1862.1 1861.8 %all-reduce.3.cloned.1.call-start = ((), (), s32[]{:S(2)}) async-start(), calls=%async_computation.29 | async-start | bytes 109051904 | tf_op jit(solution)/shard_map/psum | solution.py:408
  (84 other events, 3288.6 us)
Sparse Core Ops, SparseCore 0:
  20.3 21.6 all-gather.10
  83.8 99.0 reduce-scatter.10
  194.5 34.4 all-gather.26
  256.5 22.5 all-gather.12
  280.5 21.3 all-gather.18
  304.5 31.8 reduce-scatter.12
  446.4 22.2 all-gather.14
  496.2 127.0 reduce-scatter.20
  753.9 20.5 reduce-scatter.14
  787.6 235.8 reduce-scatter.16
  1053.8 58.2 all-gather.16
  1113.6 105.9 all-gather.20
  1483.5 31.9 reduce-scatter.22
  1527.0 20.3 all-gather.22
  1563.9 44.4 reduce-scatter.24
  1683.8 71.7 reduce-scatter.26
  1768.0 46.3 all-gather.24
  1844.0 31.8 reduce-scatter.28
  1878.8 31.8 reduce-scatter.18
  1927.6 1796.3 all-reduce.2
where the time goes:
time: 3810 us; the launch traced here: 3790 us
  waiting for transfers between devices  2330 us (61%)
  local copies, waits for them, and re-layouts  892 us (23%)
  matrix products  221 us (6%)
  other arithmetic  211 us (6%)
  blocking collectives  121 us (3%)
    psum x1, waiting for transfers between devices, on_device(): lax.psum(query_gradient.astype(jnp.bfloat16), 'dp').astype(jnp.float32)  1710 us
    gather x5, local copies, waits for them, and re-layouts, to_routes(): return jnp.take(flat_rows, position, axis=0)  227 us
    reduce_scatter x1, waiting for transfers between devices, on_device(): lax.psum_scatter(gate_up_part.reshape(shared, row_count, top_count * 2 *...  226 us
    reduce_scatter x4, waiting for transfers between devices, reduce_rows(): return lax.psum_scatter(value, 'row', scatter_dimension=1, tiled=True)  207 us
    all_gather x4, waiting for transfers between devices, gather_rows(): return lax.all_gather(value, 'row', axis=1, tiled=True)  127 us
  transfers between devices with their start and end apart: 20, of which 12 were waited for; matrix products, arithmetic and copies ran while one was open for 21% of the time, Pallas kernels for 0%

commit v1 on v0

v1 whole, which is shorter than its diff:
```python
import functools

import jax
import jax.numpy as jnp
from jax import lax
from jax.experimental import pallas as pl
from jax.experimental.pallas import tpu as pltpu
from jax.sharding import PartitionSpec as P

HEAD_DIM = 128
MAX_LEN = 2048
EPSILON = 1e-05
NEGATIVE = -1e30

TILE = 128
WIDE = 512
SUB = 1024
RING = 8
MEGA = 1 << 20
BF = jnp.bfloat16
F32 = jnp.float32


def dot(left, right):
    return jnp.dot(left, right, preferred_element_type=F32)


def dot_nt(left, right):
    return lax.dot_general(left, right, (((1,), (1,)), ((), ())), preferred_element_type=F32)


def dot_tn(left, right):
    return lax.dot_general(left, right, (((0,), (0,)), ((), ())), preferred_element_type=F32)


def iota(shape, axis):
    return lax.broadcasted_iota(jnp.int32, shape, axis)


def params(mebibytes):
    return pltpu.CompilerParams(vmem_limit_bytes=mebibytes * MEGA)


def cost(flops, nbytes):
    return pl.CostEstimate(flops=int(flops), bytes_accessed=int(nbytes), transcendentals=0)


def once(shape, index):
    return pl.BlockSpec(shape, index, pipeline_mode=pl.Buffered(buffer_count=1))


def project_kernel(x_ref, q_ref, k_ref, v_ref, o_ref):
    width = q_ref.shape[1]
    x = x_ref[...]
    o_ref[0, :, :width] = dot(x, q_ref[...]).astype(BF)
    o_ref[0, :, width : 2 * width] = dot(x, k_ref[...]).astype(BF)
    o_ref[0, :, 2 * width :] = dot(x, v_ref[...]).astype(BF)


def project(x, query, key, value, spans, slots):
    tokens, depth = x.shape
    width, span = query.shape[1] // slots, tokens // spans
    weight = pl.BlockSpec((depth, width), lambda s, h: (0, h))
    return pl.pallas_call(
        project_kernel,
        grid=(spans, slots),
        in_specs=[pl.BlockSpec((span, depth), lambda s, h: (s, 0)), weight, weight, weight],
        out_specs=pl.BlockSpec((1, span, 3 * width), lambda s, h: (s * slots + h, 0, 0)),
        out_shape=jax.ShapeDtypeStruct((spans * slots, span, 3 * width), BF),
        compiler_params=params(48),
        cost_estimate=cost(6 * tokens * depth * width * slots, 6 * tokens * width * slots),
        name="project",
    )(x, query, key, value)


def project_back_kernel(d_ref, q_ref, k_ref, v_ref, o_ref, acc):
    slot = pl.program_id(1)
    width = q_ref.shape[1]

    @pl.when(slot == 0)
    def _():
        acc[...] = jnp.zeros_like(acc)

    acc[...] += (
        dot_nt(d_ref[0, :, :width], q_ref[...])
        + dot_nt(d_ref[0, :, width : 2 * width], k_ref[...])
        + dot_nt(d_ref[0, :, 2 * width :], v_ref[...])
    )

    @pl.when(slot == pl.num_programs(1) - 1)
    def _():
        o_ref[...] = acc[...].astype(BF)


def project_back(delta, query, key, value, spans, slots):
    _, span, joint = delta.shape
    depth, width = query.shape[0], joint // 3
    weight = pl.BlockSpec((depth, width), lambda s, h: (0, h))
    return pl.pallas_call(
        project_back_kernel,
        grid=(spans, slots),
        in_specs=[
            pl.BlockSpec((1, span, joint), lambda s, h: (s * slots + h, 0, 0)),
            weight,
            weight,
            weight,
        ],
        out_specs=pl.BlockSpec((span, depth), lambda s, h: (s, 0)),
        out_shape=jax.ShapeDtypeStruct((spans * span, depth), BF),
        scratch_shapes=[pltpu.VMEM((span, depth), F32)],
        compiler_params=params(48),
        cost_estimate=cost(2 * spans * span * depth * joint * slots, 2 * spans * span * joint * slots),
        name="project_back",
    )(delta, query, key, value)


def project_gradient_kernel(x_ref, d_ref, q_ref, k_ref, v_ref, acc):
    span = pl.program_id(1)
    made = dot(x_ref[...], d_ref[0])

    @pl.when(span == 0)
    def _():
        acc[...] = made

    @pl.when(span > 0)
    def _():
        acc[...] += made

    @pl.when(span == pl.num_programs(1) - 1)
    def _():
        width = q_ref.shape[1]
        q_ref[...] = acc[:, :width].astype(BF)
        k_ref[...] = acc[:, width : 2 * width].astype(BF)
        v_ref[...] = acc[:, 2 * width :].astype(BF)


def project_gradient(turned, delta, spans, slots):
    depth, tokens = turned.shape
    _, span, joint = delta.shape
    width = joint // 3
    out = pl.BlockSpec((depth, width), lambda h, s: (0, h))
    return pl.pallas_call(
        project_gradient_kernel,
        grid=(slots, spans),
        in_specs=[
            pl.BlockSpec((depth, span), lambda h, s: (0, s)),
            pl.BlockSpec((1, span, joint), lambda h, s: (s * slots + h, 0, 0)),
        ],
        out_specs=[out, out, out],
        out_shape=[jax.ShapeDtypeStruct((depth, width * slots), BF)] * 3,
        scratch_shapes=[pltpu.VMEM((depth, joint), F32)],
        compiler_params=params(48),
        cost_estimate=cost(2 * tokens * depth * joint * slots, 2 * tokens * joint * slots),
        name="project_gradient",
    )(turned, delta)


def output_kernel(m_ref, w_ref, o_ref, acc):
    slot = pl.program_id(1)

    @pl.when(slot == 0)
    def _():
        acc[...] = jnp.zeros_like(acc)

    acc[...] += dot(m_ref[0], w_ref[...])

    @pl.when(slot == pl.num_programs(1) - 1)
    def _():
        o_ref[...] = acc[...].astype(BF)


def output_project(mixed, weight, spans, slots):
    _, span, width = mixed.shape
    depth = weight.shape[1]
    return pl.pallas_call(
        output_kernel,
        grid=(spans, slots),
        in_specs=[
            pl.BlockSpec((1, span, width), lambda s, h: (s * slots + h, 0, 0)),
            pl.BlockSpec((width, depth), lambda s, h: (h, 0)),
        ],
        out_specs=pl.BlockSpec((span, depth), lambda s, h: (s, 0)),
        out_shape=jax.ShapeDtypeStruct((spans * span, depth), BF),
        scratch_shapes=[pltpu.VMEM((span, depth), F32)],
        compiler_params=params(48),
        cost_estimate=cost(2 * spans * span * depth * width * slots, 2 * spans * span * width * slots),
        name="output_project",
    )(mixed, weight)


def output_back_kernel(d_ref, w_ref, o_ref):
    o_ref[0] = dot_nt(d_ref[...], w_ref[...]).astype(BF)


def output_back(delta, weight, spans, slots):
    tokens, depth = delta.shape
    width, span = weight.shape[0] // slots, tokens // spans
    return pl.pallas_call(
        output_back_kernel,
        grid=(spans, slots),
        in_specs=[
            pl.BlockSpec((span, depth), lambda s, h: (s, 0)),
            pl.BlockSpec((width, depth), lambda s, h: (h, 0)),
        ],
        out_specs=pl.BlockSpec((1, span, width), lambda s, h: (s * slots + h, 0, 0)),
        out_shape=jax.ShapeDtypeStruct((spans * slots, span, width), BF),
        compiler_params=params(48),
        cost_estimate=cost(2 * tokens * depth * width * slots, 2 * tokens * width * slots),
        name="output_back",
    )(delta, weight)


def allowed_pairs(column_ref, row_ref, start, block, reach):
    marks = column_ref[start : start + block, :] == row_ref[0, :, :reach]
    places = iota((block, reach), 1) <= iota((block, reach), 0) + start
    return marks & places


def attend_kernel(q_ref, k_ref, v_ref, column_ref, row_ref, o_ref, log_ref):
    length = q_ref.shape[0]
    block = min(256, length)
    for start in range(0, length, block):
        reach = start + block
        scores = dot_nt(q_ref[start:reach, :], k_ref[:reach, :]) * HEAD_DIM**-0.5
        scores = jnp.where(
            allowed_pairs(column_ref, row_ref, start, block, reach), scores, NEGATIVE
        )
        largest = jnp.max(scores, axis=1, keepdims=True)
        raised = jnp.exp(scores - largest)
        summed = jnp.sum(raised, axis=1, keepdims=True)
        weights = (raised * (1.0 / summed)).astype(BF)
        o_ref[start:reach, :] = dot(weights, v_ref[:reach, :]).astype(BF)
        log_ref[0, start:reach, :] = largest + jnp.log(summed)


def attend(query, key, value, marks, length):
    tokens, width = query.shape
    heads, count = width // HEAD_DIM, tokens // length
    rows = pl.BlockSpec((length, HEAD_DIM), lambda b, h: (b, h))
    return pl.pallas_call(
        attend_kernel,
        grid=(count, heads),
        in_specs=[
            rows,
            rows,
            rows,
            pl.BlockSpec((length, 1), lambda b, h: (b, 0)),
            pl.BlockSpec((1, 1, length), lambda b, h: (b, 0, 0)),
        ],
        out_specs=[rows, pl.BlockSpec((1, length, 1), lambda b, h: (h, b, 0))],
        out_shape=[
            jax.ShapeDtypeStruct((tokens, width), BF),
            jax.ShapeDtypeStruct((heads, tokens, 1), F32),
        ],
        compiler_params=params(48),
        cost_estimate=cost(4 * tokens * length * width, 8 * tokens * width),
        name="attend",
    )(query, key, value, marks.reshape(tokens, 1), marks.reshape(count, 1, length))


def attend_back_kernel(
    q_ref, k_ref, v_ref, d_ref, log_ref, column_ref, row_ref, dq_ref, dk_ref, dv_ref
):
    length = q_ref.shape[0]
    block = min(256, length)
    scale = HEAD_DIM**-0.5
    for start in reversed(range(0, length, block)):
        reach = start + block
        query, delta = q_ref[start:reach, :], d_ref[start:reach, :]
        key, value = k_ref[:reach, :], v_ref[:reach, :]
        scores = dot_nt(query, key) * scale
        allowed = allowed_pairs(column_ref, row_ref, start, block, reach)
        probs = jnp.where(allowed, jnp.exp(scores - log_ref[0, start:reach, :]), 0.0)
        weights_delta = dot_nt(delta, value)
        centre = jnp.sum(probs * weights_delta, axis=1, keepdims=True)
        score_delta = (probs * (weights_delta - centre)).astype(BF)
        dq_ref[start:reach, :] = dot(score_delta, key) * scale
        key_delta = dot_tn(score_delta, query) * scale
        value_delta = dot_tn(probs.astype(BF), delta)
        if reach == length:
            dk_ref[...] = key_delta
            dv_ref[...] = value_delta
        else:
            dk_ref[:reach, :] += key_delta
            dv_ref[:reach, :] += value_delta


def attend_back(query, key, value, delta, logs, marks, length):
    tokens, width = query.shape
    heads, count = width // HEAD_DIM, tokens // length
    rows = pl.BlockSpec((length, HEAD_DIM), lambda b, h: (b, h))
    return pl.pallas_call(
        attend_back_kernel,
        grid=(count, heads),
        in_specs=[
            rows,
            rows,
            rows,
            rows,
            pl.BlockSpec((1, length, 1), lambda b, h: (h, b, 0)),
            pl.BlockSpec((length, 1), lambda b, h: (b, 0)),
            pl.BlockSpec((1, 1, length), lambda b, h: (b, 0, 0)),
        ],
        out_specs=[rows, rows, rows],
        out_shape=[jax.ShapeDtypeStruct((tokens, width), F32)] * 3,
        compiler_params=params(48),
        cost_estimate=cost(10 * tokens * length * width, 20 * tokens * width),
        name="attend_back",
    )(query, key, value, delta, logs, marks.reshape(tokens, 1), marks.reshape(count, 1, length))


def dispatch_kernel(token_ref, source_ref, o_ref):
    tokens = source_ref.shape[1]
    bands = []
    for i in range(WIDE // TILE):
        ids = jnp.broadcast_to(token_ref[0, 0, i : i + 1, :], (TILE, TILE)).T
        bands.append(
            jnp.concatenate(
                [
                    jnp.where(ids == iota((TILE, TILE), 1) + j, 1.0, 0.0).astype(BF)
                    for j in range(0, tokens, TILE)
                ],
                axis=1,
            )
        )
    o_ref[0] = dot(jnp.concatenate(bands, axis=0), source_ref[0]).astype(BF)


def dispatch(tokens_of, source):
    groups, rows = tokens_of.shape
    _, tokens, depth = source.shape
    return pl.pallas_call(
        dispatch_kernel,
        grid=(groups, rows // WIDE),
        in_specs=[
            pl.BlockSpec((1, 1, WIDE // TILE, TILE), lambda g, i: (g, i, 0, 0)),
            pl.BlockSpec((1, tokens, depth), lambda g, i: (g, 0, 0)),
        ],
        out_specs=pl.BlockSpec((1, WIDE, depth), lambda g, i: (g, i, 0)),
        out_shape=jax.ShapeDtypeStruct((groups, rows, depth), BF),
        compiler_params=params(48),
        cost_estimate=cost(2 * groups * rows * tokens * depth, 2 * groups * rows * depth),
        name="dispatch",
    )(tokens_of.reshape(groups, rows // WIDE, WIDE // TILE, TILE), source)


def dispatch_turned_kernel(token_ref, scale_ref, first_ref, second_ref, a_ref, b_ref):
    tokens = first_ref.shape[2]
    chosen = jnp.where(iota((tokens, WIDE), 0) == token_ref[0, 0], 1.0, 0.0).astype(BF)
    scale = scale_ref[0, 0]
    for source, out in ((first_ref, a_ref), (second_ref, b_ref)):
        rows = (dot(source[0], chosen) * scale).astype(BF)
        for i in range(WIDE // TILE):
            out[0, i] = rows[:, i * TILE : (i + 1) * TILE]


def dispatch_turned(tokens_of, scale, first, second):
    groups, rows = tokens_of.shape
    _, depth, tokens = first.shape
    line = pl.BlockSpec((1, 1, 1, WIDE), lambda g, i: (g, i, 0, 0))
    source = pl.BlockSpec((1, depth, tokens), lambda g, i: (g, 0, 0))
    out = pl.BlockSpec((1, WIDE // TILE, depth, TILE), lambda g, i: (g, i, 0, 0))
    return pl.pallas_call(
        dispatch_turned_kernel,
        grid=(groups, rows // WIDE),
        in_specs=[line, line, source, source],
        out_specs=[out, out],
        out_shape=[jax.ShapeDtypeStruct((groups, rows // TILE, depth, TILE), BF)] * 2,
        compiler_params=params(48),
        cost_estimate=cost(4 * groups * rows * tokens * depth, 4 * groups * rows * depth),
        name="dispatch_turned",
    )(
        tokens_of.reshape(groups, rows // WIDE, 1, WIDE),
        scale.reshape(groups, rows // WIDE, 1, WIDE),
        first,
        second,
    )


def pick_kernel(token_ref, expert_ref, probs_ref, o_ref):
    experts, tokens = probs_ref.shape[1], probs_ref.shape[2]
    left, parts = probs_ref[0], []
    for _ in range(3):
        part = left.astype(BF)
        parts.append(part)
        left = left - part.astype(F32)
    chosen = jnp.where(iota((tokens, WIDE), 0) == token_ref[0, 0], 1.0, 0.0).astype(BF)
    found = dot(parts[0], chosen) + dot(parts[1], chosen) + dot(parts[2], chosen)
    match = iota((experts, WIDE), 0) == expert_ref[0, 0]
    o_ref[0, 0] = jnp.sum(jnp.where(match, found, 0.0), axis=0, keepdims=True)


def pick(tokens_of, experts_of, probs):
    groups, rows = tokens_of.shape
    _, experts, tokens = probs.shape
    line = pl.BlockSpec((1, 1, 1, WIDE), lambda g, i: (g, i, 0, 0))
    shape = (groups, rows // WIDE, 1, WIDE)
    return pl.pallas_call(
        pick_kernel,
        grid=(groups, rows // WIDE),
        in_specs=[line, line, pl.BlockSpec((1, experts, tokens), lambda g, i: (g, 0, 0))],
        out_specs=line,
        out_shape=jax.ShapeDtypeStruct(shape, F32),
        compiler_params=params(48),
        cost_estimate=cost(6 * groups * rows * tokens * experts, 8 * groups * rows),
        name="pick",
    )(tokens_of.reshape(shape), experts_of.reshape(shape), probs).reshape(groups, rows)


def each_tile(low, high, run):
    first = low // TILE
    count = jnp.where(high > low, (high + TILE - 1) // TILE - first, 0)
    full = count // 4

    def step(i, carry):
        run(pl.multiple_of((first + 4 * i) * TILE, TILE), 4)
        return carry

    lax.fori_loop(0, full, step, 0)
    left = count - 4 * full
    for some in (1, 2, 3):

        @pl.when(left == some)
        def _():
            run(pl.multiple_of((first + 4 * full) * TILE, TILE), some)


def kept(base, rows, low, high):
    places = base + iota((rows, 1), 0)
    return (places >= low) & (places < high)


def gate_up_kernel(offset_ref, x_ref, gate_ref, up_ref, o_ref):
    group, expert = pl.program_id(0), pl.program_id(1)
    low, high = offset_ref[group, expert], offset_ref[group, expert + 1]
    half = gate_ref.shape[2]

    def run(base, tiles):
        rows = pl.ds(base, tiles * TILE)
        keep = kept(base, tiles * TILE, low, high)
        x = x_ref[0, rows, :]
        for start, weight in ((0, gate_ref), (half, up_ref)):
            columns = slice(start, start + half)
            made = dot(x, weight[0]).astype(BF)
            o_ref[0, rows, columns] = jnp.where(keep, made, o_ref[0, rows, columns])

    each_tile(low, high, run)


def gate_up(offsets, x, gate, up, part, half):
    groups, rows, depth = x.shape
    experts = gate.shape[0]
    weight = pl.BlockSpec((1, depth, half), lambda g, e, o: (e, 0, part))
    return pl.pallas_call(
        gate_up_kernel,
        grid_spec=pltpu.PrefetchScalarGridSpec(
            num_scalar_prefetch=1,
            grid=(groups, experts),
            in_specs=[once((1, rows, depth), lambda g, e, o: (g, 0, 0)), weight, weight],
            out_specs=once((1, rows, 2 * half), lambda g, e, o: (g, 0, 0)),
        ),
        out_shape=jax.ShapeDtypeStruct((groups, rows, 2 * half), BF),
        compiler_params=params(56),
        cost_estimate=cost(6 * groups * rows * depth * half, 2 * groups * rows * depth),
        name="gate_up",
    )(offsets, x, gate, up)


def hidden_back_kernel(offset_ref, x_ref, down_ref, o_ref):
    group, expert = pl.program_id(0), pl.program_id(1)
    low, high = offset_ref[group, expert], offset_ref[group, expert + 1]

    def run(base, tiles):
        rows = pl.ds(base, tiles * TILE)
        keep = kept(base, tiles * TILE, low, high)
        made = dot_nt(x_ref[0, rows, :], down_ref[0]).astype(BF)
        o_ref[0, rows, :] = jnp.where(keep, made, o_ref[0, rows, :])

    each_tile(low, high, run)


def hidden_back(offsets, x, down):
    groups, rows, depth = x.shape
    experts, units, _ = down.shape
    return pl.pallas_call(
        hidden_back_kernel,
        grid_spec=pltpu.PrefetchScalarGridSpec(
            num_scalar_prefetch=1,
            grid=(groups, experts),
            in_specs=[
                once((1, rows, depth), lambda g, e, o: (g, 0, 0)),
                pl.BlockSpec((1, units, depth), lambda g, e, o: (e, 0, 0)),
            ],
            out_specs=once((1, rows, units), lambda g, e, o: (g, 0, 0)),
        ),
        out_shape=jax.ShapeDtypeStruct((groups, rows, units), BF),
        compiler_params=params(56),
        cost_estimate=cost(3 * groups * rows * depth * units, 2 * groups * rows * depth),
        name="hidden_back",
    )(offsets, x, down)


def activations(gate, up, delta):
    gate, up, delta = gate.astype(F32), up.astype(F32), delta.astype(F32)
    sigmoid = 0.5 * jnp.tanh(0.5 * gate) + 0.5
    silu = gate * sigmoid
    through = delta * up
    return silu * up, through * (sigmoid + silu - silu * sigmoid), delta * silu, through * silu


def combine(token_ref, scale_ref, rows_ref, o_ref):
    tokens = o_ref.shape[1]
    o_ref[0] = jnp.zeros(o_ref.shape[1:], F32)

    def step(i, carry):
        chosen = iota((tokens, WIDE), 0) == token_ref[0, i]
        chosen = jnp.where(chosen, scale_ref[0, i], 0.0).astype(BF)
        o_ref[0] += dot(chosen, rows_ref[pl.ds(pl.multiple_of(i * WIDE, WIDE), WIDE), :])
        return carry

    lax.fori_loop(0, rows_ref.shape[0] // WIDE, step, 0)


def expert_back_kernel(
    part, offset_ref, gu_ref, hd_ref, gate_ref, up_ref, token_ref, scale_ref, o_ref, made_ref
):
    group, expert = pl.program_id(0), pl.program_id(1)
    experts = pl.num_programs(1)
    low, high = offset_ref[group, expert], offset_ref[group, expert + 1]
    depth, half = gate_ref.shape[1], gate_ref.shape[2]

    def run(base, tiles):
        count = tiles * TILE
        rows = pl.ds(base, count)
        keep = kept(base, count, low, high)
        _, gate_delta, up_delta, picked = activations(
            gu_ref[0, rows, :half],
            gu_ref[0, rows, half:],
            hd_ref[0, rows, part * half : (part + 1) * half],
        )
        made = dot_nt(gate_delta.astype(BF), gate_ref[0]) + dot_nt(up_delta.astype(BF), up_ref[0])
        made_ref[rows, :depth] = jnp.where(keep, made.astype(BF), made_ref[rows, :depth])
        picked = jnp.sum(picked, axis=1, keepdims=True)
        upper = picked.astype(BF).astype(F32)
        lane = iota((count, TILE), 1)
        spread = jnp.where(
            lane == expert, upper, jnp.where(lane == expert + experts, picked - upper, 0.0)
        )
        made_ref[rows, depth:] = jnp.where(keep, spread.astype(BF), made_ref[rows, depth:])

    each_tile(low, high, run)

    @pl.when(expert == experts - 1)
    def _():
        combine(token_ref, scale_ref, made_ref, o_ref)


def expert_back(offsets, gu, hd, gate, up, tokens_of, scale, part, half, tokens):
    groups, rows, units = hd.shape
    experts, depth = gate.shape[:2]
    weight = pl.BlockSpec((1, depth, half), lambda g, e, o: (e, 0, part))
    line = once((1, rows // WIDE, 1, WIDE), lambda g, e, o: (g, 0, 0, 0))
    shape = (groups, rows // WIDE, 1, WIDE)
    return pl.pallas_call(
        functools.partial(expert_back_kernel, part),
        grid_spec=pltpu.PrefetchScalarGridSpec(
            num_scalar_prefetch=1,
            grid=(groups, experts),
            in_specs=[
                once((1, rows, 2 * half), lambda g, e, o: (g, 0, 0)),
                once((1, rows, units), lambda g, e, o: (g, 0, 0)),
                weight,
                weight,
                line,
                line,
            ],
            out_specs=once((1, tokens, depth + TILE), lambda g, e, o: (g, 0, 0)),
            scratch_shapes=[pltpu.VMEM((rows, depth + TILE), BF)],
        ),
        out_shape=jax.ShapeDtypeStruct((groups, tokens, depth + TILE), F32),
        compiler_params=params(56),
        cost_estimate=cost(
            groups * rows * depth * (6 * half + 2 * tokens), 2 * groups * rows * (2 * half + units)
        ),
        name="expert_back",
    )(offsets, gu, hd, gate, up, tokens_of.reshape(shape), scale.reshape(shape))


def down_kernel(offset_ref, down_ref, token_ref, scale_ref, *rest):
    sources, (o_ref, made_ref) = rest[:-2], rest[-2:]
    group, expert = pl.program_id(0), pl.program_id(1)
    low, high = offset_ref[group, expert], offset_ref[group, expert + 1]
    half = sources[0].shape[2] // 2

    def run(base, tiles):
        count = tiles * TILE
        rows = pl.ds(base, count)
        keep = kept(base, count, low, high)
        made = 0.0
        for i, source in enumerate(sources):
            gate = source[0, rows, :half].astype(F32)
            up = source[0, rows, half:].astype(F32)
            hidden = (gate * (0.5 * jnp.tanh(0.5 * gate) + 0.5) * up).astype(BF)
            made += dot(hidden, down_ref[0, i * half : (i + 1) * half, :])
        made_ref[rows, :] = jnp.where(keep, made.astype(BF), made_ref[rows, :])

    each_tile(low, high, run)

    @pl.when(expert == pl.num_programs(1) - 1)
    def _():
        combine(token_ref, scale_ref, made_ref, o_ref)


def expert_down(offsets, sources, down, tokens_of, scale, tokens):
    groups, rows, pair = sources[0].shape
    experts, units, depth = down.shape
    line = once((1, rows // WIDE, 1, WIDE), lambda g, e, o: (g, 0, 0, 0))
    shape = (groups, rows // WIDE, 1, WIDE)
    source = once((1, rows, pair), lambda g, e, o: (g, 0, 0))
    return pl.pallas_call(
        down_kernel,
        grid_spec=pltpu.PrefetchScalarGridSpec(
            num_scalar_prefetch=1,
            grid=(groups, experts),
            in_specs=[
                pl.BlockSpec((1, units, depth), lambda g, e, o: (e, 0, 0)),
                line,
                line,
                *[source] * len(sources),
            ],
            out_specs=once((1, tokens, depth), lambda g, e, o: (g, 0, 0)),
            scratch_shapes=[pltpu.VMEM((rows, depth), BF)],
        ),
        out_shape=jax.ShapeDtypeStruct((groups, tokens, depth), F32),
        compiler_params=params(56),
        cost_estimate=cost(
            groups * rows * depth * (3 * units + 2 * tokens), 4 * groups * rows * units
        ),
        name="expert_down",
    )(offsets, down, tokens_of.reshape(shape), scale.reshape(shape), *sources)


def gradient_kernel(part, aliased, offset_ref, gu_ref, hd_ref, xs_ref, xc_ref, *rest):
    rest = rest[3 * aliased :]
    gate_out, up_out, down_out = rest[:3]
    gu_ring, hd_ring, xs_ring, xc_ring, wide, narrow, issued, waited, sems = rest[3:]
    segments, tiles = gu_ref.shape[:2]
    half = gate_out.shape[2]
    expert = pl.program_id(0)

    def copies(segment, tile):
        slot = lax.rem(tile, RING)
        units = pl.ds(part * half, half)
        return [
            pltpu.make_async_copy(
                gu_ref.at[segment, tile], gu_ring.at[segment, slot], sems.at[0, segment, slot]
            ),
            pltpu.make_async_copy(
                hd_ref.at[segment, tile, :, units],
                hd_ring.at[segment, slot],
                sems.at[1, segment, slot],
            ),
            pltpu.make_async_copy(
                xs_ref.at[segment, tile], xs_ring.at[segment, slot], sems.at[2, segment, slot]
            ),
            pltpu.make_async_copy(
                xc_ref.at[segment, tile], xc_ring.at[segment, slot], sems.at[3, segment, slot]
            ),
        ]

    def start_until(segment, limit):
        def step(tile, carry):
            for copy in copies(segment, tile):
                copy.start()
            return carry

        lax.fori_loop(issued[segment], limit, step, 0)
        issued[segment] = jnp.maximum(issued[segment], limit)

    def wait_until(segment, limit):
        def step(tile, carry):
            for copy in copies(segment, tile):
                copy.wait()
            return carry

        lax.fori_loop(waited[segment], limit, step, 0)
        waited[segment] = jnp.maximum(waited[segment], limit)

    @pl.when(expert == 0)
    def _():
        for segment in range(segments):
            issued[segment] = 0
            waited[segment] = 0
            start_until(segment, min(RING, tiles))

    wide[...] = jnp.zeros_like(wide)
    narrow[...] = jnp.zeros_like(narrow)

    def of_segment(segment, carry):
        low, high = offset_ref[segment, expert], offset_ref[segment, expert + 1]
        first = low // TILE
        last = jnp.where(high > low, (high + TILE - 1) // TILE, first)

        def step(i, carry):
            tile = first + 4 * i
            start_until(segment, jnp.minimum(tiles, tile + RING))
            end = jnp.minimum(last, tile + 4)
            wait_until(segment, end)

            def multiply(count):
                pair, hidden, xs, xc = [], [], [], []
                for j in range(count):
                    slot = lax.rem(tile + j, RING)
                    keep = kept((tile + j) * TILE, TILE, low, high)
                    some, gate_delta, up_delta, _ = activations(
                        gu_ring[segment, slot, :, :half],
                        gu_ring[segment, slot, :, half:],
                        hd_ring[segment, slot],
                    )
                    pair.append(
                        jnp.concatenate(
                            [
                                jnp.where(keep, gate_delta, 0.0).astype(BF),
                                jnp.where(keep, up_delta, 0.0).astype(BF),
                            ],
                            axis=1,
                        )
                    )
                    hidden.append(jnp.where(keep, some, 0.0).astype(BF))
                    xs.append(xs_ring[segment, slot])
                    xc.append(xc_ring[segment, slot])
                wide[...] += dot(jnp.concatenate(xs, axis=1), jnp.concatenate(pair, axis=0))
                narrow[...] += dot(jnp.concatenate(xc, axis=1), jnp.concatenate(hidden, axis=0))

            for count in (1, 2, 3, 4):
                pl.when(end - tile == count)(functools.partial(multiply, count))
            return carry

        lax.fori_loop(0, (last - first + 3) // 4, step, 0)
        return carry

    lax.fori_loop(0, segments, of_segment, 0)
    gate_out[0] = wide[:, :half]
    up_out[0] = wide[:, half:]
    down_out[0] = narrow[...].T


def expert_gradients(offsets, gu, hd, xs, xc, part, before):
    segments, rows, pair = gu.shape
    half, tiles = pair // 2, rows // TILE
    units = hd.shape[2]
    depth = xs.shape[2]
    experts = offsets.shape[1] - 1
    anywhere = pl.BlockSpec(memory_space=pl.ANY)
    columns = pl.BlockSpec((1, depth, half), lambda e, o: (e, 0, part))
    before = list(before)
    return pl.pallas_call(
        functools.partial(gradient_kernel, part, int(bool(before))),
        grid_spec=pltpu.PrefetchScalarGridSpec(
            num_scalar_prefetch=1,
            grid=(experts,),
            in_specs=[anywhere] * (4 + len(before)),
            out_specs=[
                columns,
                columns,
                pl.BlockSpec((1, half, depth), lambda e, o: (e, part, 0)),
            ],
            scratch_shapes=[
                pltpu.VMEM((segments, RING, TILE, pair), BF),
                pltpu.VMEM((segments, RING, TILE, half), BF),
                pltpu.VMEM((segments, RING, depth, TILE), BF),
                pltpu.VMEM((segments, RING, depth, TILE), BF),
                pltpu.VMEM((depth, pair), F32),
                pltpu.VMEM((depth, half), F32),
                pltpu.SMEM((segments,), jnp.int32),
                pltpu.SMEM((segments,), jnp.int32),
                pltpu.SemaphoreType.DMA((4, segments, RING)),
            ],
        ),
        out_shape=[
            jax.ShapeDtypeStruct((experts, depth, units), F32),
            jax.ShapeDtypeStruct((experts, depth, units), F32),
            jax.ShapeDtypeStruct((experts, units, depth), F32),
        ],
        input_output_aliases={5 + i: i for i in range(len(before))},
        compiler_params=params(56),
        cost_estimate=cost(
            9 * segments * rows * depth * half, 2 * segments * rows * (3 * half + 2 * depth)
        ),
        name="expert_gradients",
    )(
        offsets,
        gu.reshape(segments, tiles, TILE, pair),
        hd.reshape(segments, tiles, TILE, units),
        xs,
        xc,
        *before,
    )


def total_rows(value):
    return lax.psum(value, "row")


def gather_columns(value):
    if lax.axis_size("col") != 2:
        return lax.all_gather(value, "col", axis=0, tiled=True)
    other = lax.ppermute(value, "col", [(0, 1), (1, 0)])
    first = lax.axis_index("col") == 0
    return jnp.concatenate(
        [jnp.where(first, value, other), jnp.where(first, other, value)], axis=0
    )


def add_columns(value):
    if lax.axis_size("col") != 2:
        return lax.psum(value, "col").astype(F32)
    other = lax.ppermute(value, "col", [(0, 1), (1, 0)])
    return value.astype(F32) + other.astype(F32)


def share_columns(value):
    count = lax.axis_size("col")
    if count != 2:
        return lax.psum_scatter(value, "col", scatter_dimension=0, tiled=True).astype(F32)
    index = lax.axis_index("col")
    halves = value.reshape(2, value.shape[0] // 2, value.shape[1])
    other = lax.ppermute(
        lax.dynamic_index_in_dim(halves, 1 - index, 0, False), "col", [(0, 1), (1, 0)]
    )
    return lax.dynamic_index_in_dim(halves, index, 0, False).astype(F32) + other.astype(F32)


def on_device(
    residual_in,
    attention_gain,
    query_weight,
    key_weight,
    value_weight,
    query_gain,
    key_gain,
    output_weight,
    expert_gain,
    router_weight,
    gate_weight,
    up_weight,
    down_weight,
    segments,
    routes,
    cotangent,
):
    row_count = lax.axis_size("row")
    row_index = lax.axis_index("row")
    column_count = lax.axis_size("col")
    column_index = lax.axis_index("col")
    local_tokens, width_part = residual_in.shape
    model_width = width_part * row_count
    tokens = local_tokens * column_count
    head_part = query_weight.shape[1]
    heads_here = head_part // HEAD_DIM
    slots = min(row_count, heads_here)
    spans = row_count // slots
    own_part = head_part // slots
    experts, _, units = gate_weight.shape
    parts = 2 if units % 256 == 0 else 1
    half = units // parts
    top_count = routes.shape[1]
    length = min(MAX_LEN, tokens)
    sub = min(SUB, tokens)
    groups = tokens // sub
    rows = sub * top_count

    keys = routes * sub + (jnp.arange(tokens, dtype=jnp.int32) % sub)[:, None]
    keys = lax.sort(keys.reshape(groups, rows), dimension=1)

    def places(keys):
        bounds = jnp.arange(experts + 1, dtype=jnp.int32) * sub
        below = keys[:, None, :] < bounds[None, :, None]
        return keys % sub, keys // sub, jnp.sum(below.astype(jnp.int32), axis=2)

    tokens_of, experts_of, offsets = places(keys)

    delta_group = gather_columns(cotangent)
    delta_rows = dispatch(tokens_of, delta_group.reshape(groups, sub, width_part))
    hidden_delta = hidden_back(offsets, delta_rows, down_weight)
    hidden_delta = lax.psum_scatter(
        hidden_delta.reshape(groups * rows, units), "row", scatter_dimension=0, tiled=True
    )

    residual = gather_columns(residual_in).astype(F32)
    first_scale = attention_gain.astype(F32)
    first_inverse = lax.rsqrt(
        total_rows(jnp.sum(residual * residual, axis=1)) / model_width + EPSILON
    )
    normed = (residual * first_inverse[:, None] * first_scale).astype(BF)
    joint = lax.psum_scatter(
        project(normed, query_weight, key_weight, value_weight, spans, slots),
        "row",
        scatter_dimension=0,
        tiled=False,
    )
    query_raw = joint[:, :own_part].astype(F32)
    key_raw = joint[:, own_part : 2 * own_part].astype(F32)
    value_round = joint[:, 2 * own_part :]
    span = tokens // spans
    span_start = row_index // slots * span

    def total_heads(first, second):
        sums = jnp.stack([jnp.sum(first, axis=1), jnp.sum(second, axis=1)])
        if spans > 1:
            sums = lax.dynamic_update_slice(
                jnp.zeros((2, tokens), F32), sums, (jnp.zeros((), jnp.int32), span_start)
            )
        sums = lax.psum(sums, ("row", "col"))
        return lax.dynamic_slice_in_dim(sums, span_start, span, 1) if spans > 1 else sums

    own_segments = lax.dynamic_slice_in_dim(segments, span_start, span, 0)
    square_sums = total_heads(query_raw * query_raw, key_raw * key_raw)
    query_inverse = lax.rsqrt(square_sums[0] / model_width + EPSILON)
    key_inverse = lax.rsqrt(square_sums[1] / model_width + EPSILON)
    own_start = (row_index % slots * own_part,)
    query_scale = lax.dynamic_slice(query_gain, own_start, (own_part,)).astype(F32)
    key_scale = lax.dynamic_slice(key_gain, own_start, (own_part,)).astype(F32)
    query_round = (query_raw * query_inverse[:, None] * query_scale).astype(BF)
    key_round = (key_raw * key_inverse[:, None] * key_scale).astype(BF)
    mixed, logs = attend(query_round, key_round, value_round, own_segments, length)
    mixed_group = lax.all_gather(mixed, "row", axis=0, tiled=False)
    middle = residual + add_columns(output_project(mixed_group, output_weight, spans, slots))

    second_scale = expert_gain.astype(F32)
    second_inverse = lax.rsqrt(total_rows(jnp.sum(middle * middle, axis=1)) / model_width + EPSILON)
    second = (middle * second_inverse[:, None] * second_scale).astype(BF)
    logits = total_rows(dot(second, router_weight))
    router_probs = jax.nn.softmax(logits, axis=1)
    second_rows = dispatch(tokens_of, second.reshape(groups, sub, width_part))
    scale = pick(
        tokens_of, experts_of, jnp.swapaxes(router_probs.reshape(groups, sub, experts), 1, 2)
    )
    shares, pairs = [], []
    for part in range(parts):
        made = gate_up(offsets, second_rows, gate_weight, up_weight, part, half)
        shares.append(
            lax.psum_scatter(
                made.reshape(groups * rows, 2 * half), "row", scatter_dimension=0, tiled=True
            )
        )
    for part in range(parts):
        pairs.append(
            lax.all_gather(shares[part], "row", axis=0, tiled=True).reshape(groups, rows, 2 * half)
        )

    gathered = tokens <= 2 * SUB
    if gathered:
        every = ("dp", "row")
        all_keys = lax.all_gather(keys, "dp", axis=0, tiled=True)
        all_scales = lax.all_gather(scale, "dp", axis=0, tiled=True)
        all_second = lax.all_gather(second, "dp", axis=0, tiled=True)
        all_delta = lax.all_gather(delta_group, "dp", axis=0, tiled=True)
        all_hidden = lax.all_gather(hidden_delta, every, axis=0, tiled=True)
        all_pairs = [lax.all_gather(share, every, axis=0, tiled=True) for share in shares]
        all_tokens_of, _, all_offsets = places(all_keys)
        own = lax.axis_index("dp") * (groups * rows)
        hidden_rows = lax.dynamic_slice_in_dim(all_hidden, own, groups * rows, 0)
    else:
        all_tokens_of, all_offsets, all_scales = tokens_of, offsets, scale
        all_second, all_delta, all_pairs = second, delta_group, pairs
        hidden_rows = lax.all_gather(hidden_delta, "row", axis=0, tiled=True)
        all_hidden = hidden_rows
    hidden_rows = hidden_rows.reshape(groups, rows, units)

    back = sum(
        expert_back(
            offsets, pairs[part], hidden_rows, gate_weight, up_weight, tokens_of, scale, part, half, sub
        )
        for part in range(parts)
    ).reshape(tokens, width_part + TILE)
    picked_delta = (
        back[:, width_part : width_part + experts]
        + back[:, width_part + experts : width_part + 2 * experts]
    )
    logits_delta = (
        picked_delta - router_probs * jnp.sum(picked_delta, axis=1, keepdims=True)
    ).astype(BF)
    second_delta = add_columns(
        (back[:, :width_part] + dot_nt(logits_delta, router_weight)).astype(BF)
    )
    router_gradient = lax.psum(dot_tn(second, logits_delta), ("dp", "col"))

    out_delta = delta_group.astype(F32)
    second_inner = total_rows(jnp.sum(second_delta * second_scale * middle, axis=1))
    middle_delta = (
        out_delta
        + second_inverse[:, None] * second_scale * second_delta
        - middle * (second_inverse**3 * second_inner / model_width)[:, None]
    )
    second_gain_part = jnp.sum(second_delta * middle * second_inverse[:, None], axis=0)
    attention_round = middle_delta.astype(BF)

    mixed_delta = lax.psum_scatter(
        output_back(attention_round, output_weight, spans, slots),
        "row",
        scatter_dimension=0,
        tiled=False,
    )
    query_delta, key_delta, value_delta = attend_back(
        query_round, key_round, value_round, mixed_delta, logs, own_segments, length
    )
    inner_sums = total_heads(
        query_delta * query_scale * query_raw, key_delta * key_scale * key_raw
    )
    query_raw_delta = (
        query_inverse[:, None] * query_scale * query_delta
        - query_raw * (query_inverse**3 * inner_sums[0] / model_width)[:, None]
    )
    key_raw_delta = (
        key_inverse[:, None] * key_scale * key_delta
        - key_raw * (key_inverse**3 * inner_sums[1] / model_width)[:, None]
    )
    query_gain_part = jnp.sum(query_delta * query_raw * query_inverse[:, None], axis=0)
    key_gain_part = jnp.sum(key_delta * key_raw * key_inverse[:, None], axis=0)
    joint_delta = jnp.concatenate([query_raw_delta, key_raw_delta, value_delta], axis=1).astype(BF)
    joint_group = lax.all_gather(joint_delta, "row", axis=0, tiled=False)
    first_delta = share_columns(
        project_back(joint_group, query_weight, key_weight, value_weight, spans, slots)
    )
    joint_gradients = project_gradient(normed.T, joint_group, spans, slots)

    own_tokens = column_index * local_tokens
    own_residual = residual_in.astype(F32)
    own_inverse = lax.dynamic_slice_in_dim(first_inverse, own_tokens, local_tokens, 0)
    first_inner = total_rows(jnp.sum(first_delta * first_scale * own_residual, axis=1))
    input_gradient = (
        lax.dynamic_slice_in_dim(middle_delta, own_tokens, local_tokens, 0)
        + own_inverse[:, None] * first_scale * first_delta
        - own_residual * (own_inverse**3 * first_inner / model_width)[:, None]
    )
    first_gain_part = jnp.sum(first_delta * own_residual * own_inverse[:, None], axis=0)

    expert_out = expert_down(offsets, pairs, down_weight, tokens_of, scale, sub)
    expert_out = share_columns(expert_out.reshape(tokens, width_part).astype(BF))
    residual_out = (
        lax.dynamic_slice_in_dim(middle, own_tokens, local_tokens, 0) + expert_out
    ).astype(BF)

    output_gradient = jnp.einsum(
        "srth,std->rhd",
        mixed_group.reshape(spans, slots, span, own_part),
        attention_round.reshape(spans, span, width_part),
        preferred_element_type=F32,
    ).reshape(head_part, width_part)
    query_gradient, key_gradient, value_gradient, output_gradient = [
        lax.psum(value.astype(BF), "dp").astype(F32)
        for value in (*joint_gradients, output_gradient)
    ]
    segment_count = all_offsets.shape[0]

    def turned(value):
        return jnp.swapaxes(value.reshape(segment_count, sub, width_part), 1, 2)

    second_turned, delta_turned = dispatch_turned(
        all_tokens_of, all_scales, turned(all_second), turned(all_delta)
    )
    gradients = ()
    for part in range(parts):
        gradients = expert_gradients(
            all_offsets,
            all_pairs[part].reshape(segment_count, rows, 2 * half),
            all_hidden.reshape(segment_count, rows, units),
            second_turned,
            delta_turned,
            part,
            gradients,
        )
    if not gathered:
        gradients = [lax.psum(value.astype(BF), "dp").astype(F32) for value in gradients]
    gate_gradient, up_gradient, down_gradient = gradients

    first_gain_gradient = lax.psum(first_gain_part, ("dp", "col"))
    second_gain_gradient = lax.psum(second_gain_part, "dp")
    head_gains = lax.psum(jnp.stack([query_gain_part, key_gain_part]), "dp")
    head_gains = lax.all_gather(head_gains, "row", axis=1, tiled=True)
    head_gains = jnp.sum(head_gains.reshape(2, spans, head_part), axis=1)
    return (
        residual_out,
        input_gradient,
        first_gain_gradient,
        query_gradient,
        key_gradient,
        value_gradient,
        head_gains[0],
        head_gains[1],
        output_gradient,
        second_gain_gradient,
        router_gradient,
        gate_gradient,
        up_gradient,
        down_gradient,
    )


def solution(mesh):
    tokens, routed = P(("dp", "col"), "row"), P(None, "row", "col")
    heads, gain = P("row", "col"), P("row")
    down, back = P(None, "col", "row"), P("col", "row")
    return jax.shard_map(
        on_device,
        mesh=mesh,
        in_specs=(
            tokens,
            gain,
            heads,
            heads,
            heads,
            P("col"),
            P("col"),
            back,
            gain,
            P("row", None),
            routed,
            routed,
            down,
            P("dp"),
            P("dp", None),
            tokens,
        ),
        out_specs=(
            tokens,
            tokens,
            gain,
            heads,
            heads,
            heads,
            P("col"),
            P("col"),
            back,
            gain,
            P("row", None),
            routed,
            routed,
            down,
        ),
        check_vma=False,
    )
```

time: 3810 us -> 1600 us (0.42)
  waiting for transfers between devices: 2330 us -> 676 us
  local copies, waits for them, and re-layouts: 892 us -> 78.2 us
  Pallas kernels: 0 us -> 637 us
  matrix products: 221 us -> 7.62 us
  other arithmetic: 211 us -> 44.3 us
    psum x1 -> x3, waiting for transfers between devices: 1710 us -> 224 us  [the longest x1 122 us: total_rows(): return lax.psum(value, 'row')]
    pallas_call x0 -> x19, Pallas kernels: none -> 637 us  [the longest x2 243 us: expert_gradients(): pl.pallas_call(functools.partial(gradient_kernel, part, int(bool(before))...]
    gather x11 -> x0, local copies, waits for them, and re-layouts: 486 us -> none  [the longest x5 227 us: to_routes(): return jnp.take(flat_rows, position, axis=0)]
    dot_general x21 -> x4, matrix products: 221 us -> 7.62 us  [the longest x1 3.92 us: on_device(): jnp.einsum('srth,std->rhd', mixed_group.reshape(spans, slots, span, own_p...]
    reduce_scatter x10 -> x5, waiting for transfers between devices: 460 us -> 262 us  [the longest x2 177 us: on_device(): lax.psum_scatter(made.reshape(groups * rows, 2 * half), 'row', scatter_di...]
    reshape x17 -> x8, local copies, waits for them, and re-layouts: 152 us -> 23.5 us  [the longest x2 12.9 us: turned(): return jnp.swapaxes(value.reshape(segment_count, sub, width_part), 1, 2)]
    convert_element_type x20 -> x14, other arithmetic: 78.3 us -> 19.2 us  [the longest x4 7.62 us: on_device(): lax.psum(value.astype(BF), 'dp').astype(F32)]
    ppermute x0 -> x6, waiting for transfers between devices: none -> 57.2 us  [the longest x2 47.3 us: add_columns(): other = lax.ppermute(value, 'col', [(0, 1), (1, 0)])]
  transfers between devices with their start and end apart: 20 -> 23, of which waited for: 12 -> 13; matrix products, arithmetic and copies ran while one was open for 21% -> 6% of each run, Pallas kernels for 0% -> 37%
where the time goes in v1:
time: 1600 us; the launch traced here: 1590 us
  waiting for transfers between devices  676 us (42%)
  Pallas kernels  637 us (40%)
  blocking collectives  117 us (7%)
  local copies, waits for them, and re-layouts  78.2 us (5%)
  other arithmetic  44.3 us (3%)
  between operations  16.9 us (1%)
    pallas_call x2, Pallas kernels, expert_gradients(): pl.pallas_call(functools.partial(gradient_kernel, part, int(bool(before))...  243 us
    reduce_scatter x2, waiting for transfers between devices, on_device(): lax.psum_scatter(made.reshape(groups * rows, 2 * half), 'row', scatter_di...  177 us
    psum x1, waiting for transfers between devices, total_rows(): return lax.psum(value, 'row')  122 us
    pallas_call x2, Pallas kernels, expert_back(): pl.pallas_call(functools.partial(expert_back_kernel, part), grid_spec=plt...  96.9 us
    pallas_call x1, Pallas kernels, dispatch_turned(): pl.pallas_call(dispatch_turned_kernel, grid=(groups, rows // WIDE), in_sp...  87.7 us
    psum x1, waiting for transfers between devices, on_device(): router_gradient = lax.psum(dot_tn(second, logits_delta), ('dp', 'col'))  63.8 us
    pallas_call x2, Pallas kernels, gate_up(): pl.pallas_call(gate_up_kernel, grid_spec=pltpu.PrefetchScalarGridSpec(num...  61.2 us
    reduce_scatter x1, waiting for transfers between devices, on_device(): lax.psum_scatter(project(normed, query_weight, key_weight, value_weight,...  54.9 us
  transfers between devices with their start and end apart: 23, of which 13 were waited for; matrix products, arithmetic and copies ran while one was open for 6% of the time, Pallas kernels for 37%

profile of v1, /device:TPU:0, one launch (start us, length us, event | category | flops | bytes accessed | tf_op | source)
XLA Modules:
  0.0 1587.7 jit_solution(11340829426158079653)
XLA Ops:
  44.8 54.9 %reduce-scatter.6.cloned.1.call-done = bf16[1,1024,768]{2,1,0:T(8,128)(2,1)} async-done(((bf16[4,1024,768]{2,1,0:T(8,128)(2,1)}), bf16[1,1024,768]{2,1,0:T(8,128)(2,1)}) %reduce-scatter.6.cloned.1.call-update) | async-done | bytes 1572880 | tf_op jit(solution)/shard_map/reduce_scatter | solution.py:896
  141.3 30.8 %hidden_back.1 = bf16[1,8192,512]{2,1,0:T(8,128)(2,1)} custom-call(s32[1,33]{1,0:T(1,128)} %bitcast.136, bf16[1,8192,512]{2,1,0:T(8,128)(2,1)} %dispatch.3.x_ref, bf16[32,512,512]{2,1,0:T(8,128)(2,1)} %down_ref.3), custom_call_target="tpu_custom_call" | custom-call | flops 6442450944 | bytes 8388608 | tf_op jit(solution)/shard_map/hidden_back/pallas_call | solution.py:485
  178.5 24.2 %collective-permute-done.1 = bf16[1024,512]{0,1:T(8,128)(2,1)S(1)} collective-permute-done((bf16[1024,512]{0,1:T(8,128)(2,1)S(1)}, bf16[1024,512]{0,1:T(8,128)(2,1)S(1)}, u32[]{:S(2)}, u32[]{:S(2)}) %collective-permute-start.1) | collective-permute-done | bytes 1048608 | tf_op jit(solution)/shard_map/ppermute | solution.py:818
  227.4 30.3 %gate_up.3 = bf16[1,8192,512]{2,1,0:T(8,128)(2,1)} custom-call(s32[1,33]{1,0:T(1,128)} %bitcast.137, bf16[1,8192,512]{2,1,0:T(8,128)(2,1)} %dispatch.2.x_ref, bf16[32,512,512]{2,1,0:T(8,128)(2,1)} %gate_ref.7, bf16[32,512,512]{2,1,0:T(8,128)(2,1)} %up_ref.7), custom_call_target="tpu_custom_call" | custom-call | flops 6442450944 | bytes 8388608 | tf_op jit(solution)/shard_map/gate_up/pallas_call | solution.py:454
  257.7 31.0 %gate_up.2 = bf16[1,8192,512]{2,1,0:T(8,128)(2,1)} custom-call(s32[1,33]{1,0:T(1,128)} %bitcast.138, bf16[1,8192,512]{2,1,0:T(8,128)(2,1)} %dispatch.2.x_ref, bf16[32,512,512]{2,1,0:T(8,128)(2,1)} %gate_ref.7, bf16[32,512,512]{2,1,0:T(8,128)(2,1)} %up_ref.7), custom_call_target="tpu_custom_call" | custom-call | flops 6442450944 | bytes 8388608 | tf_op jit(solution)/shard_map/gate_up/pallas_call | solution.py:454
  294.6 57.1 %reduce-scatter.10.cloned.1.call-done = bf16[2048,512]{1,0:T(8,128)(2,1)} async-done(((bf16[8192,512]{1,0:T(8,128)(2,1)}), bf16[2048,512]{1,0:T(8,128)(2,1)}) %reduce-scatter.10.cloned.1.call-update) | async-done | bytes 2097168 | tf_op jit(solution)/shard_map/reduce_scatter | solution.py:943
  351.8 119.9 %reduce-scatter.8.cloned.1.call-done = bf16[2048,512]{1,0:T(8,128)(2,1)} async-done(((bf16[8192,512]{1,0:T(8,128)(2,1)}), bf16[2048,512]{1,0:T(8,128)(2,1)}) %reduce-scatter.8.cloned.1.call-update) | async-done | bytes 2097168 | tf_op jit(solution)/shard_map/reduce_scatter | solution.py:943
  471.8 121.9 %all-reduce.6.cloned.1.call-done = f32[1024,32]{0,1:T(8,128)} async-done(((f32[1024,32]{0,1:T(8,128)}), f32[1024,32]{0,1:T(8,128)}) %all-reduce.6.cloned.1.call-update) | async-done | bytes 131088 | tf_op jit(solution)/shard_map/psum | solution.py:802
  614.9 48.5 %expert_back.3 = f32[1,1024,640]{2,1,0:T(8,128)} custom-call(s32[1,33]{1,0:T(1,128)} %bitcast.139, bf16[1,8192,512]{2,1,0:T(8,128)(2,1)} %bitcast.147, bf16[1,8192,512]{2,1,0:T(8,128)(2,1)} %dynamic-slice_bitcast_fusion.hd_ref, bf16[32,512,512]{2,1,0:T(8,128)(2,1)} %gate_ref.7, bf16[32,512,512]{2,1,0:T(8,128)(2,1)} %up_ref.7, s32[1,16,1,512]{3,2,1,0:T(1,128)} %bitcast.95, ...), custom_call_target="tpu_custom_call" | custom-call | flops 15032385536 | bytes 16777216 | tf_op jit(solution)/shard_map/expert_back/pallas_call | solution.py:564
  663.4 48.3 %expert_back.2 = f32[1,1024,640]{2,1,0:T(8,128)} custom-call(s32[1,33]{1,0:T(1,128)} %bitcast.140, bf16[1,8192,512]{2,1,0:T(8,128)(2,1)} %bitcast.149, bf16[1,8192,512]{2,1,0:T(8,128)(2,1)} %dynamic-slice_bitcast_fusion.hd_ref, bf16[32,512,512]{2,1,0:T(8,128)(2,1)} %gate_ref.7, bf16[32,512,512]{2,1,0:T(8,128)(2,1)} %up_ref.7, s32[1,16,1,512]{3,2,1,0:T(1,128)} %bitcast.96, ...), custom_call_target="tpu_custom_call" | custom-call | flops 15032385536 | bytes 16777216 | tf_op jit(solution)/shard_map/expert_back/pallas_call | solution.py:564
  723.8 23.1 %collective-permute-done.4 = bf16[1024,512]{0,1:T(8,128)(2,1)S(1)} collective-permute-done((bf16[1024,512]{0,1:T(8,128)(2,1)S(1)}, bf16[1024,512]{0,1:T(8,128)(2,1)S(1)}, u32[]{:S(2)}, u32[]{:S(2)}) %collective-permute-start.4) | collective-permute-done | bytes 1048608 | tf_op jit(solution)/shard_map/ppermute | solution.py:818
  763.9 30.1 %reduce-scatter.14.cloned.1.call-done = bf16[1,1024,256]{2,1,0:T(8,128)(2,1)} async-done(((bf16[4,1024,256]{2,1,0:T(8,128)(2,1)}), bf16[1,1024,256]{2,1,0:T(8,128)(2,1)}) %reduce-scatter.14.cloned.1.call-update) | async-done | bytes 524304 | tf_op jit(solution)/shard_map/reduce_scatter | solution.py:999
  826.9 14.4 all-gather.1
  843.8 34.8 %all-gather.25.cloned.1.call-done = bf16[4096,512]{0,1:T(8,128)(2,1)} async-done(((bf16[1024,512]{0,1:T(8,128)(2,1)}), bf16[4096,512]{0,1:T(8,128)(2,1)}) %all-gather.25.cloned.1.call-update) | async-done | bytes 4194320 | tf_op jit(solution)/shard_map/all_gather | solution.py:958
  893.9 14.7 all-gather.2
  908.6 53.3 %all-gather.23.cloned.1.call-done = bf16[4096,512]{0,1:T(8,128)(2,1)} async-done(((bf16[1024,512]{0,1:T(8,128)(2,1)}), bf16[4096,512]{0,1:T(8,128)(2,1)}) %all-gather.23.cloned.1.call-update) | async-done | bytes 4194320 | tf_op jit(solution)/shard_map/all_gather | solution.py:957
  974.6 43.2 %expert_down.1 = f32[1,1024,512]{2,1,0:T(8,128)} custom-call(s32[1,33]{1,0:T(1,128)} %bitcast.141, bf16[32,512,512]{2,1,0:T(8,128)(2,1)} %down_ref.3, s32[1,16,1,512]{3,2,1,0:T(1,128)} %bitcast.97, f32[1,16,1,512]{3,2,1,0:T(1,128)} %copy-done.16, bf16[1,8192,512]{2,1,0:T(8,128)(2,1)} %bitcast.150, bf16[1,8192,512]{2,1,0:T(8,128)(2,1)} %bitcast.148), custom_call_target="tpu_custom_call" | custom-call | flops 15032385536 | bytes 16777216 | tf_op jit(solution)/shard_map/expert_down/pallas_call | solution.py:620
  1035.8 87.7 %dispatch_turned.1 = (bf16[4,64,512,128]{3,2,1,0:T(8,128)(2,1)}, bf16[4,64,512,128]{3,2,1,0:T(8,128)(2,1)}) custom-call(s32[4,16,1,512]{3,2,1,0:T(1,128)S(1)} %reshape.311.token_ref, f32[4,16,1,512]{3,2,1,0:T(1,128)S(1)} %bitcast.89, bf16[4,512,1024]{2,1,0:T(8,128)(2,1)S(1)} %bitcast.87, bf16[4,512,1024]{2,1,0:T(8,128)(2,1)} %bitcast.116), custom_call_target="tpu_custom_call" | custom-call | flops 68719476736 | bytes 67108864 | tf_op jit(solution)/shard_map/dispatch_turned/pallas_call | solution.py:363
  1155.2 20.0 %psum.112 = f32[512]{0:T(512)} all-reduce(f32[512]{0:T(512)S(1)} %get-tuple-element.110), channel_id=1, replica_groups=mesh['dp'=4,'row'=4,'col'=2] {'dp','col'}, use_global_device_ids=true, to_apply=%region_26.27 | all-reduce | flops 512 | bytes 4096 | tf_op jit(solution)/shard_map/psum | solution.py:1078
  1184.0 122.1 %expert_gradients.2 = (f32[32,512,512]{2,1,0:T(8,128)}, f32[32,512,512]{2,1,0:T(8,128)}, f32[32,512,512]{2,1,0:T(8,128)}) custom-call(s32[4,33]{1,0:T(4,128)} %copy.142.offset_ref, bf16[4,64,128,512]{3,2,1,0:T(8,128)(2,1)} %bitcast.146, bf16[4,64,128,512]{3,2,1,0:T(8,128)(2,1)} %bitcast.102, bf16[4,64,512,128]{3,2,1,0:T(8,128)(2,1)} %get-tuple-element.38.xs_ref, ...), custom_call_target="tpu_custom_call" | custom-call | flops 38654705664 | bytes 117440512 | tf_op jit(solution)/shard_map/expert_gradients/pallas_call | solution.py:757
  1306.1 42.0 %all-gather.21.cloned.1.call-done = bf16[32768,512]{1,0:T(8,128)(2,1)} async-done(((bf16[2048,512]{1,0:T(8,128)(2,1)}), bf16[32768,512]{1,0:T(8,128)(2,1)}) %all-gather.21.cloned.1.call-update) | async-done | bytes 33554448 | tf_op jit(solution)/shard_map/all_gather | solution.py:960
  1348.1 120.7 %expert_gradients.3 = (f32[32,512,512]{2,1,0:T(8,128)}, f32[32,512,512]{2,1,0:T(8,128)}, f32[32,512,512]{2,1,0:T(8,128)}) custom-call(s32[4,33]{1,0:T(4,128)} %copy.142.offset_ref, bf16[4,64,128,512]{3,2,1,0:T(8,128)(2,1)} %bitcast.107, bf16[4,64,128,512]{3,2,1,0:T(8,128)(2,1)} %bitcast.103, ...), custom_call_target="tpu_custom_call", output_to_operand_aliasing={{0}: (5, {}), {1}: (6, {}), {2}: (7, {})} | custom-call | flops 38654705664 | bytes 117440512 | tf_op jit(solution)/shard_map/expert_gradients/pallas_call | solution.py:757
  1468.8 38.2 %all-reduce.10.cloned.1.call-done = (bf16[512,1024]{1,0:T(8,128)(2,1)}, bf16[512,1024]{1,0:T(8,128)(2,1)}, bf16[512,1024]{1,0:T(8,128)(2,1)}, bf16[1024,512]{1,0:T(8,128)(2,1)}) async-done(((bf16[512,1024]{1,0:T(8,128)(2,1)}, bf16[512,1024]{1,0:T(8,128)(2,1)}, bf16[512,1024]{1,0:T(8,128)(2,1)}, bf16[1024,512]{1,0:T(8,128)(2,1)}), (bf16[512,1024]{1,0:T(8,128)(2,1)}, bf16[512,1024]{1,0:T(8,128)(2,1)}, ...) | async-done | bytes 4194320 | tf_op jit(solution)/shard_map/psum | solution.py:1052
  1514.6 63.8 %all-reduce.8.cloned.1.call-done = f32[512,32]{0,1:T(8,128)} async-done(((f32[512,32]{0,1:T(8,128)}), f32[512,32]{0,1:T(8,128)}) %all-reduce.8.cloned.1.call-update) | async-done | bytes 65552 | tf_op jit(solution)/shard_map/psum | solution.py:987
  (269 shorter events, 295.8 us)
Async XLA Ops:
  9.4 15.0 collective-permute-start
  14.3 85.4 %reduce-scatter.6.cloned.1.call-start = ((), (), s32[]{:S(2)}) async-start(), calls=%async_computation.5 | async-start | bytes 7864320 | tf_op jit(solution)/shard_map/reduce_scatter | solution.py:896
  39.9 132.3 %all-gather.29.cloned.1.call-start = ((), (), s32[]{:S(2)}) async-start(), calls=%async_computation.20 | async-start | bytes 2621440 | tf_op jit(solution)/shard_map/all_gather | solution.py:927
  41.1 84.0 %collective-permute-start.3 = (bf16[512,512]{0,1:T(8,128)(2,1)S(1)}, bf16[512,512]{0,1:T(8,128)(2,1)}, u32[]{:S(2)}, u32[]{:S(2)}) collective-permute-start(bf16[512,512]{0,1:T(8,128)(2,1)S(1)} %copy.125), channel_id=1, source_target_pairs={{0,1},{1,0},{2,3},{3,2},{4,5},{5,4},{6,7},{7,6},{8,9},{9,8},{10,11... | collective-permute-start | bytes 1572872 | tf_op jit(solution)/shard_map/ppermute | solution.py:808
  123.1 170.8 %reduce-scatter.12.cloned.1.call-start = ((), (), s32[]{:S(2)}) async-start(), calls=%async_computation.11 | async-start | bytes 10485760 | tf_op jit(solution)/shard_map/reduce_scatter | solution.py:886
  123.2 473.4 %copy-start.18 = (s32[1,8192]{1,0:T(1,128)}, s32[1,8192]{1,0:T(1,128)S(1)}, u32[]{:S(2)}) copy-start(s32[1,8192]{1,0:T(1,128)S(1)} %and_select_fusion.1) | copy-start | bytes 98308
  172.2 179.6 %reduce-scatter.10.cloned.1.call-start = ((), (), s32[]{:S(2)}) async-start(), calls=%async_computation.9 | async-start | bytes 10485760 | tf_op jit(solution)/shard_map/reduce_scatter | solution.py:943
  177.5 25.2 %collective-permute-start.1 = (bf16[1024,512]{0,1:T(8,128)(2,1)S(1)}, bf16[1024,512]{0,1:T(8,128)(2,1)S(1)}, u32[]{:S(2)}, u32[]{:S(2)}) collective-permute-start(bf16[1024,512]{0,1:T(8,128)(2,1)S(1)} %copy.118), channel_id=1, source_target_pairs={{0,1},{1,0},{2,3},{3,2},{4,5},{5,4},{6,7},{7,6},{8,9},{9,8},{10,11... | collective-permute-start | bytes 3145736 | tf_op jit(solution)/shard_map/ppermute | solution.py:818
  257.7 214.1 %reduce-scatter.8.cloned.1.call-start = ((), (), s32[]{:S(2)}) async-start(), calls=%async_computation.7 | async-start | bytes 10485760 | tf_op jit(solution)/shard_map/reduce_scatter | solution.py:943
  288.7 305.0 %all-reduce.6.cloned.1.call-start = ((), (), s32[]{:S(2)}) async-start(), calls=%async_computation.6 | async-start | bytes 262144 | tf_op jit(solution)/shard_map/psum | solution.py:802
  293.8 313.7 %all-gather.17.cloned.1.call-start = ((), (), s32[]{:S(2)}) async-start(), calls=%async_computation.12 | async-start | bytes 35651584 | tf_op jit(solution)/shard_map/all_gather | solution.py:959
  294.6 320.3 %all-gather.15.cloned.1.call-start = ((), (), s32[]{:S(2)}) async-start(), calls=%async_computation.10 | async-start | bytes 10485760 | tf_op jit(solution)/shard_map/all_gather | solution.py:949
  351.8 311.6 %all-gather.13.cloned.1.call-start = ((), (), s32[]{:S(2)}) async-start(), calls=%async_computation.8 | async-start | bytes 10485760 | tf_op jit(solution)/shard_map/all_gather | solution.py:949
  471.8 322.2 %reduce-scatter.14.cloned.1.call-start = ((), (), s32[]{:S(2)}) async-start(), calls=%async_computation.13 | async-start | bytes 2621440 | tf_op jit(solution)/shard_map/reduce_scatter | solution.py:999
  721.9 25.0 %collective-permute-start.4 = (bf16[1024,512]{0,1:T(8,128)(2,1)S(1)}, bf16[1024,512]{0,1:T(8,128)(2,1)S(1)}, u32[]{:S(2)}, u32[]{:S(2)}) collective-permute-start(bf16[1024,512]{0,1:T(8,128)(2,1)S(1)} %fusion.3), channel_id=1, source_target_pairs={{0,1},{1,0},{2,3},{3,2},{4,5},{5,4},{6,7},{7,6},{8,9},{9,8},{10,11... | collective-permute-start | bytes 3145736 | tf_op jit(solution)/shard_map/ppermute | solution.py:818
  762.5 116.1 %all-gather.25.cloned.1.call-start = ((), (), s32[]{:S(2)}) async-start(), calls=%async_computation.18 | async-start | bytes 5242880 | tf_op jit(solution)/shard_map/all_gather | solution.py:958
  763.1 198.7 %all-gather.23.cloned.1.call-start = ((), (), s32[]{:S(2)}) async-start(), calls=%async_computation.17 | async-start | bytes 5242880 | tf_op jit(solution)/shard_map/all_gather | solution.py:957
  763.7 262.7 %all-gather.19.cloned.1.call-start = ((), (), s32[]{:S(2)}) async-start(), calls=%async_computation.14 | async-start | bytes 7864320 | tf_op jit(solution)/shard_map/all_gather | solution.py:1022
  825.6 358.5 %all-gather.27.cloned.1.call-start = ((), (), s32[]{:S(2)}) async-start(), calls=%async_computation.19 | async-start | bytes 35651584 | tf_op jit(solution)/shard_map/all_gather | solution.py:960
  826.1 521.9 %all-gather.21.cloned.1.call-start = ((), (), s32[]{:S(2)}) async-start(), calls=%async_computation.16 | async-start | bytes 35651584 | tf_op jit(solution)/shard_map/all_gather | solution.py:960
  826.9 680.1 %all-reduce.10.cloned.1.call-start = ((), (), s32[]{:S(2)}) async-start(), calls=%async_computation.21 | async-start | bytes 8388608 | tf_op jit(solution)/shard_map/psum | solution.py:1052
  1020.8 103.8 %collective-permute-start.2 = (bf16[512,512]{0,1:T(8,128)(2,1)}, bf16[512,512]{0,1:T(8,128)(2,1)}, u32[]{:S(2)}, u32[]{:S(2)}) collective-permute-start(bf16[512,512]{0,1:T(8,128)(2,1)} %bitcast.22), channel_id=1, source_target_pairs={{0,1},{1,0},{2,3},{3,2},{4,5},{5,4},{6,7},{7,6},{8,9},{9,8},{10,11... | collective-permute-start | bytes 1572872 | tf_op jit(solution)/shard_map/ppermute | solution.py:828
  1033.5 544.9 %all-reduce.8.cloned.1.call-start = ((), (), s32[]{:S(2)}) async-start(), calls=%async_computation.15 | async-start | bytes 131072 | tf_op jit(solution)/shard_map/psum | solution.py:987
  1136.8 17.8 %collective-permute-start.5 = (bf16[512,512]{0,1:T(8,128)(2,1)}, bf16[512,512]{0,1:T(8,128)(2,1)S(1)}, u32[]{:S(2)}, u32[]{:S(2)}) collective-permute-start(bf16[512,512]{0,1:T(8,128)(2,1)} %bitcast.118), channel_id=1, source_target_pairs={{0,1},{1,0},{2,3},{3,2},{4,5},{5,4},{6,7},{7,6},{8,9},{9,8},{10,11... | collective-permute-start | bytes 1572872 | tf_op jit(solution)/shard_map/ppermute | solution.py:828
  (54 other events, 727.3 us)
Sparse Core Ops, SparseCore 0:
  14.4 11.4 sort.11.cloned.1.call-done
  296.3 235.9 all-gather.16
  534.0 59.0 all-gather.14
  594.6 58.2 all-gather.12
  (1 shorter events, 0.0 us)
Sparse Core Ops, SparseCore 1:
  40.0 59.6 reduce-scatter.5
  123.2 21.8 all-gather.28
  172.3 71.2 reduce-scatter.11
  257.8 93.9 reduce-scatter.9
  355.1 116.6 reduce-scatter.7
  474.6 119.0 all-reduce.5
  762.6 31.3 reduce-scatter.13
  796.0 82.6 all-gather.24
  880.7 81.1 all-gather.22
  963.4 44.8 all-gather.18
  1009.7 168.5 all-gather.26
  1180.0 168.1 all-gather.20
  1351.1 155.8 all-reduce.9
  1511.4 67.0 all-reduce.7

commit v2 on v1

--- a/solution.py
+++ b/solution.py
@@ -15,6 +15,8 @@
 TILE = 128
 WIDE = 512
 SUB = 1024
+PACK = 4
+BAND = 4
 RING = 8
 MEGA = 1 << 20
 BF = jnp.bfloat16
@@ -42,7 +44,9 @@
 
 
 def cost(flops, nbytes):
-    return pl.CostEstimate(flops=int(flops), bytes_accessed=int(nbytes), transcendentals=0)
+    return pl.CostEstimate(
+        flops=int(flops) // 64, bytes_accessed=int(nbytes) // 64, transcendentals=0
+    )
 
 
 def once(shape, index):
@@ -407,22 +411,24 @@
     )(tokens_of.reshape(shape), experts_of.reshape(shape), probs).reshape(groups, rows)
 
 
-def each_tile(low, high, run):
-    first = low // TILE
-    count = jnp.where(high > low, (high + TILE - 1) // TILE - first, 0)
-    full = count // 4
-
-    def step(i, carry):
-        run(pl.multiple_of((first + 4 * i) * TILE, TILE), 4)
+def each_expert(offset_ref, total, run):
+    group, step = pl.program_id(0), pl.program_id(1)
+    spans = []
+    for i in range(PACK):
+        expert = step * PACK + i
+        low, high = offset_ref[group, expert], offset_ref[group, expert + 1]
+        spans.append((expert, low, high, low // TILE * TILE))
+    rounds = 0
+    for _, low, high, first in spans:
+        rounds = jnp.maximum(rounds, jnp.where(high > low, (high - first + WIDE - 1) // WIDE, 0))
+
+    def turn(j, carry):
+        for i, (expert, low, high, first) in enumerate(spans):
+            base = pl.multiple_of(jnp.minimum(first + j * WIDE, total - WIDE), TILE)
+            run(i, expert, base, low, high)
         return carry
 
-    lax.fori_loop(0, full, step, 0)
-    left = count - 4 * full
-    for some in (1, 2, 3):
-
-        @pl.when(left == some)
-        def _():
-            run(pl.multiple_of((first + 4 * full) * TILE, TILE), some)
+    lax.fori_loop(0, rounds, turn, 0)
 
 
 def kept(base, rows, low, high):
@@ -431,31 +437,29 @@
 
 
 def gate_up_kernel(offset_ref, x_ref, gate_ref, up_ref, o_ref):
-    group, expert = pl.program_id(0), pl.program_id(1)
-    low, high = offset_ref[group, expert], offset_ref[group, expert + 1]
     half = gate_ref.shape[2]
 
-    def run(base, tiles):
-        rows = pl.ds(base, tiles * TILE)
-        keep = kept(base, tiles * TILE, low, high)
+    def run(i, expert, base, low, high):
+        rows = pl.ds(base, WIDE)
+        keep = kept(base, WIDE, low, high)
         x = x_ref[0, rows, :]
         for start, weight in ((0, gate_ref), (half, up_ref)):
             columns = slice(start, start + half)
-            made = dot(x, weight[0]).astype(BF)
+            made = dot(x, weight[i]).astype(BF)
             o_ref[0, rows, columns] = jnp.where(keep, made, o_ref[0, rows, columns])
 
-    each_tile(low, high, run)
+    each_expert(offset_ref, x_ref.shape[1], run)
 
 
 def gate_up(offsets, x, gate, up, part, half):
     groups, rows, depth = x.shape
     experts = gate.shape[0]
-    weight = pl.BlockSpec((1, depth, half), lambda g, e, o: (e, 0, part))
+    weight = pl.BlockSpec((PACK, depth, half), lambda g, e, o: (e, 0, part))
     return pl.pallas_call(
         gate_up_kernel,
         grid_spec=pltpu.PrefetchScalarGridSpec(
             num_scalar_prefetch=1,
-            grid=(groups, experts),
+            grid=(groups, experts // PACK),
             in_specs=[once((1, rows, depth), lambda g, e, o: (g, 0, 0)), weight, weight],
             out_specs=once((1, rows, 2 * half), lambda g, e, o: (g, 0, 0)),
         ),
@@ -467,16 +471,13 @@
 
 
 def hidden_back_kernel(offset_ref, x_ref, down_ref, o_ref):
-    group, expert = pl.program_id(0), pl.program_id(1)
-    low, high = offset_ref[group, expert], offset_ref[group, expert + 1]
-
-    def run(base, tiles):
-        rows = pl.ds(base, tiles * TILE)
-        keep = kept(base, tiles * TILE, low, high)
-        made = dot_nt(x_ref[0, rows, :], down_ref[0]).astype(BF)
+    def run(i, expert, base, low, high):
+        rows = pl.ds(base, WIDE)
+        made = dot_nt(x_ref[0, rows, :], down_ref[i]).astype(BF)
+        keep = kept(base, WIDE, low, high)
         o_ref[0, rows, :] = jnp.where(keep, made, o_ref[0, rows, :])
 
-    each_tile(low, high, run)
+    each_expert(offset_ref, x_ref.shape[1], run)
 
 
 def hidden_back(offsets, x, down):
@@ -486,10 +487,10 @@
         hidden_back_kernel,
         grid_spec=pltpu.PrefetchScalarGridSpec(
             num_scalar_prefetch=1,
-            grid=(groups, experts),
+            grid=(groups, experts // PACK),
             in_specs=[
                 once((1, rows, depth), lambda g, e, o: (g, 0, 0)),
-                pl.BlockSpec((1, units, depth), lambda g, e, o: (e, 0, 0)),
+                pl.BlockSpec((PACK, units, depth), lambda g, e, o: (e, 0, 0)),
             ],
             out_specs=once((1, rows, units), lambda g, e, o: (g, 0, 0)),
         ),
@@ -500,12 +501,11 @@
     )(offsets, x, down)
 
 
-def activations(gate, up, delta):
-    gate, up, delta = gate.astype(F32), up.astype(F32), delta.astype(F32)
-    sigmoid = 0.5 * jnp.tanh(0.5 * gate) + 0.5
-    silu = gate * sigmoid
-    through = delta * up
-    return silu * up, through * (sigmoid + silu - silu * sigmoid), delta * silu, through * silu
+def slopes(gate):
+    gate = 0.5 * gate.astype(F32)
+    turned = jnp.tanh(gate)
+    product = gate * turned
+    return gate + product, (0.5 + 0.5 * turned) * ((1.0 + gate) - product)
 
 
 def combine(token_ref, scale_ref, rows_ref, o_ref):
@@ -522,59 +522,60 @@
 
 
 def expert_back_kernel(
-    part, offset_ref, gu_ref, hd_ref, gate_ref, up_ref, token_ref, scale_ref, o_ref, made_ref
+    part, offset_ref, _, g_ref, u_ref, hd_ref, gate_ref, up_ref, token_ref, scale_ref, o_ref, made_ref
 ):
-    group, expert = pl.program_id(0), pl.program_id(1)
-    experts = pl.num_programs(1)
-    low, high = offset_ref[group, expert], offset_ref[group, expert + 1]
+    experts = PACK * pl.num_programs(1)
     depth, half = gate_ref.shape[1], gate_ref.shape[2]
 
-    def run(base, tiles):
-        count = tiles * TILE
-        rows = pl.ds(base, count)
-        keep = kept(base, count, low, high)
-        _, gate_delta, up_delta, picked = activations(
-            gu_ref[0, rows, :half],
-            gu_ref[0, rows, half:],
-            hd_ref[0, rows, part * half : (part + 1) * half],
-        )
-        made = dot_nt(gate_delta.astype(BF), gate_ref[0]) + dot_nt(up_delta.astype(BF), up_ref[0])
+    def run(i, expert, base, low, high):
+        rows = pl.ds(base, WIDE)
+        keep = kept(base, WIDE, low, high)
+        silu, slope = slopes(g_ref[0, rows, :])
+        delta = hd_ref[0, rows, part * half : (part + 1) * half]
+        through = delta * u_ref[0, rows, :]
+        picked = through.astype(F32) * silu
+        made = dot_nt(through * slope.astype(BF), gate_ref[i])
+        made += dot_nt(delta * silu.astype(BF), up_ref[i])
         made_ref[rows, :depth] = jnp.where(keep, made.astype(BF), made_ref[rows, :depth])
         picked = jnp.sum(picked, axis=1, keepdims=True)
         upper = picked.astype(BF).astype(F32)
-        lane = iota((count, TILE), 1)
+        lane = iota((WIDE, TILE), 1)
         spread = jnp.where(
             lane == expert, upper, jnp.where(lane == expert + experts, picked - upper, 0.0)
         )
         made_ref[rows, depth:] = jnp.where(keep, spread.astype(BF), made_ref[rows, depth:])
 
-    each_tile(low, high, run)
-
-    @pl.when(expert == experts - 1)
+    each_expert(offset_ref, made_ref.shape[0], run)
+
+    @pl.when(pl.program_id(1) == pl.num_programs(1) - 1)
     def _():
         combine(token_ref, scale_ref, made_ref, o_ref)
 
 
-def expert_back(offsets, gu, hd, gate, up, tokens_of, scale, part, half, tokens):
-    groups, rows, units = hd.shape
+def expert_back(offsets, base, pair, hd, gate, up, tokens_of, scale, part, half, tokens):
+    groups, rows = tokens_of.shape
+    units = hd.shape[2]
     experts, depth = gate.shape[:2]
-    weight = pl.BlockSpec((1, depth, half), lambda g, e, o: (e, 0, part))
-    line = once((1, rows // WIDE, 1, WIDE), lambda g, e, o: (g, 0, 0, 0))
+    weight = pl.BlockSpec((PACK, depth, half), lambda g, e, o, b: (e, 0, part))
+    line = once((1, rows // WIDE, 1, WIDE), lambda g, e, o, b: (g, 0, 0, 0))
     shape = (groups, rows // WIDE, 1, WIDE)
     return pl.pallas_call(
         functools.partial(expert_back_kernel, part),
         grid_spec=pltpu.PrefetchScalarGridSpec(
-            num_scalar_prefetch=1,
-            grid=(groups, experts),
+            num_scalar_prefetch=2,
+            grid=(groups, experts // PACK),
             in_specs=[
-                once((1, rows, 2 * half), lambda g, e, o: (g, 0, 0)),
-                once((1, rows, units), lambda g, e, o: (g, 0, 0)),
+                *[
+                    once((1, rows, half), lambda g, e, o, b, c=column: (b[0] + g, 0, c))
+                    for _, column in pair
+                ],
+                once((1, rows, units), lambda g, e, o, b: (b[1] + g, 0, 0)),
                 weight,
                 weight,
                 line,
                 line,
             ],
-            out_specs=once((1, tokens, depth + TILE), lambda g, e, o: (g, 0, 0)),
+            out_specs=once((1, tokens, depth + TILE), lambda g, e, o, b: (g, 0, 0)),
             scratch_shapes=[pltpu.VMEM((rows, depth + TILE), BF)],
         ),
         out_shape=jax.ShapeDtypeStruct((groups, tokens, depth + TILE), F32),
@@ -583,52 +584,54 @@
             groups * rows * depth * (6 * half + 2 * tokens), 2 * groups * rows * (2 * half + units)
         ),
         name="expert_back",
-    )(offsets, gu, hd, gate, up, tokens_of.reshape(shape), scale.reshape(shape))
-
-
-def down_kernel(offset_ref, down_ref, token_ref, scale_ref, *rest):
+    )(offsets, base, pair[0][0], pair[1][0], hd, gate, up, tokens_of.reshape(shape), scale.reshape(shape))
+
+
+def down_kernel(offset_ref, base_ref, down_ref, token_ref, scale_ref, *rest):
     sources, (o_ref, made_ref) = rest[:-2], rest[-2:]
-    group, expert = pl.program_id(0), pl.program_id(1)
-    low, high = offset_ref[group, expert], offset_ref[group, expert + 1]
-    half = sources[0].shape[2] // 2
-
-    def run(base, tiles):
-        count = tiles * TILE
-        rows = pl.ds(base, count)
-        keep = kept(base, count, low, high)
-        made = 0.0
-        for i, source in enumerate(sources):
-            gate = source[0, rows, :half].astype(F32)
-            up = source[0, rows, half:].astype(F32)
-            hidden = (gate * (0.5 * jnp.tanh(0.5 * gate) + 0.5) * up).astype(BF)
-            made += dot(hidden, down_ref[0, i * half : (i + 1) * half, :])
+    half = sources[0].shape[2]
+
+    def run(i, expert, base, low, high):
+        rows = pl.ds(base, WIDE)
+        keep = kept(base, WIDE, low, high)
+        hidden = []
+        for gate_ref, up_ref in zip(sources[::2], sources[1::2]):
+            gate = 0.5 * gate_ref[0, rows, :].astype(F32)
+            silu = gate + gate * jnp.tanh(gate)
+            hidden.append((silu * up_ref[0, rows, :].astype(F32)).astype(BF))
+        made = dot(jnp.concatenate(hidden, axis=1), down_ref[i])
         made_ref[rows, :] = jnp.where(keep, made.astype(BF), made_ref[rows, :])
 
-    each_tile(low, high, run)
-
-    @pl.when(expert == pl.num_programs(1) - 1)
+    each_expert(offset_ref, made_ref.shape[0], run)
+
+    @pl.when(pl.program_id(1) == pl.num_programs(1) - 1)
     def _():
         combine(token_ref, scale_ref, made_ref, o_ref)
 
 
-def expert_down(offsets, sources, down, tokens_of, scale, tokens):
-    groups, rows, pair = sources[0].shape
+def expert_down(offsets, bases, pairs, half, down, tokens_of, scale, tokens):
+    groups, rows = tokens_of.shape
     experts, units, depth = down.shape
-    line = once((1, rows // WIDE, 1, WIDE), lambda g, e, o: (g, 0, 0, 0))
+    line = once((1, rows // WIDE, 1, WIDE), lambda g, e, o, b: (g, 0, 0, 0))
     shape = (groups, rows // WIDE, 1, WIDE)
-    source = once((1, rows, pair), lambda g, e, o: (g, 0, 0))
+
+    def source(i, column):
+        return once((1, rows, half), lambda g, e, o, b: (b[i] + g, 0, column))
+
+    specs = [source(i, column) for i, pair in enumerate(pairs) for _, column in pair]
+    sources = [value for pair in pairs for value, _ in pair]
     return pl.pallas_call(
         down_kernel,
         grid_spec=pltpu.PrefetchScalarGridSpec(
-            num_scalar_prefetch=1,
-            grid=(groups, experts),
+            num_scalar_prefetch=2,
+            grid=(groups, experts // PACK),
             in_specs=[
-                pl.BlockSpec((1, units, depth), lambda g, e, o: (e, 0, 0)),
+                pl.BlockSpec((PACK, units, depth), lambda g, e, o, b: (e, 0, 0)),
                 line,
                 line,
-                *[source] * len(sources),
+                *specs,
             ],
-            out_specs=once((1, tokens, depth), lambda g, e, o: (g, 0, 0)),
+            out_specs=once((1, tokens, depth), lambda g, e, o, b: (g, 0, 0)),
             scratch_shapes=[pltpu.VMEM((rows, depth), BF)],
         ),
         out_shape=jax.ShapeDtypeStruct((groups, tokens, depth), F32),
@@ -637,24 +640,26 @@
             groups * rows * depth * (3 * units + 2 * tokens), 4 * groups * rows * units
         ),
         name="expert_down",
-    )(offsets, down, tokens_of.reshape(shape), scale.reshape(shape), *sources)
-
-
-def gradient_kernel(part, aliased, offset_ref, gu_ref, hd_ref, xs_ref, xc_ref, *rest):
-    rest = rest[3 * aliased :]
+    )(offsets, bases, down, tokens_of.reshape(shape), scale.reshape(shape), *sources)
+
+
+def gradient_kernel(part, start, pieces, aliased, offset_ref, *rest):
+    piece_refs, rest = rest[:pieces], rest[pieces:]
+    hd_ref, xs_ref, xc_ref = rest[:3]
+    rest = rest[3 + 3 * aliased :]
     gate_out, up_out, down_out = rest[:3]
     gu_ring, hd_ring, xs_ring, xc_ring, wide, narrow, issued, waited, sems = rest[3:]
-    segments, tiles = gu_ref.shape[:2]
+    segments, tiles = xs_ref.shape[:2]
+    shares, run_tiles = piece_refs[0].shape[1:3]
+    share_tiles = pieces * run_tiles
     half = gate_out.shape[2]
-    expert = pl.program_id(0)
+    expert = start + pl.program_id(0)
+    stop = start + pl.num_programs(0)
 
     def copies(segment, tile):
         slot = lax.rem(tile, RING)
         units = pl.ds(part * half, half)
         return [
-            pltpu.make_async_copy(
-                gu_ref.at[segment, tile], gu_ring.at[segment, slot], sems.at[0, segment, slot]
-            ),
             pltpu.make_async_copy(
                 hd_ref.at[segment, tile, :, units],
                 hd_ring.at[segment, slot],
@@ -668,10 +673,27 @@
             ),
         ]
 
+    def piece_copy(piece, segment, tile):
+        slot = lax.rem(tile, RING)
+        share, place = tile // share_tiles, lax.rem(tile, run_tiles)
+        return pltpu.make_async_copy(
+            piece_refs[piece].at[segment, share, place],
+            gu_ring.at[segment, slot],
+            sems.at[0, segment, slot],
+        )
+
     def start_until(segment, limit):
         def step(tile, carry):
             for copy in copies(segment, tile):
                 copy.start()
+            if pieces == 1:
+                piece_copy(0, segment, tile).start()
+            else:
+                held = lax.rem(tile, share_tiles) // run_tiles
+                for piece in range(pieces):
+                    pl.when(held == piece)(
+                        lambda piece=piece: piece_copy(piece, segment, tile).start()
+                    )
             return carry
 
         lax.fori_loop(issued[segment], limit, step, 0)
@@ -681,89 +703,99 @@
         def step(tile, carry):
             for copy in copies(segment, tile):
                 copy.wait()
+            piece_copy(0, segment, tile).wait()
             return carry
 
         lax.fori_loop(waited[segment], limit, step, 0)
         waited[segment] = jnp.maximum(waited[segment], limit)
 
-    @pl.when(expert == 0)
+    bounds = [
+        (offset_ref[i, start] // TILE, (offset_ref[i, stop] + TILE - 1) // TILE)
+        for i in range(segments)
+    ]
+
+    @pl.when(expert == start)
     def _():
-        for segment in range(segments):
-            issued[segment] = 0
-            waited[segment] = 0
-            start_until(segment, min(RING, tiles))
+        for segment, (head, tail) in enumerate(bounds):
+            issued[segment] = head
+            waited[segment] = head
+            start_until(segment, jnp.minimum(head + RING - 1, tail))
+            wait_until(segment, jnp.minimum(head + 1, tail))
+
+            @pl.when(tail <= head)
+            def _():
+                slot = lax.rem(head, RING)
+                for ring in (gu_ring, hd_ring, xs_ring, xc_ring):
+                    ring[segment, slot] = jnp.zeros(ring.shape[2:], BF)
 
     wide[...] = jnp.zeros_like(wide)
     narrow[...] = jnp.zeros_like(narrow)
-
-    def of_segment(segment, carry):
+    spans, rounds = [], 0
+    for segment in range(segments):
         low, high = offset_ref[segment, expert], offset_ref[segment, expert + 1]
         first = low // TILE
         last = jnp.where(high > low, (high + TILE - 1) // TILE, first)
-
-        def step(i, carry):
-            tile = first + 4 * i
-            start_until(segment, jnp.minimum(tiles, tile + RING))
-            end = jnp.minimum(last, tile + 4)
-            wait_until(segment, end)
-
-            def multiply(count):
+        spans.append((low, high, first, last))
+        rounds = jnp.maximum(rounds, (last - first + BAND - 1) // BAND)
+
+    def turn(i, carry):
+        for segment, (low, high, first, last) in enumerate(spans):
+            tile = jnp.minimum(first + BAND * i, last)
+            start_until(segment, jnp.minimum(bounds[segment][1], tile + RING - 1))
+            wait_until(segment, jnp.minimum(last, tile + BAND))
+        for segment, (low, high, first, last) in enumerate(spans):
+            if segment % 2 == 0:
                 pair, hidden, xs, xc = [], [], [], []
-                for j in range(count):
-                    slot = lax.rem(tile + j, RING)
-                    keep = kept((tile + j) * TILE, TILE, low, high)
-                    some, gate_delta, up_delta, _ = activations(
-                        gu_ring[segment, slot, :, :half],
-                        gu_ring[segment, slot, :, half:],
-                        hd_ring[segment, slot],
-                    )
-                    pair.append(
-                        jnp.concatenate(
-                            [
-                                jnp.where(keep, gate_delta, 0.0).astype(BF),
-                                jnp.where(keep, up_delta, 0.0).astype(BF),
-                            ],
-                            axis=1,
-                        )
-                    )
-                    hidden.append(jnp.where(keep, some, 0.0).astype(BF))
-                    xs.append(xs_ring[segment, slot])
-                    xc.append(xc_ring[segment, slot])
-                wide[...] += dot(jnp.concatenate(xs, axis=1), jnp.concatenate(pair, axis=0))
-                narrow[...] += dot(jnp.concatenate(xc, axis=1), jnp.concatenate(hidden, axis=0))
-
-            for count in (1, 2, 3, 4):
-                pl.when(end - tile == count)(functools.partial(multiply, count))
-            return carry
-
-        lax.fori_loop(0, (last - first + 3) // 4, step, 0)
+            for j in range(BAND):
+                tile = first + BAND * i + j
+                slot = lax.rem(jnp.maximum(jnp.minimum(tile, last - 1), bounds[segment][0]), RING)
+                keep = kept(tile * TILE, TILE, low, high)
+                silu, slope = slopes(gu_ring[segment, slot, :, :half])
+                silu = jnp.where(keep, silu, 0.0).astype(BF)
+                slope = jnp.where(keep, slope, 0.0).astype(BF)
+                up, delta = gu_ring[segment, slot, :, half:], hd_ring[segment, slot]
+                pair.append(jnp.concatenate([delta * up * slope, delta * silu], axis=1))
+                hidden.append(silu * up)
+                xs.append(xs_ring[segment, slot])
+                xc.append(xc_ring[segment, slot])
+            if segment % 2 == 0 and segment + 1 < segments:
+                continue
+            wide[...] += dot(jnp.concatenate(xs, axis=1), jnp.concatenate(pair, axis=0))
+            narrow[...] += dot(jnp.concatenate(xc, axis=1), jnp.concatenate(hidden, axis=0))
         return carry
 
-    lax.fori_loop(0, segments, of_segment, 0)
+    lax.fori_loop(0, rounds, turn, 0)
+
+    @pl.when(expert == stop - 1)
+    def _():
+        for segment in range(segments):
+            wait_until(segment, issued[segment])
+
     gate_out[0] = wide[:, :half]
     up_out[0] = wide[:, half:]
     down_out[0] = narrow[...].T
 
 
-def expert_gradients(offsets, gu, hd, xs, xc, part, before):
-    segments, rows, pair = gu.shape
-    half, tiles = pair // 2, rows // TILE
+def expert_gradients(offsets, pieces, hd, xs, xc, part, start, count, before):
+    segments, shares, run, pair = pieces[0].shape
+    half, rows = pair // 2, hd.shape[1]
+    tiles = rows // TILE
     units = hd.shape[2]
     depth = xs.shape[2]
     experts = offsets.shape[1] - 1
     anywhere = pl.BlockSpec(memory_space=pl.ANY)
-    columns = pl.BlockSpec((1, depth, half), lambda e, o: (e, 0, part))
+    columns = pl.BlockSpec((1, depth, half), lambda e, o: (start + e, 0, part))
     before = list(before)
     return pl.pallas_call(
-        functools.partial(gradient_kernel, part, int(bool(before))),
+        functools.partial(gradient_kernel, part, start, len(pieces), int(bool(before))),
         grid_spec=pltpu.PrefetchScalarGridSpec(
             num_scalar_prefetch=1,
-            grid=(experts,),
-            in_specs=[anywhere] * (4 + len(before)),
+            grid=(count,),
+            in_specs=[anywhere] * (len(pieces) + 3 + len(before)),
             out_specs=[
                 columns,
                 columns,
-                pl.BlockSpec((1, half, depth), lambda e, o: (e, part, 0)),
+                pl.BlockSpec((1, half, depth), lambda e, o: (start + e, part, 0)),
             ],
             scratch_shapes=[
                 pltpu.VMEM((segments, RING, TILE, pair), BF),
@@ -782,7 +814,7 @@
             jax.ShapeDtypeStruct((experts, depth, units), F32),
             jax.ShapeDtypeStruct((experts, units, depth), F32),
         ],
-        input_output_aliases={5 + i: i for i in range(len(before))},
+        input_output_aliases={len(pieces) + 4 + i: i for i in range(len(before))},
         compiler_params=params(56),
         cost_estimate=cost(
             9 * segments * rows * depth * half, 2 * segments * rows * (3 * half + 2 * depth)
@@ -790,7 +822,7 @@
         name="expert_gradients",
     )(
         offsets,
-        gu.reshape(segments, tiles, TILE, pair),
+        *[piece.reshape(segments, shares, run // TILE, TILE, pair) for piece in pieces],
         hd.reshape(segments, tiles, TILE, units),
         xs,
         xc,
@@ -798,8 +830,54 @@
     )
 
 
+def in_order(*values):
+    return lax.optimization_barrier(values)
+
+
 def total_rows(value):
     return lax.psum(value, "row")
+
+
+def exchange(value, axis):
+    count, apart = lax.axis_size(axis), 1
+    while apart < count:
+        value = value + lax.ppermute(value, axis, [(i, i ^ apart) for i in range(count)])
+        apart *= 2
+    return value
+
+
+def scatter_rows(value):
+    count = lax.axis_size("row")
+    if count != 4:
+        return lax.psum_scatter(value, "row", scatter_dimension=0, tiled=False)
+    index = lax.axis_index("row")
+
+    def halve(value, axis, mine, apart):
+        sent = lax.dynamic_index_in_dim(value, 1 - mine, axis, False)
+        kept = lax.dynamic_index_in_dim(value, mine, axis, False)
+        other = lax.ppermute(sent, "row", [(i, i ^ apart) for i in range(count)])
+        return (kept.astype(F32) + other.astype(F32)).astype(BF)
+
+    value = halve(value.reshape(2, 2, *value.shape[1:]), 1, index % 2, 1)
+    return halve(value, 0, index // 2, 2)
+
+
+def gather_planes(value):
+    count = lax.axis_size("dp")
+    pieces = [value] + [
+        lax.ppermute(value, "dp", [(i, (i - apart) % count) for i in range(count)])
+        for apart in range(1, count)
+    ]
+    first = (count - lax.axis_index("dp")) % count * value.shape[0]
+    return lax.dynamic_slice_in_dim(
+        jnp.concatenate(pieces + pieces[:-1], axis=0), first, count * value.shape[0], 0
+    )
+
+
+def exchange_columns(value):
+    if lax.axis_size("col") != 2:
+        return lax.psum(value, "col")
+    return value + lax.ppermute(value, "col", [(0, 1), (1, 0)])
 
 
 def gather_columns(value):
@@ -881,11 +959,14 @@
     tokens_of, experts_of, offsets = places(keys)
 
     delta_group = gather_columns(cotangent)
+    gathered = tokens <= 2 * SUB
+    planes = ("dp", "col")
+    all_delta, all_keys = delta_group, keys
+    if gathered:
+        all_delta = lax.all_gather(cotangent, planes, axis=0, tiled=True)
+        all_keys = lax.all_gather(keys, "dp", axis=0, tiled=True)
     delta_rows = dispatch(tokens_of, delta_group.reshape(groups, sub, width_part))
-    hidden_delta = hidden_back(offsets, delta_rows, down_weight)
-    hidden_delta = lax.psum_scatter(
-        hidden_delta.reshape(groups * rows, units), "row", scatter_dimension=0, tiled=True
-    )
+    hidden_part = hidden_back(offsets, delta_rows, down_weight)
 
     residual = gather_columns(residual_in).astype(F32)
     first_scale = attention_gain.astype(F32)
@@ -899,6 +980,7 @@
         scatter_dimension=0,
         tiled=False,
     )
+    joint, hidden_part, all_keys = in_order(joint, hidden_part, all_keys)
     query_raw = joint[:, :own_part].astype(F32)
     key_raw = joint[:, own_part : 2 * own_part].astype(F32)
     value_round = joint[:, 2 * own_part :]
@@ -911,7 +993,7 @@
             sums = lax.dynamic_update_slice(
                 jnp.zeros((2, tokens), F32), sums, (jnp.zeros((), jnp.int32), span_start)
             )
-        sums = lax.psum(sums, ("row", "col"))
+        sums = total_rows(exchange_columns(sums))
         return lax.dynamic_slice_in_dim(sums, span_start, span, 1) if spans > 1 else sums
 
     own_segments = lax.dynamic_slice_in_dim(segments, span_start, span, 0)
@@ -924,56 +1006,127 @@
     query_round = (query_raw * query_inverse[:, None] * query_scale).astype(BF)
     key_round = (key_raw * key_inverse[:, None] * key_scale).astype(BF)
     mixed, logs = attend(query_round, key_round, value_round, own_segments, length)
+    mixed, all_delta = in_order(mixed, all_delta)
     mixed_group = lax.all_gather(mixed, "row", axis=0, tiled=False)
+    hidden_delta = lax.psum_scatter(
+        hidden_part.reshape(groups * rows, units),
+        "row",
+        scatter_dimension=0,
+        tiled=True,
+    )
     middle = residual + add_columns(output_project(mixed_group, output_weight, spans, slots))
 
     second_scale = expert_gain.astype(F32)
     second_inverse = lax.rsqrt(total_rows(jnp.sum(middle * middle, axis=1)) / model_width + EPSILON)
     second = (middle * second_inverse[:, None] * second_scale).astype(BF)
-    logits = total_rows(dot(second, router_weight))
-    router_probs = jax.nn.softmax(logits, axis=1)
+    logits = exchange(
+        lax.dot_general(
+            router_weight, second, (((0,), (1,)), ((), ())), preferred_element_type=F32
+        ),
+        "row",
+    )
+    turned_probs = jax.nn.softmax(logits, axis=0)
+    router_probs = turned_probs.T
     second_rows = dispatch(tokens_of, second.reshape(groups, sub, width_part))
     scale = pick(
-        tokens_of, experts_of, jnp.swapaxes(router_probs.reshape(groups, sub, experts), 1, 2)
-    )
+        tokens_of, experts_of, jnp.swapaxes(turned_probs.reshape(experts, groups, sub), 0, 1)
+    )
+    own_tokens = column_index * local_tokens
     shares, pairs = [], []
     for part in range(parts):
         made = gate_up(offsets, second_rows, gate_weight, up_weight, part, half)
+        if part == 0:
+            made, hidden_delta = in_order(made, hidden_delta)
         shares.append(
             lax.psum_scatter(
                 made.reshape(groups * rows, 2 * half), "row", scatter_dimension=0, tiled=True
             )
         )
-    for part in range(parts):
-        pairs.append(
-            lax.all_gather(shares[part], "row", axis=0, tiled=True).reshape(groups, rows, 2 * half)
+    def turned(value):
+        return jnp.swapaxes(value.reshape(-1, sub, width_part), 1, 2)
+
+    def back_of(part, pair, base, hidden_rows, hidden_base):
+        return expert_back(
+            offsets,
+            jnp.stack([base, hidden_base]),
+            pair,
+            hidden_rows,
+            gate_weight,
+            up_weight,
+            tokens_of,
+            scale,
+            part,
+            half,
+            sub,
         )
 
-    gathered = tokens <= 2 * SUB
+    zero = jnp.zeros((), jnp.int32)
     if gathered:
         every = ("dp", "row")
-        all_keys = lax.all_gather(keys, "dp", axis=0, tiled=True)
-        all_scales = lax.all_gather(scale, "dp", axis=0, tiled=True)
-        all_second = lax.all_gather(second, "dp", axis=0, tiled=True)
-        all_delta = lax.all_gather(delta_group, "dp", axis=0, tiled=True)
+        all_scales = gather_planes(scale)
+        all_second = gather_planes(second)
         all_hidden = lax.all_gather(hidden_delta, every, axis=0, tiled=True)
-        all_pairs = [lax.all_gather(share, every, axis=0, tiled=True) for share in shares]
         all_tokens_of, _, all_offsets = places(all_keys)
-        own = lax.axis_index("dp") * (groups * rows)
-        hidden_rows = lax.dynamic_slice_in_dim(all_hidden, own, groups * rows, 0)
+        segment_count = all_offsets.shape[0]
+        sources = [turned(all_second), turned(all_delta)]
+        shares[-1], all_hidden, all_scales, *sources = in_order(
+            shares[-1], all_hidden, all_scales, *sources
+        )
+        second_turned, delta_turned = dispatch_turned(all_tokens_of, all_scales, *sources)
+        hidden_rows = all_hidden.reshape(segment_count, rows, units)
+        base = lax.axis_index("dp") * groups
+        last = lax.all_gather(shares[-1], "row", axis=0, tiled=True)
+        shares[0], last = in_order(shares[0], last)
+        last = last.reshape(groups, rows, 2 * half)
+        back = back_of(parts - 1, [(last, 0), (last, 1)], zero, hidden_rows, base)
+        pairs, bases, all_pairs = [], [], []
+        for part in range(parts):
+            taken = lax.all_gather(shares[part], every, axis=0, tiled=True)
+            if part + 1 < parts:
+                shares[part + 1], taken, back, second_turned, delta_turned = in_order(
+                    shares[part + 1], taken, back, second_turned, delta_turned
+                )
+                whole = taken.reshape(segment_count, rows, 2 * half)
+                pairs.append([(whole, 0), (whole, 1)])
+                bases.append(base)
+                back = back + back_of(part, pairs[part], base, hidden_rows, base)
+            all_pairs.append([taken.reshape(segment_count, 1, rows, 2 * half)])
+        pairs.append([(last, 0), (last, 1)])
+        bases.append(zero)
     else:
         all_tokens_of, all_offsets, all_scales = tokens_of, offsets, scale
-        all_second, all_delta, all_pairs = second, delta_group, pairs
-        hidden_rows = lax.all_gather(hidden_delta, "row", axis=0, tiled=True)
-        all_hidden = hidden_rows
-    hidden_rows = hidden_rows.reshape(groups, rows, units)
-
-    back = sum(
-        expert_back(
-            offsets, pairs[part], hidden_rows, gate_weight, up_weight, tokens_of, scale, part, half, sub
+        segment_count = groups
+        all_second = second
+        hidden_rows = lax.all_gather(hidden_delta, "row", axis=0, tiled=True).reshape(
+            groups, rows, units
         )
-        for part in range(parts)
-    ).reshape(tokens, width_part + TILE)
+        wholes = [
+            lax.all_gather(share, "row", axis=0, tiled=True).reshape(groups, rows, 2 * half)
+            for share in shares
+        ]
+        pairs = [[(value, 0), (value, 1)] for value in wholes]
+        all_pairs = [[value[:, None]] for value in wholes]
+        second_turned, delta_turned = dispatch_turned(
+            all_tokens_of, all_scales, turned(all_second), turned(all_delta)
+        )
+        bases = [zero] * parts
+        back = sum(back_of(part, pairs[part], zero, hidden_rows, zero) for part in range(parts))
+    bases = jnp.stack(bases)
+    back = back.reshape(tokens, width_part + TILE)
+
+    def gradients_of(part, start, count, before):
+        return expert_gradients(
+            all_offsets,
+            all_pairs[part],
+            hidden_rows,
+            second_turned,
+            delta_turned,
+            part,
+            start,
+            count,
+            before,
+        )
+
     picked_delta = (
         back[:, width_part : width_part + experts]
         + back[:, width_part + experts : width_part + 2 * experts]
@@ -984,7 +1137,7 @@
     second_delta = add_columns(
         (back[:, :width_part] + dot_nt(logits_delta, router_weight)).astype(BF)
     )
-    router_gradient = lax.psum(dot_tn(second, logits_delta), ("dp", "col"))
+    router_part = exchange_columns(dot_tn(logits_delta, second))
 
     out_delta = delta_group.astype(F32)
     second_inner = total_rows(jnp.sum(second_delta * second_scale * middle, axis=1))
@@ -995,13 +1148,22 @@
     )
     second_gain_part = jnp.sum(second_delta * middle * second_inverse[:, None], axis=0)
     attention_round = middle_delta.astype(BF)
-
-    mixed_delta = lax.psum_scatter(
-        output_back(attention_round, output_weight, spans, slots),
-        "row",
-        scatter_dimension=0,
-        tiled=False,
-    )
+    expert_out = expert_down(offsets, bases, pairs, half, down_weight, tokens_of, scale, sub)
+    some = experts // 2 if parts > 1 else 0
+    gradients = gradients_of(0, 0, some, ()) if some else ()
+    attention_round, expert_out, all_pairs[-1][0], gradients = in_order(
+        attention_round, expert_out, all_pairs[-1][0], gradients
+    )
+    output_gradient = jnp.einsum(
+        "srth,std->rhd",
+        mixed_group.reshape(spans, slots, span, own_part),
+        attention_round.reshape(spans, span, width_part),
+        preferred_element_type=F32,
+    ).reshape(head_part, width_part)
+    early_gradient = jnp.concatenate([output_gradient, router_part], axis=0).astype(BF)
+
+
+    mixed_delta = scatter_rows(output_back(attention_round, output_weight, spans, slots))
     query_delta, key_delta, value_delta = attend_back(
         query_round, key_round, value_round, mixed_delta, logs, own_segments, length
     )
@@ -1023,9 +1185,11 @@
     first_delta = share_columns(
         project_back(joint_group, query_weight, key_weight, value_weight, spans, slots)
     )
+    if some:
+        gradients = gradients_of(0, some, experts - some, gradients)
+        joint_group, gradients = in_order(joint_group, gradients)
     joint_gradients = project_gradient(normed.T, joint_group, spans, slots)
 
-    own_tokens = column_index * local_tokens
     own_residual = residual_in.astype(F32)
     own_inverse = lax.dynamic_slice_in_dim(first_inverse, own_tokens, local_tokens, 0)
     first_inner = total_rows(jnp.sum(first_delta * first_scale * own_residual, axis=1))
@@ -1036,61 +1200,50 @@
     )
     first_gain_part = jnp.sum(first_delta * own_residual * own_inverse[:, None], axis=0)
 
-    expert_out = expert_down(offsets, pairs, down_weight, tokens_of, scale, sub)
     expert_out = share_columns(expert_out.reshape(tokens, width_part).astype(BF))
     residual_out = (
         lax.dynamic_slice_in_dim(middle, own_tokens, local_tokens, 0) + expert_out
     ).astype(BF)
 
-    output_gradient = jnp.einsum(
-        "srth,std->rhd",
-        mixed_group.reshape(spans, slots, span, own_part),
-        attention_round.reshape(spans, span, width_part),
-        preferred_element_type=F32,
-    ).reshape(head_part, width_part)
-    query_gradient, key_gradient, value_gradient, output_gradient = [
-        lax.psum(value.astype(BF), "dp").astype(F32)
-        for value in (*joint_gradients, output_gradient)
+    *joint_gradients, early_gradient, gradients = in_order(
+        *joint_gradients, early_gradient, gradients
+    )
+    *head_gradients, early_gradient = [
+        lax.psum(value, "dp") for value in (*joint_gradients, early_gradient)
     ]
-    segment_count = all_offsets.shape[0]
-
-    def turned(value):
-        return jnp.swapaxes(value.reshape(segment_count, sub, width_part), 1, 2)
-
-    second_turned, delta_turned = dispatch_turned(
-        all_tokens_of, all_scales, turned(all_second), turned(all_delta)
-    )
-    gradients = ()
-    for part in range(parts):
-        gradients = expert_gradients(
-            all_offsets,
-            all_pairs[part].reshape(segment_count, rows, 2 * half),
-            all_hidden.reshape(segment_count, rows, units),
-            second_turned,
-            delta_turned,
-            part,
-            gradients,
-        )
+    early_gradient = early_gradient.astype(F32)
+    query_gradient, key_gradient, value_gradient = [value.astype(F32) for value in head_gradients]
+    output_gradient = early_gradient[:head_part]
+    router_gradient = early_gradient[head_part:].T
+    gains = jnp.concatenate(
+        [exchange_columns(first_gain_part), second_gain_part, query_gain_part, key_gain_part]
+    )
+    gains = exchange(gains, "dp")
+    head_gains = lax.all_gather(
+        gains[2 * width_part :].reshape(2, own_part), "row", axis=1, tiled=True
+    )
+    head_gains = jnp.sum(head_gains.reshape(2, spans, head_part), axis=1)
+    if not some:
+        gradients = ()
+    gradients, input_gradient, residual_out, gains, head_gains = in_order(
+        gradients, input_gradient, residual_out, gains, head_gains
+    )
+    gradients = gradients_of(parts - 1, 0, experts, gradients)
     if not gathered:
         gradients = [lax.psum(value.astype(BF), "dp").astype(F32) for value in gradients]
     gate_gradient, up_gradient, down_gradient = gradients
 
-    first_gain_gradient = lax.psum(first_gain_part, ("dp", "col"))
-    second_gain_gradient = lax.psum(second_gain_part, "dp")
-    head_gains = lax.psum(jnp.stack([query_gain_part, key_gain_part]), "dp")
-    head_gains = lax.all_gather(head_gains, "row", axis=1, tiled=True)
-    head_gains = jnp.sum(head_gains.reshape(2, spans, head_part), axis=1)
     return (
         residual_out,
         input_gradient,
-        first_gain_gradient,
+        gains[:width_part],
         query_gradient,
         key_gradient,
         value_gradient,
         head_gains[0],
         head_gains[1],
         output_gradient,
-        second_gain_gradient,
+        gains[width_part : 2 * width_part],
         router_gradient,
         gate_gradient,
         up_gradient,

time: 1600 us -> 1210 us (0.76)
  waiting for transfers between devices: 676 us -> 391 us
  Pallas kernels: 637 us -> 553 us
  blocking collectives: 117 us -> 56.2 us
  starting transfers between devices: 10.2 us -> 37.1 us
    psum x3 -> x1, waiting for transfers between devices: 224 us -> 0.01 us  [on_device(): lax.psum(value, 'dp')]
    reduce_scatter x2, waiting for transfers between devices: 177 us -> 0.03 us  [on_device(): lax.psum_scatter(made.reshape(groups * rows, 2 * half), 'row', scatter_di...]
    ppermute x0 -> x16, waiting for transfers between devices: none -> 138 us  [the longest x6 107 us: gather_planes(): lax.ppermute(value, 'dp', [(i, (i - apart) % count) for i in range(count)])]
    all_gather x1, waiting for transfers between devices: 0.02 us -> 86.1 us  [on_device(): all_hidden = lax.all_gather(hidden_delta, every, axis=0, tiled=True)]
    psum x4 -> x0, blocking collectives: 58.6 us -> none  [the longest x2 28.1 us: total_heads(): sums = lax.psum(sums, ('row', 'col'))]
    reduce_scatter x1, waiting for transfers between devices: 54.9 us -> 4.23 us  [on_device(): lax.psum_scatter(project(normed, query_weight, key_weight, value_weight,...]
    all_gather x6 -> x4, waiting for transfers between devices: 130 us -> 95.6 us  [the longest x1 60.9 us: on_device(): last = lax.all_gather(shares[-1], 'row', axis=0, tiled=True)]
    reduce_scatter x2 -> x1, waiting for transfers between devices: 30.1 us -> 0.01 us  [on_device(): lax.psum_scatter(hidden_part.reshape(groups * rows, units), 'row', scatte...]
  transfers between devices with their start and end apart: 23 -> 34, of which waited for: 13 -> 20; matrix products, arithmetic and copies ran while one was open for 6% -> 9% of each run, Pallas kernels for 37% -> 44%
where the time goes in v2:
time: 1210 us; the launch traced here: 1200 us
  Pallas kernels  553 us (46%)
  waiting for transfers between devices  391 us (32%)
  local copies, waits for them, and re-layouts  90.2 us (7%)
  blocking collectives  56.2 us (5%)
  other arithmetic  48.3 us (4%)
  starting transfers between devices  37.1 us (3%)
  between operations  17 us (1%)
    pallas_call x3, Pallas kernels, expert_gradients(): pl.pallas_call(functools.partial(gradient_kernel, part, start, len(pieces...  213 us
    ppermute x6, waiting for transfers between devices, gather_planes(): lax.ppermute(value, 'dp', [(i, (i - apart) % count) for i in range(count)])  107 us
    pallas_call x1, Pallas kernels, dispatch_turned(): pl.pallas_call(dispatch_turned_kernel, grid=(groups, rows // WIDE), in_sp...  87.6 us
    all_gather x1, waiting for transfers between devices, on_device(): all_hidden = lax.all_gather(hidden_delta, every, axis=0, tiled=True)  86.1 us
    pallas_call x2, Pallas kernels, expert_back(): pl.pallas_call(functools.partial(expert_back_kernel, part), grid_spec=plt...  84.9 us
    all_gather x1, waiting for transfers between devices, on_device(): last = lax.all_gather(shares[-1], 'row', axis=0, tiled=True)  60.9 us
    pallas_call x2, Pallas kernels, gate_up(): pl.pallas_call(gate_up_kernel, grid_spec=pltpu.PrefetchScalarGridSpec(num...  39.8 us
    psum x6, blocking collectives, total_rows(): return lax.psum(value, 'row')  37.2 us
  transfers between devices with their start and end apart: 34, of which 20 were waited for; matrix products, arithmetic and copies ran while one was open for 9% of the time, Pallas kernels for 44%

profile of v2, /device:TPU:0, one launch (start us, length us, event | category | flops | bytes accessed | tf_op | source)
XLA Modules:
  0.0 1197.3 jit_solution(11876209359717771870)
XLA Ops:
  14.4 9.9 collective-permute-done
  46.0 13.9 %all-gather.1 = s32[4,1,8192]{2,1,0:T(1,128)S(1)} all-gather(s32[1,1,8192]{2,1,0:T(1,128)} %bitcast.153), channel_id=1, replica_groups=mesh['dp'=4,'row'=4,'col'=2] {'dp'}, dimensions={0}, use_global_device_ids=true | all-gather | bytes 163840 | tf_op jit(solution)/shard_map/all_gather | solution.py:967
  64.5 13.2 %dispatch.2.x_ref = bf16[1,8192,512]{2,1,0:T(8,128)(2,1)} custom-call(s32[1,16,4,128]{3,2,1,0:T(4,128)S(1)} %bitcast.104, bf16[1,1024,512]{2,1,0:T(8,128)(2,1)S(1)} %copy.124.source_ref), custom_call_target="tpu_custom_call" | custom-call | flops 134217728 | bytes 131072 | tf_op jit(solution)/shard_map/dispatch/pallas_call | solution.py:336
  77.7 20.1 %hidden_back.1 = bf16[1,8192,512]{2,1,0:T(8,128)(2,1)} custom-call(s32[1,33]{1,0:T(1,128)} %bitcast.171, bf16[1,8192,512]{2,1,0:T(8,128)(2,1)} %dispatch.2.x_ref, bf16[32,512,512]{2,1,0:T(8,128)(2,1)} %down_ref.3), custom_call_target="tpu_custom_call" | custom-call | flops 100663296 | bytes 131072 | tf_op jit(solution)/shard_map/hidden_back/pallas_call | solution.py:486
  124.5 21.5 %all-gather.22.cloned.1.call-done = bf16[4096,256]{1,0:T(8,128)(2,1)} async-done(((bf16[1024,256]{1,0:T(8,128)(2,1)}), bf16[4096,256]{1,0:T(8,128)(2,1)}) %all-gather.22.cloned.1.call-update) | async-done | bytes 2097168 | tf_op jit(solution)/shard_map/all_gather | solution.py:1010
  151.7 23.8 %collective-permute-done.3 = bf16[1024,512]{0,1:T(8,128)(2,1)S(1)} collective-permute-done((bf16[1024,512]{0,1:T(8,128)(2,1)S(1)}, bf16[1024,512]{0,1:T(8,128)(2,1)S(1)}, u32[]{:S(2)}, u32[]{:S(2)}) %collective-permute-start.3) | collective-permute-done | bytes 1048608 | tf_op jit(solution)/shard_map/ppermute | solution.py:896
  187.1 13.2 %dispatch.3.x_ref = bf16[1,8192,512]{2,1,0:T(8,128)(2,1)} custom-call(s32[1,16,4,128]{3,2,1,0:T(4,128)S(1)} %bitcast.105, bf16[1,1024,512]{2,1,0:T(8,128)(2,1)S(1)} %copy.128.source_ref), custom_call_target="tpu_custom_call" | custom-call | flops 134217728 | bytes 131072 | tf_op jit(solution)/shard_map/dispatch/pallas_call | solution.py:336
  200.2 19.4 %gate_up.2 = bf16[1,8192,512]{2,1,0:T(8,128)(2,1)} custom-call(s32[1,33]{1,0:T(1,128)} %bitcast.172, bf16[1,8192,512]{2,1,0:T(8,128)(2,1)} %dispatch.3.x_ref, bf16[32,512,512]{2,1,0:T(8,128)(2,1)} %gate_ref.7, bf16[32,512,512]{2,1,0:T(8,128)(2,1)} %up_ref.7), custom_call_target="tpu_custom_call" | custom-call | flops 100663296 | bytes 131072 | tf_op jit(solution)/shard_map/gate_up/pallas_call | solution.py:458
  219.7 20.4 %gate_up.3 = bf16[1,8192,512]{2,1,0:T(8,128)(2,1)} custom-call(s32[1,33]{1,0:T(1,128)} %bitcast.173, bf16[1,8192,512]{2,1,0:T(8,128)(2,1)} %dispatch.3.x_ref, bf16[32,512,512]{2,1,0:T(8,128)(2,1)} %gate_ref.7, bf16[32,512,512]{2,1,0:T(8,128)(2,1)} %up_ref.7), custom_call_target="tpu_custom_call" | custom-call | flops 100663296 | bytes 131072 | tf_op jit(solution)/shard_map/gate_up/pallas_call | solution.py:458
  249.6 10.9 pick.1.scale_ref
  272.6 22.5 %collective-permute-done.6 = f32[1,8192]{1,0:T(1,128)S(1)} collective-permute-done((f32[1,8192]{1,0:T(1,128)S(1)}, f32[1,8192]{1,0:T(1,128)S(1)}, u32[]{:S(2)}, u32[]{:S(2)}) %collective-permute-start.6) | collective-permute-done | bytes 32800 | tf_op jit(solution)/shard_map/ppermute | solution.py:868
  302.4 82.6 %collective-permute-done.10 = bf16[1024,512]{0,1:T(8,128)(2,1)} collective-permute-done((bf16[1024,512]{0,1:T(8,128)(2,1)S(1)}, bf16[1024,512]{0,1:T(8,128)(2,1)}, u32[]{:S(2)}, u32[]{:S(2)}) %collective-permute-start.10) | collective-permute-done | bytes 1048608 | tf_op jit(solution)/shard_map/ppermute | solution.py:868
  411.9 86.1 %all-gather.12.cloned.1.call-done = bf16[32768,512]{1,0:T(8,128)(2,1)} async-done(((bf16[2048,512]{1,0:T(8,128)(2,1)}), bf16[32768,512]{1,0:T(8,128)(2,1)}) %all-gather.12.cloned.1.call-update) | async-done | bytes 33554448 | tf_op jit(solution)/shard_map/all_gather | solution.py:1068
  498.2 60.9 %all-gather.14.cloned.1.call-done = bf16[8192,512]{1,0:T(8,128)(2,1)} async-done(((bf16[2048,512]{1,0:T(8,128)(2,1)}), bf16[8192,512]{1,0:T(8,128)(2,1)}) %all-gather.14.cloned.1.call-update) | async-done | bytes 8388624 | tf_op jit(solution)/shard_map/all_gather | solution.py:1078
  562.4 87.6 %dispatch_turned.1 = (bf16[4,64,512,128]{3,2,1,0:T(8,128)(2,1)}, bf16[4,64,512,128]{3,2,1,0:T(8,128)(2,1)}) custom-call(s32[4,16,1,512]{3,2,1,0:T(1,128)S(1)} %reshape.323.token_ref, f32[4,16,1,512]{3,2,1,0:T(1,128)S(1)} %reshape.324.scale_ref, bf16[4,512,1024]{2,1,0:T(8,128)(2,1)S(1)} %bitcast.97, bf16[4,512,1024]{2,1,0:T(8,128)(2,1)} %bitcast.139), custom_call_target="tpu_custom_call" | custom-call | flops 1073741824 | bytes 1048576 | tf_op jit(solution)/shard_map/dispatch_turned/pallas_call | solution.py:367
  650.0 42.6 %expert_back.2 = f32[1,1024,640]{2,1,0:T(8,128)} custom-call(s32[1,33]{1,0:T(1,128)} %bitcast.174, s32[2]{0:T(128)} %pad_add_fusion._, bf16[1,8192,512]{2,1,0:T(8,128)(2,1)} %bitcast.130, bf16[1,8192,512]{2,1,0:T(8,128)(2,1)} %bitcast.131, bf16[4,8192,512]{2,1,0:T(8,128)(2,1)} %bitcast.125, bf16[32,512,512]{2,1,0:T(8,128)(2,1)} %gate_ref.7, ...), custom_call_target="tpu_custom_call" | custom-call | flops 234881024 | bytes 262144 | tf_op jit(solution)/shard_map/expert_back/pallas_call | solution.py:562
  692.6 34.7 %all-gather.16.cloned.1.call-done = bf16[32768,512]{1,0:T(8,128)(2,1)} async-done(((bf16[2048,512]{1,0:T(8,128)(2,1)}), bf16[32768,512]{1,0:T(8,128)(2,1)}) %all-gather.16.cloned.1.call-update) | async-done | bytes 33554448 | tf_op jit(solution)/shard_map/all_gather | solution.py:1084
  727.3 8.7 all-gather.20.cloned.1.call-start
  736.6 42.3 %expert_back.3 = f32[1,1024,640]{2,1,0:T(8,128)} custom-call(s32[1,33]{1,0:T(1,128)} %bitcast.175, s32[2]{0:T(128)} %pad_add_fusion.2._, bf16[4,8192,512]{2,1,0:T(8,128)(2,1)} %bitcast.119, bf16[4,8192,512]{2,1,0:T(8,128)(2,1)} %bitcast.120, bf16[4,8192,512]{2,1,0:T(8,128)(2,1)} %bitcast.126, bf16[32,512,512]{2,1,0:T(8,128)(2,1)} %gate_ref.7, ...), custom_call_target="tpu_custom_call" | custom-call | flops 234881024 | bytes 262144 | tf_op jit(solution)/shard_map/expert_back/pallas_call | solution.py:562
  794.1 34.5 %expert_down.1 = f32[1,1024,512]{2,1,0:T(8,128)} custom-call(s32[1,33]{1,0:T(1,128)} %bitcast.176, s32[2]{0:T(128)} %pad_add_fusion.1.base_ref, bf16[32,512,512]{2,1,0:T(8,128)(2,1)} %down_ref.3, s32[1,16,1,512]{3,2,1,0:T(1,128)} %bitcast.109, f32[1,16,1,512]{3,2,1,0:T(1,128)} %copy-done.26, bf16[4,8192,512]{2,1,0:T(8,128)(2,1)} %bitcast.121, ...), custom_call_target="tpu_custom_call" | custom-call | flops 234881024 | bytes 262144 | tf_op jit(solution)/shard_map/expert_down/pallas_call | solution.py:623
  828.7 55.0 %expert_gradients.3 = (f32[32,512,512]{2,1,0:T(8,128)}, f32[32,512,512]{2,1,0:T(8,128)}, f32[32,512,512]{2,1,0:T(8,128)}) custom-call(s32[4,33]{1,0:T(4,128)} %copy.135.offset_ref, bf16[4,1,64,128,512]{4,3,2,1,0:T(8,128)(2,1)} %bitcast.123, bf16[4,64,128,512]{3,2,1,0:T(8,128)(2,1)} %bitcast.127, bf16[4,64,512,128]{3,2,1,0:T(8,128)(2,1)} %get-tuple-element.96.rest_2_, ...), custom_call_target="tpu_custom_call" | custom-call | flops 603979776 | bytes 1835008 | tf_op jit(solution)/shard_map/expert_gradients/pallas_call | solution.py:789
  912.3 13.5 %collective-permute-done.14 = bf16[1024,256]{1,0:T(8,128)(2,1)} collective-permute-done((bf16[1024,256]{1,0:T(8,128)(2,1)}, bf16[1024,256]{1,0:T(8,128)(2,1)}, u32[]{:S(2)}, u32[]{:S(2)}) %collective-permute-start.14) | collective-permute-done | bytes 524320 | tf_op jit(solution)/shard_map/ppermute | solution.py:858
  954.8 55.7 %expert_gradients.4 = (f32[32,512,512]{2,1,0:T(8,128)}, f32[32,512,512]{2,1,0:T(8,128)}, f32[32,512,512]{2,1,0:T(8,128)}) custom-call(s32[4,33]{1,0:T(4,128)} %copy.135.offset_ref, bf16[4,1,64,128,512]{4,3,2,1,0:T(8,128)(2,1)} %bitcast.124, bf16[4,64,128,512]{3,2,1,0:T(8,128)(2,1)} %bitcast.128, ...), custom_call_target="tpu_custom_call", output_to_operand_aliasing={{0}: (5, {}), {1}: (6, {}), {2}: (7, {})} | custom-call | flops 603979776 | bytes 1835008 | tf_op jit(solution)/shard_map/expert_gradients/pallas_call | solution.py:789
  1077.9 102.0 %expert_gradients.5 = (f32[32,512,512]{2,1,0:T(8,128)}, f32[32,512,512]{2,1,0:T(8,128)}, f32[32,512,512]{2,1,0:T(8,128)}) custom-call(s32[4,33]{1,0:T(4,128)} %copy.135.offset_ref, bf16[4,1,64,128,512]{4,3,2,1,0:T(8,128)(2,1)} %bitcast.137, bf16[4,64,128,512]{3,2,1,0:T(8,128)(2,1)} %bitcast.129, ...), custom_call_target="tpu_custom_call", output_to_operand_aliasing={{0}: (5, {}), {1}: (6, {}), {2}: (7, {})} | custom-call | flops 603979776 | bytes 1835008 | tf_op jit(solution)/shard_map/expert_gradients/pallas_call | solution.py:789
  (354 shorter events, 285.4 us)
Async XLA Ops:
  9.4 15.0 %collective-permute-start = (bf16[512,512]{0,1:T(8,128)(2,1)S(1)}, bf16[512,512]{0,1:T(8,128)(2,1)S(1)}, u32[]{:S(2)}, u32[]{:S(2)}) collective-permute-start(bf16[512,512]{0,1:T(8,128)(2,1)S(1)} %copy.117), channel_id=1, source_target_pairs={{0,1},{1,0},{2,3},{3,2},{4,5},{5,4},{6,7},{7,6},{8,9},{9,8},{10,11... | collective-permute-start | bytes 1572872 | tf_op jit(solution)/shard_map/ppermute | solution.py:886
  14.3 87.7 %reduce-scatter.5.cloned.1.call-start = ((), (), s32[]{:S(2)}) async-start(), calls=%async_computation.4 | async-start | bytes 7864320 | tf_op jit(solution)/shard_map/reduce_scatter | solution.py:977
  42.2 81.3 %all-gather.10.cloned.1.call-start = ((), (), s32[]{:S(2)}) async-start(), calls=%async_computation.5 | async-start | bytes 4718592 | tf_op jit(solution)/shard_map/all_gather | solution.py:966
  43.0 103.0 %all-gather.22.cloned.1.call-start = ((), (), s32[]{:S(2)}) async-start(), calls=%async_computation.14 | async-start | bytes 2621440 | tf_op jit(solution)/shard_map/all_gather | solution.py:1010
  43.5 19.3 %collective-permute-start.1 = (bf16[512,512]{0,1:T(8,128)(2,1)S(1)}, bf16[512,512]{0,1:T(8,128)(2,1)S(1)}, u32[]{:S(2)}, u32[]{:S(2)}) collective-permute-start(bf16[512,512]{0,1:T(8,128)(2,1)S(1)} %copy.122), channel_id=1, source_target_pairs={{0,1},{1,0},{2,3},{3,2},{4,5},{5,4},{6,7},{7,6},{8,9},{9,8},{10,11... | collective-permute-start | bytes 1572872 | tf_op jit(solution)/shard_map/ppermute | solution.py:886
  123.6 116.5 %reduce-scatter.9.cloned.1.call-start = ((), (), s32[]{:S(2)}) async-start(), calls=%async_computation.7 | async-start | bytes 10485760 | tf_op jit(solution)/shard_map/reduce_scatter | solution.py:1011
  124.2 287.8 %reduce-scatter.7.cloned.1.call-start = ((), (), s32[]{:S(2)}) async-start(), calls=%async_computation.6 | async-start | bytes 10485760 | tf_op jit(solution)/shard_map/reduce_scatter | solution.py:1041
  150.2 25.4 %collective-permute-start.3 = (bf16[1024,512]{0,1:T(8,128)(2,1)S(1)}, bf16[1024,512]{0,1:T(8,128)(2,1)S(1)}, u32[]{:S(2)}, u32[]{:S(2)}) collective-permute-start(bf16[1024,512]{0,1:T(8,128)(2,1)S(1)} %copy.126), channel_id=1, source_target_pairs={{0,1},{1,0},{2,3},{3,2},{4,5},{5,4},{6,7},{7,6},{8,9},{9,8},{10,11... | collective-permute-start | bytes 3145736 | tf_op jit(solution)/shard_map/ppermute | solution.py:896
  219.6 278.4 %all-gather.12.cloned.1.call-start = ((), (), s32[]{:S(2)}) async-start(), calls=%async_computation.8 | async-start | bytes 35651584 | tf_op jit(solution)/shard_map/all_gather | solution.py:1068
  240.1 258.1 %reduce-scatter.11.cloned.1.call-start = ((), (), s32[]{:S(2)}) async-start(), calls=%async_computation.9 | async-start | bytes 10485760 | tf_op jit(solution)/shard_map/reduce_scatter | solution.py:1041
  240.8 318.2 %all-gather.14.cloned.1.call-start = ((), (), s32[]{:S(2)}) async-start(), calls=%async_computation.10 | async-start | bytes 10485760 | tf_op jit(solution)/shard_map/all_gather | solution.py:1078
  244.7 56.6 %collective-permute-start.9 = (bf16[1024,512]{0,1:T(8,128)(2,1)S(1)}, bf16[1024,512]{0,1:T(8,128)(2,1)S(1)}, u32[]{:S(2)}, u32[]{:S(2)}) collective-permute-start(bf16[1024,512]{0,1:T(8,128)(2,1)S(1)} %copy-done.33), channel_id=1, source_target_pairs={{0,24},{8,0},{16,8},{24,16},{1,25},{9,1},{17,9},{25,17},{2,26},{10... | collective-permute-start | bytes 3145736 | tf_op jit(solution)/shard_map/ppermute | solution.py:868
  260.6 34.5 %collective-permute-start.6 = (f32[1,8192]{1,0:T(1,128)S(1)}, f32[1,8192]{1,0:T(1,128)S(1)}, u32[]{:S(2)}, u32[]{:S(2)}) collective-permute-start(f32[1,8192]{1,0:T(1,128)S(1)} %bitcast.110), channel_id=1, source_target_pairs={{0,24},{8,0},{16,8},{24,16},{1,25},{9,1},{17,9},{25,17},{2,26},{10... | collective-permute-start | bytes 98312 | tf_op jit(solution)/shard_map/ppermute | solution.py:868
  263.4 34.5 %collective-permute-start.7 = (f32[1,8192]{1,0:T(1,128)S(1)}, f32[1,8192]{1,0:T(1,128)S(1)}, u32[]{:S(2)}, u32[]{:S(2)}) collective-permute-start(f32[1,8192]{1,0:T(1,128)S(1)} %bitcast.111), channel_id=1, source_target_pairs={{0,16},{8,24},{16,0},{24,8},{1,17},{9,25},{17,1},{25,9},{2,18},{10... | collective-permute-start | bytes 98312 | tf_op jit(solution)/shard_map/ppermute | solution.py:868
  263.4 34.5 %collective-permute-start.8 = (f32[1,8192]{1,0:T(1,128)S(1)}, f32[1,8192]{1,0:T(1,128)}, u32[]{:S(2)}, u32[]{:S(2)}) collective-permute-start(f32[1,8192]{1,0:T(1,128)S(1)} %bitcast.112), channel_id=1, source_target_pairs={{0,8},{8,16},{16,24},{24,0},{1,9},{9,17},{17,25},{25,1},{2,10},{10... | collective-permute-start | bytes 98312 | tf_op jit(solution)/shard_map/ppermute | solution.py:868
  264.5 120.5 %collective-permute-start.10 = (bf16[1024,512]{0,1:T(8,128)(2,1)S(1)}, bf16[1024,512]{0,1:T(8,128)(2,1)}, u32[]{:S(2)}, u32[]{:S(2)}) collective-permute-start(bf16[1024,512]{0,1:T(8,128)(2,1)S(1)} %copy-done.33), channel_id=1, source_target_pairs={{0,16},{8,24},{16,0},{24,8},{1,17},{9,25},{17,1},{25,9},{2,18},{10... | collective-permute-start | bytes 3145736 | tf_op jit(solution)/shard_map/ppermute | solution.py:868
  295.1 92.4 %collective-permute-start.11 = (bf16[1024,512]{0,1:T(8,128)(2,1)S(1)}, bf16[1024,512]{0,1:T(8,128)(2,1)}, u32[]{:S(2)}, u32[]{:S(2)}) collective-permute-start(bf16[1024,512]{0,1:T(8,128)(2,1)S(1)} %copy-done.33), channel_id=1, source_target_pairs={{0,8},{8,16},{16,24},{24,0},{1,9},{9,17},{17,25},{25,1},{2,10},{10... | collective-permute-start | bytes 3145736 | tf_op jit(solution)/shard_map/ppermute | solution.py:868
  498.1 229.2 %all-gather.16.cloned.1.call-start = ((), (), s32[]{:S(2)}) async-start(), calls=%async_computation.11 | async-start | bytes 35651584 | tf_op jit(solution)/shard_map/all_gather | solution.py:1084
  559.1 338.5 %all-gather.18.cloned.1.call-start = ((), (), s32[]{:S(2)}) async-start(), calls=%async_computation.12 | async-start | bytes 35651584 | tf_op jit(solution)/shard_map/all_gather | solution.py:1084
  727.3 285.6 %all-gather.20.cloned.1.call-start = ((), (), s32[]{:S(2)}) async-start(), calls=%async_computation.13 | async-start | bytes 7864320 | tf_op jit(solution)/shard_map/all_gather | solution.py:1184
  790.0 93.7 %collective-permute-start.12 = (bf16[1024,512]{0,1:T(8,128)(2,1)}, bf16[1024,512]{0,1:T(8,128)(2,1)}, u32[]{:S(2)}, u32[]{:S(2)}) collective-permute-start(bf16[1024,512]{0,1:T(8,128)(2,1)} %fusion.3), channel_id=1, source_target_pairs={{0,1},{1,0},{2,3},{3,2},{4,5},{5,4},{6,7},{7,6},{8,9},{9,8},{10,11... | collective-permute-start | bytes 3145736 | tf_op jit(solution)/shard_map/ppermute | solution.py:896
  948.7 232.4 %all-reduce.3.cloned.1.call-start = ((), (), s32[]{:S(2)}) async-start(), calls=%async_computation.15 | async-start | bytes 8454144 | tf_op jit(solution)/shard_map/psum | solution.py:1212
  1025.0 15.2 %collective-permute-start.18 = (bf16[512,512]{0,1:T(8,128)(2,1)}, bf16[512,512]{0,1:T(8,128)(2,1)}, u32[]{:S(2)}, u32[]{:S(2)}) collective-permute-start(bf16[512,512]{0,1:T(8,128)(2,1)} %bitcast.151), channel_id=1, source_target_pairs={{0,1},{1,0},{2,3},{3,2},{4,5},{5,4},{6,7},{7,6},{8,9},{9,8},{10,11... | collective-permute-start | bytes 1572872 | tf_op jit(solution)/shard_map/ppermute | solution.py:906
  1034.2 15.1 %collective-permute-start.17 = (bf16[512,512]{0,1:T(8,128)(2,1)}, bf16[512,512]{0,1:T(8,128)(2,1)}, u32[]{:S(2)}, u32[]{:S(2)}) collective-permute-start(bf16[512,512]{0,1:T(8,128)(2,1)} %bitcast.152), channel_id=1, source_target_pairs={{0,1},{1,0},{2,3},{3,2},{4,5},{5,4},{6,7},{7,6},{8,9},{9,8},{10,11... | collective-permute-start | bytes 1572872 | tf_op jit(solution)/shard_map/ppermute | solution.py:906
  (87 other events, 1397.6 us)
Sparse Core Ops, SparseCore 0:
  14.4 11.4 sort.11.cloned.1.call-done
  45.4 75.1 all-gather.9
  240.2 257.8 all-gather.11
  559.2 168.0 all-gather.15
  728.7 168.0 all-gather.17
  (1 shorter events, 0.0 us)
Sparse Core Ops, SparseCore 1:
  42.3 59.7 reduce-scatter.4
  123.7 22.3 all-gather.21
  148.6 71.7 reduce-scatter.8
  223.6 97.3 reduce-scatter.6
  324.3 100.5 reduce-scatter.10
  498.2 60.8 all-gather.13
  948.8 45.9 all-gather.19
  1020.0 156.9 all-reduce.2

commit v3 on v2

--- a/solution.py
+++ b/solution.py
@@ -508,9 +508,9 @@
     return gate + product, (0.5 + 0.5 * turned) * ((1.0 + gate) - product)
 
 
-def combine(token_ref, scale_ref, rows_ref, o_ref):
+def combine(token_ref, scale_ref, rows_ref, o_ref, before_ref=None):
     tokens = o_ref.shape[1]
-    o_ref[0] = jnp.zeros(o_ref.shape[1:], F32)
+    o_ref[0] = jnp.zeros(o_ref.shape[1:], F32) if before_ref is None else before_ref[0]
 
     def step(i, carry):
         chosen = iota((tokens, WIDE), 0) == token_ref[0, i]
@@ -522,8 +522,9 @@
 
 
 def expert_back_kernel(
-    part, offset_ref, _, g_ref, u_ref, hd_ref, gate_ref, up_ref, token_ref, scale_ref, o_ref, made_ref
+    part, offset_ref, _, g_ref, u_ref, hd_ref, gate_ref, up_ref, token_ref, scale_ref, *rest
 ):
+    *before_ref, o_ref, made_ref = rest
     experts = PACK * pl.num_programs(1)
     depth, half = gate_ref.shape[1], gate_ref.shape[2]
 
@@ -549,16 +550,17 @@
 
     @pl.when(pl.program_id(1) == pl.num_programs(1) - 1)
     def _():
-        combine(token_ref, scale_ref, made_ref, o_ref)
-
-
-def expert_back(offsets, base, pair, hd, gate, up, tokens_of, scale, part, half, tokens):
+        combine(token_ref, scale_ref, made_ref, o_ref, *before_ref)
+
+
+def expert_back(offsets, base, pair, hd, gate, up, tokens_of, scale, part, half, tokens, before):
     groups, rows = tokens_of.shape
     units = hd.shape[2]
     experts, depth = gate.shape[:2]
     weight = pl.BlockSpec((PACK, depth, half), lambda g, e, o, b: (e, 0, part))
     line = once((1, rows // WIDE, 1, WIDE), lambda g, e, o, b: (g, 0, 0, 0))
     shape = (groups, rows // WIDE, 1, WIDE)
+    total = once((1, tokens, depth + TILE), lambda g, e, o, b: (g, 0, 0))
     return pl.pallas_call(
         functools.partial(expert_back_kernel, part),
         grid_spec=pltpu.PrefetchScalarGridSpec(
@@ -574,8 +576,9 @@
                 weight,
                 line,
                 line,
+                *[total] * len(before),
             ],
-            out_specs=once((1, tokens, depth + TILE), lambda g, e, o, b: (g, 0, 0)),
+            out_specs=total,
             scratch_shapes=[pltpu.VMEM((rows, depth + TILE), BF)],
         ),
         out_shape=jax.ShapeDtypeStruct((groups, tokens, depth + TILE), F32),
@@ -584,7 +587,7 @@
             groups * rows * depth * (6 * half + 2 * tokens), 2 * groups * rows * (2 * half + units)
         ),
         name="expert_back",
-    )(offsets, base, pair[0][0], pair[1][0], hd, gate, up, tokens_of.reshape(shape), scale.reshape(shape))
+    )(offsets, base, pair[0][0], pair[1][0], hd, gate, up, tokens_of.reshape(shape), scale.reshape(shape), *before)
 
 
 def down_kernel(offset_ref, base_ref, down_ref, token_ref, scale_ref, *rest):
@@ -648,7 +651,7 @@
     hd_ref, xs_ref, xc_ref = rest[:3]
     rest = rest[3 + 3 * aliased :]
     gate_out, up_out, down_out = rest[:3]
-    gu_ring, hd_ring, xs_ring, xc_ring, wide, narrow, issued, waited, sems = rest[3:]
+    gu_ring, hd_ring, xs_ring, xc_ring, narrow, issued, waited, sems = rest[3:]
     segments, tiles = xs_ref.shape[:2]
     shares, run_tiles = piece_refs[0].shape[1:3]
     share_tiles = pieces * run_tiles
@@ -728,8 +731,6 @@
                 for ring in (gu_ring, hd_ring, xs_ring, xc_ring):
                     ring[segment, slot] = jnp.zeros(ring.shape[2:], BF)
 
-    wide[...] = jnp.zeros_like(wide)
-    narrow[...] = jnp.zeros_like(narrow)
     spans, rounds = [], 0
     for segment in range(segments):
         low, high = offset_ref[segment, expert], offset_ref[segment, expert + 1]
@@ -738,14 +739,14 @@
         spans.append((low, high, first, last))
         rounds = jnp.maximum(rounds, (last - first + BAND - 1) // BAND)
 
-    def turn(i, carry):
+    def turn(i, carry, fresh=False):
         for segment, (low, high, first, last) in enumerate(spans):
             tile = jnp.minimum(first + BAND * i, last)
             start_until(segment, jnp.minimum(bounds[segment][1], tile + RING - 1))
             wait_until(segment, jnp.minimum(last, tile + BAND))
         for segment, (low, high, first, last) in enumerate(spans):
             if segment % 2 == 0:
-                pair, hidden, xs, xc = [], [], [], []
+                gates, ups, hidden, xs, xc = [], [], [], [], []
             for j in range(BAND):
                 tile = first + BAND * i + j
                 slot = lax.rem(jnp.maximum(jnp.minimum(tile, last - 1), bounds[segment][0]), RING)
@@ -754,25 +755,34 @@
                 silu = jnp.where(keep, silu, 0.0).astype(BF)
                 slope = jnp.where(keep, slope, 0.0).astype(BF)
                 up, delta = gu_ring[segment, slot, :, half:], hd_ring[segment, slot]
-                pair.append(jnp.concatenate([delta * up * slope, delta * silu], axis=1))
+                gates.append(delta * up * slope)
+                ups.append(delta * silu)
                 hidden.append(silu * up)
                 xs.append(xs_ring[segment, slot])
                 xc.append(xc_ring[segment, slot])
             if segment % 2 == 0 and segment + 1 < segments:
                 continue
-            wide[...] += dot(jnp.concatenate(xs, axis=1), jnp.concatenate(pair, axis=0))
-            narrow[...] += dot(jnp.concatenate(xc, axis=1), jnp.concatenate(hidden, axis=0))
+            left, right = jnp.concatenate(xs, axis=1), jnp.concatenate(xc, axis=1)
+            made = [
+                (gate_out, (0,), dot(left, jnp.concatenate(gates, axis=0))),
+                (up_out, (0,), dot(left, jnp.concatenate(ups, axis=0))),
+                (narrow, (), dot(right, jnp.concatenate(hidden, axis=0))),
+            ]
+            for out, place, value in made:
+                if fresh and segment < 2:
+                    out[(*place, ...)] = value
+                else:
+                    out[(*place, ...)] += value
         return carry
 
-    lax.fori_loop(0, rounds, turn, 0)
+    turn(0, 0, fresh=True)
+    lax.fori_loop(1, rounds, turn, 0)
 
     @pl.when(expert == stop - 1)
     def _():
         for segment in range(segments):
             wait_until(segment, issued[segment])
 
-    gate_out[0] = wide[:, :half]
-    up_out[0] = wide[:, half:]
     down_out[0] = narrow[...].T
 
 
@@ -802,7 +812,6 @@
                 pltpu.VMEM((segments, RING, TILE, half), BF),
                 pltpu.VMEM((segments, RING, depth, TILE), BF),
                 pltpu.VMEM((segments, RING, depth, TILE), BF),
-                pltpu.VMEM((depth, pair), F32),
                 pltpu.VMEM((depth, half), F32),
                 pltpu.SMEM((segments,), jnp.int32),
                 pltpu.SMEM((segments,), jnp.int32),
@@ -836,6 +845,11 @@
 
 def total_rows(value):
     return lax.psum(value, "row")
+
+
+def neighbour_sum(value, axis, apart):
+    count = lax.axis_size(axis)
+    return value + lax.ppermute(value, axis, [(i, i ^ apart) for i in range(count)])
 
 
 def exchange(value, axis):
@@ -1045,7 +1059,7 @@
     def turned(value):
         return jnp.swapaxes(value.reshape(-1, sub, width_part), 1, 2)
 
-    def back_of(part, pair, base, hidden_rows, hidden_base):
+    def back_of(part, pair, base, hidden_rows, hidden_base, before=()):
         return expert_back(
             offsets,
             jnp.stack([base, hidden_base]),
@@ -1058,6 +1072,7 @@
             part,
             half,
             sub,
+            before,
         )
 
     zero = jnp.zeros((), jnp.int32)
@@ -1089,7 +1104,7 @@
                 whole = taken.reshape(segment_count, rows, 2 * half)
                 pairs.append([(whole, 0), (whole, 1)])
                 bases.append(base)
-                back = back + back_of(part, pairs[part], base, hidden_rows, base)
+                back = back_of(part, pairs[part], base, hidden_rows, base, (back,))
             all_pairs.append([taken.reshape(segment_count, 1, rows, 2 * half)])
         pairs.append([(last, 0), (last, 1)])
         bases.append(zero)
@@ -1148,11 +1163,10 @@
     )
     second_gain_part = jnp.sum(second_delta * middle * second_inverse[:, None], axis=0)
     attention_round = middle_delta.astype(BF)
-    expert_out = expert_down(offsets, bases, pairs, half, down_weight, tokens_of, scale, sub)
-    some = experts // 2 if parts > 1 else 0
-    gradients = gradients_of(0, 0, some, ()) if some else ()
-    attention_round, expert_out, all_pairs[-1][0], gradients = in_order(
-        attention_round, expert_out, all_pairs[-1][0], gradients
+    early = parts > 1
+    gradients = gradients_of(0, 0, experts, ()) if early else ()
+    attention_round, all_pairs[-1][0], gradients = in_order(
+        attention_round, all_pairs[-1][0], gradients
     )
     output_gradient = jnp.einsum(
         "srth,std->rhd",
@@ -1161,6 +1175,10 @@
         preferred_element_type=F32,
     ).reshape(head_part, width_part)
     early_gradient = jnp.concatenate([output_gradient, router_part], axis=0).astype(BF)
+    plane_count = lax.axis_size("dp")
+    pairwise = early and plane_count == 4
+    if pairwise:
+        early_gradient = neighbour_sum(early_gradient, "dp", 1)
 
 
     mixed_delta = scatter_rows(output_back(attention_round, output_weight, spans, slots))
@@ -1181,14 +1199,23 @@
     query_gain_part = jnp.sum(query_delta * query_raw * query_inverse[:, None], axis=0)
     key_gain_part = jnp.sum(key_delta * key_raw * key_inverse[:, None], axis=0)
     joint_delta = jnp.concatenate([query_raw_delta, key_raw_delta, value_delta], axis=1).astype(BF)
+    joint_delta, early_gradient = in_order(joint_delta, early_gradient)
+    if pairwise:
+        early_gradient = neighbour_sum(early_gradient, "dp", 2)
+    else:
+        early_gradient = lax.psum(early_gradient, "dp")
     joint_group = lax.all_gather(joint_delta, "row", axis=0, tiled=False)
+    run = experts * 3 // 8
+    gradients = gradients_of(parts - 1, 0, run, gradients)
+    joint_group, gradients, early_gradient = in_order(joint_group, gradients, early_gradient)
+    joint_gradients = project_gradient(normed.T, joint_group, spans, slots)
+    *joint_gradients, joint_group = in_order(*joint_gradients, joint_group)
+    head_gradients = [lax.psum(value, "dp") for value in joint_gradients]
     first_delta = share_columns(
         project_back(joint_group, query_weight, key_weight, value_weight, spans, slots)
     )
-    if some:
-        gradients = gradients_of(0, some, experts - some, gradients)
-        joint_group, gradients = in_order(joint_group, gradients)
-    joint_gradients = project_gradient(normed.T, joint_group, spans, slots)
+    expert_out = expert_down(offsets, bases, pairs, half, down_weight, tokens_of, scale, sub)
+    first_delta, expert_out = in_order(first_delta, expert_out)
 
     own_residual = residual_in.astype(F32)
     own_inverse = lax.dynamic_slice_in_dim(first_inverse, own_tokens, local_tokens, 0)
@@ -1205,12 +1232,6 @@
         lax.dynamic_slice_in_dim(middle, own_tokens, local_tokens, 0) + expert_out
     ).astype(BF)
 
-    *joint_gradients, early_gradient, gradients = in_order(
-        *joint_gradients, early_gradient, gradients
-    )
-    *head_gradients, early_gradient = [
-        lax.psum(value, "dp") for value in (*joint_gradients, early_gradient)
-    ]
     early_gradient = early_gradient.astype(F32)
     query_gradient, key_gradient, value_gradient = [value.astype(F32) for value in head_gradients]
     output_gradient = early_gradient[:head_part]
@@ -1223,12 +1244,10 @@
         gains[2 * width_part :].reshape(2, own_part), "row", axis=1, tiled=True
     )
     head_gains = jnp.sum(head_gains.reshape(2, spans, head_part), axis=1)
-    if not some:
-        gradients = ()
-    gradients, input_gradient, residual_out, gains, head_gains = in_order(
-        gradients, input_gradient, residual_out, gains, head_gains
-    )
-    gradients = gradients_of(parts - 1, 0, experts, gradients)
+    gradients, input_gradient, gains, head_gains = in_order(
+        gradients, input_gradient, gains, head_gains
+    )
+    gradients = gradients_of(parts - 1, run, experts - run, gradients)
     if not gathered:
         gradients = [lax.psum(value.astype(BF), "dp").astype(F32) for value in gradients]
     gate_gradient, up_gradient, down_gradient = gradients

time: 1210 us -> 1190 us (0.983)
  waiting for transfers between devices: 391 us -> 371 us
    unnamed x165 -> x159, local copies, waits for them, and re-layouts: 31.1 us -> 31.6 us
  transfers between devices with their start and end apart: 34 -> 36, of which waited for: 20 -> 20; matrix products, arithmetic and copies ran while one was open for 9% -> 10% of each run, Pallas kernels for 44% -> 45%
where the time goes in v3:
time: 1190 us; the launch traced here: 1180 us
  Pallas kernels  546 us (46%)
  waiting for transfers between devices  371 us (31%)
  local copies, waits for them, and re-layouts  85.4 us (7%)
  other arithmetic  56.2 us (5%)
  blocking collectives  56.1 us (5%)
  starting transfers between devices  36.7 us (3%)
  between operations  16.6 us (1%)
    pallas_call x3, Pallas kernels, expert_gradients(): pl.pallas_call(functools.partial(gradient_kernel, part, start, len(pieces...  205 us
    ppermute x6, waiting for transfers between devices, gather_planes(): lax.ppermute(value, 'dp', [(i, (i - apart) % count) for i in range(count)])  104 us
    pallas_call x1, Pallas kernels, dispatch_turned(): pl.pallas_call(dispatch_turned_kernel, grid=(groups, rows // WIDE), in_sp...  87.6 us
    pallas_call x2, Pallas kernels, expert_back(): pl.pallas_call(functools.partial(expert_back_kernel, part), grid_spec=plt...  86.4 us
    all_gather x1, waiting for transfers between devices, on_device(): all_hidden = lax.all_gather(hidden_delta, every, axis=0, tiled=True)  82.9 us
    all_gather x1, waiting for transfers between devices, on_device(): last = lax.all_gather(shares[-1], 'row', axis=0, tiled=True)  61.8 us
    pallas_call x2, Pallas kernels, gate_up(): pl.pallas_call(gate_up_kernel, grid_spec=pltpu.PrefetchScalarGridSpec(num...  40 us
    psum x6, blocking collectives, total_rows(): return lax.psum(value, 'row')  37.1 us
  transfers between devices with their start and end apart: 36, of which 20 were waited for; matrix products, arithmetic and copies ran while one was open for 10% of the time, Pallas kernels for 45%

profile of v3, /device:TPU:0, one launch (start us, length us, event | category | flops | bytes accessed | tf_op | source)
XLA Modules:
  0.0 1177.3 jit_solution(3329045057184015986)
XLA Ops:
  14.4 9.9 collective-permute-done
  46.0 13.9 %all-gather.2 = s32[4,1,8192]{2,1,0:T(1,128)S(1)} all-gather(s32[1,1,8192]{2,1,0:T(1,128)} %bitcast.147), channel_id=1, replica_groups=mesh['dp'=4,'row'=4,'col'=2] {'dp'}, dimensions={0}, use_global_device_ids=true | all-gather | bytes 163840 | tf_op jit(solution)/shard_map/all_gather | solution.py:981
  65.9 13.2 %dispatch.2.x_ref = bf16[1,8192,512]{2,1,0:T(8,128)(2,1)} custom-call(s32[1,16,4,128]{3,2,1,0:T(4,128)S(1)} %bitcast.96, bf16[1,1024,512]{2,1,0:T(8,128)(2,1)S(1)} %copy.123.source_ref), custom_call_target="tpu_custom_call" | custom-call | flops 134217728 | bytes 131072 | tf_op jit(solution)/shard_map/dispatch/pallas_call | solution.py:336
  79.0 20.3 %hidden_back.1 = bf16[1,8192,512]{2,1,0:T(8,128)(2,1)} custom-call(s32[1,33]{1,0:T(1,128)} %bitcast.165, bf16[1,8192,512]{2,1,0:T(8,128)(2,1)} %dispatch.2.x_ref, bf16[32,512,512]{2,1,0:T(8,128)(2,1)} %down_ref.3), custom_call_target="tpu_custom_call" | custom-call | flops 100663296 | bytes 131072 | tf_op jit(solution)/shard_map/hidden_back/pallas_call | solution.py:486
  124.7 21.3 %all-gather.21.cloned.1.call-done = bf16[4096,256]{1,0:T(8,128)(2,1)} async-done(((bf16[1024,256]{1,0:T(8,128)(2,1)}), bf16[4096,256]{1,0:T(8,128)(2,1)}) %all-gather.21.cloned.1.call-update) | async-done | bytes 2097168 | tf_op jit(solution)/shard_map/all_gather | solution.py:1024
  152.4 24.0 %collective-permute-done.3 = bf16[1024,512]{0,1:T(8,128)(2,1)S(1)} collective-permute-done((bf16[1024,512]{0,1:T(8,128)(2,1)}, bf16[1024,512]{0,1:T(8,128)(2,1)S(1)}, u32[]{:S(2)}, u32[]{:S(2)}) %collective-permute-start.3) | collective-permute-done | bytes 1048608 | tf_op jit(solution)/shard_map/ppermute | solution.py:910
  190.9 13.2 %dispatch.3.x_ref = bf16[1,8192,512]{2,1,0:T(8,128)(2,1)} custom-call(s32[1,16,4,128]{3,2,1,0:T(4,128)S(1)} %bitcast.97, bf16[1,1024,512]{2,1,0:T(8,128)(2,1)S(1)} %copy.127.source_ref), custom_call_target="tpu_custom_call" | custom-call | flops 134217728 | bytes 131072 | tf_op jit(solution)/shard_map/dispatch/pallas_call | solution.py:336
  204.1 19.4 %gate_up.2 = bf16[1,8192,512]{2,1,0:T(8,128)(2,1)} custom-call(s32[1,33]{1,0:T(1,128)} %bitcast.166, bf16[1,8192,512]{2,1,0:T(8,128)(2,1)} %dispatch.3.x_ref, bf16[32,512,512]{2,1,0:T(8,128)(2,1)} %gate_ref.7, bf16[32,512,512]{2,1,0:T(8,128)(2,1)} %up_ref.7), custom_call_target="tpu_custom_call" | custom-call | flops 100663296 | bytes 131072 | tf_op jit(solution)/shard_map/gate_up/pallas_call | solution.py:458
  223.5 20.6 %gate_up.3 = bf16[1,8192,512]{2,1,0:T(8,128)(2,1)} custom-call(s32[1,33]{1,0:T(1,128)} %bitcast.167, bf16[1,8192,512]{2,1,0:T(8,128)(2,1)} %dispatch.3.x_ref, bf16[32,512,512]{2,1,0:T(8,128)(2,1)} %gate_ref.7, bf16[32,512,512]{2,1,0:T(8,128)(2,1)} %up_ref.7), custom_call_target="tpu_custom_call" | custom-call | flops 100663296 | bytes 131072 | tf_op jit(solution)/shard_map/gate_up/pallas_call | solution.py:458
  256.8 10.9 pick.1.scale_ref
  280.0 20.7 %collective-permute-done.8 = f32[1,8192]{1,0:T(1,128)} collective-permute-done((f32[1,8192]{1,0:T(1,128)S(1)}, f32[1,8192]{1,0:T(1,128)}, u32[]{:S(2)}, u32[]{:S(2)}) %collective-permute-start.8) | collective-permute-done | bytes 32800 | tf_op jit(solution)/shard_map/ppermute | solution.py:882
  308.7 82.2 %collective-permute-done.10 = bf16[1024,512]{0,1:T(8,128)(2,1)S(1)} collective-permute-done((bf16[1024,512]{0,1:T(8,128)(2,1)}, bf16[1024,512]{0,1:T(8,128)(2,1)S(1)}, u32[]{:S(2)}, u32[]{:S(2)}) %collective-permute-start.10) | collective-permute-done | bytes 1048608 | tf_op jit(solution)/shard_map/ppermute | solution.py:882
  418.5 82.9 %all-gather.13.cloned.1.call-done = bf16[32768,512]{1,0:T(8,128)(2,1)} async-done(((bf16[2048,512]{1,0:T(8,128)(2,1)}), bf16[32768,512]{1,0:T(8,128)(2,1)}) %all-gather.13.cloned.1.call-update) | async-done | bytes 33554448 | tf_op jit(solution)/shard_map/all_gather | solution.py:1083
  501.4 61.8 %all-gather.15.cloned.1.call-done = bf16[8192,512]{1,0:T(8,128)(2,1)} async-done(((bf16[2048,512]{1,0:T(8,128)(2,1)}), bf16[8192,512]{1,0:T(8,128)(2,1)}) %all-gather.15.cloned.1.call-update) | async-done | bytes 8388624 | tf_op jit(solution)/shard_map/all_gather | solution.py:1093
  566.5 87.6 %dispatch_turned.1 = (bf16[4,64,512,128]{3,2,1,0:T(8,128)(2,1)}, bf16[4,64,512,128]{3,2,1,0:T(8,128)(2,1)}) custom-call(s32[4,16,1,512]{3,2,1,0:T(1,128)S(1)} %reshape.279.token_ref, f32[4,16,1,512]{3,2,1,0:T(1,128)S(1)} %reshape.280.scale_ref, bf16[4,512,1024]{2,1,0:T(8,128)(2,1)S(1)} %bitcast.89, bf16[4,512,1024]{2,1,0:T(8,128)(2,1)} %bitcast.132), custom_call_target="tpu_custom_call" | custom-call | flops 1073741824 | bytes 1048576 | tf_op jit(solution)/shard_map/dispatch_turned/pallas_call | solution.py:367
  654.1 42.6 %expert_back.2.rest_0_ = f32[1,1024,640]{2,1,0:T(8,128)} custom-call(s32[1,33]{1,0:T(1,128)} %bitcast.168, s32[2]{0:T(128)} %pad_add_fusion._, bf16[1,8192,512]{2,1,0:T(8,128)(2,1)} %bitcast.121, bf16[1,8192,512]{2,1,0:T(8,128)(2,1)} %bitcast.122, bf16[4,8192,512]{2,1,0:T(8,128)(2,1)} %bitcast.116, bf16[32,512,512]{2,1,0:T(8,128)(2,1)} %gate_ref.7, ...), custom_call_target="tpu_custom_call" | custom-call | flops 234881024 | bytes 262144 | tf_op jit(solution)/shard_map/expert_back/pallas_call | solution.py:564
  696.8 34.7 %all-gather.17.cloned.1.call-done = bf16[32768,512]{1,0:T(8,128)(2,1)} async-done(((bf16[2048,512]{1,0:T(8,128)(2,1)}), bf16[32768,512]{1,0:T(8,128)(2,1)}) %all-gather.17.cloned.1.call-update) | async-done | bytes 33554448 | tf_op jit(solution)/shard_map/all_gather | solution.py:1099
  732.3 43.8 %expert_back.3 = f32[1,1024,640]{2,1,0:T(8,128)} custom-call(s32[1,33]{1,0:T(1,128)} %bitcast.169, s32[2]{0:T(128)} %pad_add_fusion.2._, bf16[4,8192,512]{2,1,0:T(8,128)(2,1)} %bitcast.111, bf16[4,8192,512]{2,1,0:T(8,128)(2,1)} %bitcast.112, bf16[4,8192,512]{2,1,0:T(8,128)(2,1)} %bitcast.117, bf16[32,512,512]{2,1,0:T(8,128)(2,1)} %gate_ref.7, ...), custom_call_target="tpu_custom_call" | custom-call | flops 234881024 | bytes 262144 | tf_op jit(solution)/shard_map/expert_back/pallas_call | solution.py:564
  787.1 99.0 %expert_gradients.3 = (f32[32,512,512]{2,1,0:T(8,128)}, f32[32,512,512]{2,1,0:T(8,128)}, f32[32,512,512]{2,1,0:T(8,128)}) custom-call(s32[4,33]{1,0:T(4,128)} %copy.133.offset_ref, bf16[4,1,64,128,512]{4,3,2,1,0:T(8,128)(2,1)} %bitcast.113, bf16[4,64,128,512]{3,2,1,0:T(8,128)(2,1)} %bitcast.118, bf16[4,64,512,128]{3,2,1,0:T(8,128)(2,1)} %get-tuple-element.96.rest_2_, ...), custom_call_target="tpu_custom_call" | custom-call | flops 603979776 | bytes 1835008 | tf_op jit(solution)/shard_map/expert_gradients/pallas_call | solution.py:799
  922.9 10.0 collective-permute-done.14
  934.3 7.5 attend_back.1
  961.4 41.5 %expert_gradients.4 = (f32[32,512,512]{2,1,0:T(8,128)}, f32[32,512,512]{2,1,0:T(8,128)}, f32[32,512,512]{2,1,0:T(8,128)}) custom-call(s32[4,33]{1,0:T(4,128)} %copy.133.offset_ref, bf16[4,1,64,128,512]{4,3,2,1,0:T(8,128)(2,1)} %bitcast.125, bf16[4,64,128,512]{3,2,1,0:T(8,128)(2,1)} %bitcast.119, ...), custom_call_target="tpu_custom_call", output_to_operand_aliasing={{0}: (5, {}), {1}: (6, {}), {2}: (7, {})} | custom-call | flops 603979776 | bytes 1835008 | tf_op jit(solution)/shard_map/expert_gradients/pallas_call | solution.py:799
  1030.4 34.3 %expert_down.1 = f32[1,1024,512]{2,1,0:T(8,128)} custom-call(s32[1,33]{1,0:T(1,128)} %bitcast.170, s32[2]{0:T(128)} %pad_add_fusion.1.base_ref, bf16[32,512,512]{2,1,0:T(8,128)(2,1)} %down_ref.3, s32[1,16,1,512]{3,2,1,0:T(1,128)} %bitcast.101, f32[1,16,1,512]{3,2,1,0:T(1,128)} %copy-done.27, bf16[4,8192,512]{2,1,0:T(8,128)(2,1)} %bitcast.114, ...), custom_call_target="tpu_custom_call" | custom-call | flops 234881024 | bytes 262144 | tf_op jit(solution)/shard_map/expert_down/pallas_call | solution.py:626
  1095.7 64.8 %expert_gradients.5 = (f32[32,512,512]{2,1,0:T(8,128)}, f32[32,512,512]{2,1,0:T(8,128)}, f32[32,512,512]{2,1,0:T(8,128)}) custom-call(s32[4,33]{1,0:T(4,128)} %copy.133.offset_ref, bf16[4,1,64,128,512]{4,3,2,1,0:T(8,128)(2,1)} %bitcast.126, bf16[4,64,128,512]{3,2,1,0:T(8,128)(2,1)} %bitcast.120, ...), custom_call_target="tpu_custom_call", output_to_operand_aliasing={{0}: (5, {}), {1}: (6, {}), {2}: (7, {})} | custom-call | flops 603979776 | bytes 1835008 | tf_op jit(solution)/shard_map/expert_gradients/pallas_call | solution.py:799
  (353 shorter events, 280.7 us)
Async XLA Ops:
  14.3 87.7 %reduce-scatter.5.cloned.1.call-start = ((), (), s32[]{:S(2)}) async-start(), calls=%async_computation.4 | async-start | bytes 7864320 | tf_op jit(solution)/shard_map/reduce_scatter | solution.py:991
  42.2 81.3 %all-gather.11.cloned.1.call-start = ((), (), s32[]{:S(2)}) async-start(), calls=%async_computation.5 | async-start | bytes 4718592 | tf_op jit(solution)/shard_map/all_gather | solution.py:980
  43.0 103.0 %all-gather.21.cloned.1.call-start = ((), (), s32[]{:S(2)}) async-start(), calls=%async_computation.13 | async-start | bytes 2621440 | tf_op jit(solution)/shard_map/all_gather | solution.py:1024
  123.6 120.6 %reduce-scatter.9.cloned.1.call-start = ((), (), s32[]{:S(2)}) async-start(), calls=%async_computation.7 | async-start | bytes 10485760 | tf_op jit(solution)/shard_map/reduce_scatter | solution.py:1025
  124.1 294.3 %reduce-scatter.7.cloned.1.call-start = ((), (), s32[]{:S(2)}) async-start(), calls=%async_computation.6 | async-start | bytes 10485760 | tf_op jit(solution)/shard_map/reduce_scatter | solution.py:1055
  150.9 25.5 %collective-permute-start.3 = (bf16[1024,512]{0,1:T(8,128)(2,1)}, bf16[1024,512]{0,1:T(8,128)(2,1)S(1)}, u32[]{:S(2)}, u32[]{:S(2)}) collective-permute-start(bf16[1024,512]{0,1:T(8,128)(2,1)} %copy.125), channel_id=1, source_target_pairs={{0,1},{1,0},{2,3},{3,2},{4,5},{5,4},{6,7},{7,6},{8,9},{9,8},{10,11... | collective-permute-start | bytes 3145736 | tf_op jit(solution)/shard_map/ppermute | solution.py:910
  223.5 277.8 %all-gather.13.cloned.1.call-start = ((), (), s32[]{:S(2)}) async-start(), calls=%async_computation.8 | async-start | bytes 35651584 | tf_op jit(solution)/shard_map/all_gather | solution.py:1083
  244.2 257.3 %reduce-scatter.11.cloned.1.call-start = ((), (), s32[]{:S(2)}) async-start(), calls=%async_computation.9 | async-start | bytes 10485760 | tf_op jit(solution)/shard_map/reduce_scatter | solution.py:1055
  244.9 318.3 %all-gather.15.cloned.1.call-start = ((), (), s32[]{:S(2)}) async-start(), calls=%async_computation.10 | async-start | bytes 10485760 | tf_op jit(solution)/shard_map/all_gather | solution.py:1093
  249.2 57.1 %collective-permute-start.9 = (bf16[1024,512]{0,1:T(8,128)(2,1)}, bf16[1024,512]{0,1:T(8,128)(2,1)}, u32[]{:S(2)}, u32[]{:S(2)}) collective-permute-start(bf16[1024,512]{0,1:T(8,128)(2,1)} %get-tuple-element.212), channel_id=1, source_target_pairs={{0,24},{8,0},{16,8},{24,16},{1,25},{9,1},{17,9},{25,17},{2,26},{10... | collective-permute-start | bytes 3145736 | tf_op jit(solution)/shard_map/ppermute | solution.py:882
  267.7 33.0 %collective-permute-start.8 = (f32[1,8192]{1,0:T(1,128)S(1)}, f32[1,8192]{1,0:T(1,128)}, u32[]{:S(2)}, u32[]{:S(2)}) collective-permute-start(f32[1,8192]{1,0:T(1,128)S(1)} %bitcast.102), channel_id=1, source_target_pairs={{0,8},{8,16},{16,24},{24,0},{1,9},{9,17},{17,25},{25,1},{2,10},{10... | collective-permute-start | bytes 98312 | tf_op jit(solution)/shard_map/ppermute | solution.py:882
  269.3 33.4 %collective-permute-start.7 = (f32[1,8192]{1,0:T(1,128)S(1)}, f32[1,8192]{1,0:T(1,128)S(1)}, u32[]{:S(2)}, u32[]{:S(2)}) collective-permute-start(f32[1,8192]{1,0:T(1,128)S(1)} %bitcast.103), channel_id=1, source_target_pairs={{0,16},{8,24},{16,0},{24,8},{1,17},{9,25},{17,1},{25,9},{2,18},{10... | collective-permute-start | bytes 98312 | tf_op jit(solution)/shard_map/ppermute | solution.py:882
  271.7 31.2 %collective-permute-start.6 = (f32[1,8192]{1,0:T(1,128)S(1)}, f32[1,8192]{1,0:T(1,128)S(1)}, u32[]{:S(2)}, u32[]{:S(2)}) collective-permute-start(f32[1,8192]{1,0:T(1,128)S(1)} %bitcast.104), channel_id=1, source_target_pairs={{0,24},{8,0},{16,8},{24,16},{1,25},{9,1},{17,9},{25,17},{2,26},{10... | collective-permute-start | bytes 98312 | tf_op jit(solution)/shard_map/ppermute | solution.py:882
  273.2 117.7 %collective-permute-start.10 = (bf16[1024,512]{0,1:T(8,128)(2,1)}, bf16[1024,512]{0,1:T(8,128)(2,1)S(1)}, u32[]{:S(2)}, u32[]{:S(2)}) collective-permute-start(bf16[1024,512]{0,1:T(8,128)(2,1)} %get-tuple-element.212), channel_id=1, source_target_pairs={{0,16},{8,24},{16,0},{24,8},{1,17},{9,25},{17,1},{25,9},{2,18},{10... | collective-permute-start | bytes 3145736 | tf_op jit(solution)/shard_map/ppermute | solution.py:882
  300.7 91.8 %collective-permute-start.11 = (bf16[1024,512]{0,1:T(8,128)(2,1)}, bf16[1024,512]{0,1:T(8,128)(2,1)}, u32[]{:S(2)}, u32[]{:S(2)}) collective-permute-start(bf16[1024,512]{0,1:T(8,128)(2,1)} %get-tuple-element.212), channel_id=1, source_target_pairs={{0,8},{8,16},{16,24},{24,0},{1,9},{9,17},{17,25},{25,1},{2,10},{10... | collective-permute-start | bytes 3145736 | tf_op jit(solution)/shard_map/ppermute | solution.py:882
  501.3 230.1 %all-gather.17.cloned.1.call-start = ((), (), s32[]{:S(2)}) async-start(), calls=%async_computation.11 | async-start | bytes 35651584 | tf_op jit(solution)/shard_map/all_gather | solution.py:1099
  563.2 337.8 %all-gather.19.cloned.1.call-start = ((), (), s32[]{:S(2)}) async-start(), calls=%async_computation.12 | async-start | bytes 35651584 | tf_op jit(solution)/shard_map/all_gather | solution.py:1099
  731.5 278.5 %all-gather.23.cloned.1.call-start = ((), (), s32[]{:S(2)}) async-start(), calls=%async_computation.14 | async-start | bytes 7864320 | tf_op jit(solution)/shard_map/all_gather | solution.py:1207
  783.7 102.5 %collective-permute-start.12 = (bf16[1024,512]{0,1:T(8,128)(2,1)S(1)}, bf16[1024,512]{0,1:T(8,128)(2,1)}, u32[]{:S(2)}, u32[]{:S(2)}) collective-permute-start(bf16[1024,512]{0,1:T(8,128)(2,1)S(1)} %fusion.3), channel_id=1, source_target_pairs={{0,1},{1,0},{2,3},{3,2},{4,5},{5,4},{6,7},{7,6},{8,9},{9,8},{10,11... | collective-permute-start | bytes 3145736 | tf_op jit(solution)/shard_map/ppermute | solution.py:910
  921.4 25.4 %collective-permute-start.17 = (bf16[1056,512]{1,0:T(8,128)(2,1)}, bf16[1056,512]{1,0:T(8,128)(2,1)}, u32[]{:S(2)}, u32[]{:S(2)}) collective-permute-start(bf16[1056,512]{1,0:T(8,128)(2,1)} %pad_maximum_fusion.1), channel_id=1, source_target_pairs={{0,8},{8,0},{16,24},{24,16},{1,9},{9,1},{17,25},{25,17},{2,10},{10... | collective-permute-start | bytes 3244040 | tf_op jit(solution)/shard_map/ppermute | solution.py:852
  958.4 205.6 %all-reduce.3.cloned.1.call-start = ((), (), s32[]{:S(2)}) async-start(), calls=%async_computation.15 | async-start | bytes 6291456 | tf_op jit(solution)/shard_map/psum | solution.py:1213
  958.9 49.7 %collective-permute-start.18 = (bf16[1056,512]{1,0:T(8,128)(2,1)S(1)}, bf16[1056,512]{1,0:T(8,128)(2,1)S(1)}, u32[]{:S(2)}, u32[]{:S(2)}) collective-permute-start(bf16[1056,512]{1,0:T(8,128)(2,1)S(1)} %fusion.54), channel_id=1, source_target_pairs={{0,16},{8,24},{16,0},{24,8},{1,17},{9,25},{17,1},{25,9},{2,18},{10... | collective-permute-start | bytes 3244040 | tf_op jit(solution)/shard_map/ppermute | solution.py:852
  1028.5 42.1 %collective-permute-start.19 = (bf16[512,512]{0,1:T(8,128)(2,1)}, bf16[512,512]{0,1:T(8,128)(2,1)}, u32[]{:S(2)}, u32[]{:S(2)}) collective-permute-start(bf16[512,512]{0,1:T(8,128)(2,1)} %bitcast.51), channel_id=1, source_target_pairs={{0,1},{1,0},{2,3},{3,2},{4,5},{5,4},{6,7},{7,6},{8,9},{9,8},{10,11... | collective-permute-start | bytes 1572872 | tf_op jit(solution)/shard_map/ppermute | solution.py:920
  1082.1 79.7 %collective-permute-start.20 = (bf16[512,512]{0,1:T(8,128)(2,1)}, bf16[512,512]{0,1:T(8,128)(2,1)}, u32[]{:S(2)}, u32[]{:S(2)}) collective-permute-start(bf16[512,512]{0,1:T(8,128)(2,1)} %bitcast.54), channel_id=1, source_target_pairs={{0,1},{1,0},{2,3},{3,2},{4,5},{5,4},{6,7},{7,6},{8,9},{9,8},{10,11... | collective-permute-start | bytes 1572872 | tf_op jit(solution)/shard_map/ppermute | solution.py:920
  (86 other events, 1525.0 us)
Sparse Core Ops, SparseCore 0:
  14.4 11.4 sort.11.cloned.1.call-done
  45.4 75.1 all-gather.10
  244.3 257.0 all-gather.12
  563.3 168.0 all-gather.16
  732.9 168.0 all-gather.18
  (1 shorter events, 0.0 us)
Sparse Core Ops, SparseCore 1:
  42.3 59.7 reduce-scatter.4
  123.7 22.3 all-gather.20
  148.6 71.7 reduce-scatter.8
  223.6 99.7 reduce-scatter.6
  326.7 101.3 reduce-scatter.10
  501.4 61.7 all-gather.14
  958.5 46.3 all-gather.22
  1019.1 121.6 all-reduce.2

commit v4 on v3

--- a/solution.py
+++ b/solution.py
@@ -590,8 +590,8 @@
     )(offsets, base, pair[0][0], pair[1][0], hd, gate, up, tokens_of.reshape(shape), scale.reshape(shape), *before)
 
 
-def down_kernel(offset_ref, base_ref, down_ref, token_ref, scale_ref, *rest):
-    sources, (o_ref, made_ref) = rest[:-2], rest[-2:]
+def down_kernel(start, count, offset_ref, base_ref, down_ref, token_ref, scale_ref, *rest):
+    sources, (*before_ref, o_ref, made_ref) = rest[: 2 * count], rest[2 * count :]
     half = sources[0].shape[2]
 
     def run(i, expert, base, low, high):
@@ -602,17 +602,18 @@
             gate = 0.5 * gate_ref[0, rows, :].astype(F32)
             silu = gate + gate * jnp.tanh(gate)
             hidden.append((silu * up_ref[0, rows, :].astype(F32)).astype(BF))
-        made = dot(jnp.concatenate(hidden, axis=1), down_ref[i])
+        units = slice(start * half, (start + count) * half)
+        made = dot(jnp.concatenate(hidden, axis=1), down_ref[i, units, :])
         made_ref[rows, :] = jnp.where(keep, made.astype(BF), made_ref[rows, :])
 
     each_expert(offset_ref, made_ref.shape[0], run)
 
     @pl.when(pl.program_id(1) == pl.num_programs(1) - 1)
     def _():
-        combine(token_ref, scale_ref, made_ref, o_ref)
-
-
-def expert_down(offsets, bases, pairs, half, down, tokens_of, scale, tokens):
+        combine(token_ref, scale_ref, made_ref, o_ref, *before_ref)
+
+
+def expert_down(offsets, bases, pairs, half, down, tokens_of, scale, tokens, start, before):
     groups, rows = tokens_of.shape
     experts, units, depth = down.shape
     line = once((1, rows // WIDE, 1, WIDE), lambda g, e, o, b: (g, 0, 0, 0))
@@ -621,10 +622,11 @@
     def source(i, column):
         return once((1, rows, half), lambda g, e, o, b: (b[i] + g, 0, column))
 
+    total = once((1, tokens, depth), lambda g, e, o, b: (g, 0, 0))
     specs = [source(i, column) for i, pair in enumerate(pairs) for _, column in pair]
     sources = [value for pair in pairs for value, _ in pair]
     return pl.pallas_call(
-        down_kernel,
+        functools.partial(down_kernel, start, len(pairs)),
         grid_spec=pltpu.PrefetchScalarGridSpec(
             num_scalar_prefetch=2,
             grid=(groups, experts // PACK),
@@ -633,8 +635,9 @@
                 line,
                 line,
                 *specs,
+                *[total] * len(before),
             ],
-            out_specs=once((1, tokens, depth), lambda g, e, o, b: (g, 0, 0)),
+            out_specs=total,
             scratch_shapes=[pltpu.VMEM((rows, depth), BF)],
         ),
         out_shape=jax.ShapeDtypeStruct((groups, tokens, depth), F32),
@@ -643,7 +646,7 @@
             groups * rows * depth * (3 * units + 2 * tokens), 4 * groups * rows * units
         ),
         name="expert_down",
-    )(offsets, bases, down, tokens_of.reshape(shape), scale.reshape(shape), *sources)
+    )(offsets, bases, down, tokens_of.reshape(shape), scale.reshape(shape), *sources, *before)
 
 
 def gradient_kernel(part, start, pieces, aliased, offset_ref, *rest):
@@ -1075,7 +1078,7 @@
             before,
         )
 
-    zero = jnp.zeros((), jnp.int32)
+    zero, down_part = jnp.zeros((), jnp.int32), []
     if gathered:
         every = ("dp", "row")
         all_scales = gather_planes(scale)
@@ -1094,12 +1097,27 @@
         shares[0], last = in_order(shares[0], last)
         last = last.reshape(groups, rows, 2 * half)
         back = back_of(parts - 1, [(last, 0), (last, 1)], zero, hidden_rows, base)
+        if parts > 1:
+            down_part = [
+                expert_down(
+                    offsets,
+                    zero[None],
+                    [[(last, 0), (last, 1)]],
+                    half,
+                    down_weight,
+                    tokens_of,
+                    scale,
+                    sub,
+                    parts - 1,
+                    (),
+                )
+            ]
         pairs, bases, all_pairs = [], [], []
         for part in range(parts):
             taken = lax.all_gather(shares[part], every, axis=0, tiled=True)
             if part + 1 < parts:
-                shares[part + 1], taken, back, second_turned, delta_turned = in_order(
-                    shares[part + 1], taken, back, second_turned, delta_turned
+                shares[part + 1], taken, back, second_turned, delta_turned, *down_part = in_order(
+                    shares[part + 1], taken, back, second_turned, delta_turned, *down_part
                 )
                 whole = taken.reshape(segment_count, rows, 2 * half)
                 pairs.append([(whole, 0), (whole, 1)])
@@ -1214,7 +1232,10 @@
     first_delta = share_columns(
         project_back(joint_group, query_weight, key_weight, value_weight, spans, slots)
     )
-    expert_out = expert_down(offsets, bases, pairs, half, down_weight, tokens_of, scale, sub)
+    left = parts - len(down_part)
+    expert_out = expert_down(
+        offsets, bases, pairs[:left], half, down_weight, tokens_of, scale, sub, 0, down_part
+    )
     first_delta, expert_out = in_order(first_delta, expert_out)
 
     own_residual = residual_in.astype(F32)

time: 1190 us -> 1180 us (level)
  waiting for transfers between devices: 371 us -> 342 us
  Pallas kernels: 546 us -> 570 us
    all_gather x2, waiting for transfers between devices: 36.1 us -> 7.55 us  [on_device(): taken = lax.all_gather(shares[part], every, axis=0, tiled=True)]
    pallas_call x1 -> x2, Pallas kernels: 34.3 us -> 58 us  [expert_down(): pl.pallas_call(functools.partial(down_kernel, start, len(pairs)), grid_sp...]
    unnamed x159 -> x163, local copies, waits for them, and re-layouts: 31.6 us -> 31.7 us
  transfers between devices with their start and end apart: 36 -> 36, of which waited for: 20 -> 20; matrix products, arithmetic and copies ran while one was open for 10% -> 10% of each run, Pallas kernels for 45% -> 47%
where the time goes in v4:
time: 1180 us; the launch traced here: 1170 us
  Pallas kernels  570 us (48%)
  waiting for transfers between devices  342 us (29%)
  local copies, waits for them, and re-layouts  85.6 us (7%)
  other arithmetic  56.2 us (5%)
  blocking collectives  56.1 us (5%)
  starting transfers between devices  36.1 us (3%)
  between operations  16.6 us (1%)
    pallas_call x3, Pallas kernels, expert_gradients(): pl.pallas_call(functools.partial(gradient_kernel, part, start, len(pieces...  205 us
    ppermute x6, waiting for transfers between devices, gather_planes(): lax.ppermute(value, 'dp', [(i, (i - apart) % count) for i in range(count)])  104 us
    pallas_call x1, Pallas kernels, dispatch_turned(): pl.pallas_call(dispatch_turned_kernel, grid=(groups, rows // WIDE), in_sp...  87.6 us
    pallas_call x2, Pallas kernels, expert_back(): pl.pallas_call(functools.partial(expert_back_kernel, part), grid_spec=plt...  86.4 us
    all_gather x1, waiting for transfers between devices, on_device(): all_hidden = lax.all_gather(hidden_delta, every, axis=0, tiled=True)  82.9 us
    all_gather x1, waiting for transfers between devices, on_device(): last = lax.all_gather(shares[-1], 'row', axis=0, tiled=True)  61.7 us
    pallas_call x2, Pallas kernels, expert_down(): pl.pallas_call(functools.partial(down_kernel, start, len(pairs)), grid_sp...  58 us
    pallas_call x2, Pallas kernels, gate_up(): pl.pallas_call(gate_up_kernel, grid_spec=pltpu.PrefetchScalarGridSpec(num...  39.9 us
  transfers between devices with their start and end apart: 36, of which 20 were waited for; matrix products, arithmetic and copies ran while one was open for 10% of the time, Pallas kernels for 47%

profile of v4, /device:TPU:0, one launch (start us, length us, event | category | flops | bytes accessed | tf_op | source)
XLA Modules:
  0.0 1171.7 jit_solution(241269883068749664)
XLA Ops:
  14.4 9.9 collective-permute-done
  46.0 13.9 %all-gather.2 = s32[4,1,8192]{2,1,0:T(1,128)S(1)} all-gather(s32[1,1,8192]{2,1,0:T(1,128)} %bitcast.148), channel_id=1, replica_groups=mesh['dp'=4,'row'=4,'col'=2] {'dp'}, dimensions={0}, use_global_device_ids=true | all-gather | bytes 163840 | tf_op jit(solution)/shard_map/all_gather | solution.py:984
  65.9 13.2 %dispatch.2.x_ref = bf16[1,8192,512]{2,1,0:T(8,128)(2,1)} custom-call(s32[1,16,4,128]{3,2,1,0:T(4,128)S(1)} %bitcast.96, bf16[1,1024,512]{2,1,0:T(8,128)(2,1)S(1)} %copy.123.source_ref), custom_call_target="tpu_custom_call" | custom-call | flops 134217728 | bytes 131072 | tf_op jit(solution)/shard_map/dispatch/pallas_call | solution.py:336
  79.0 20.3 %hidden_back.1 = bf16[1,8192,512]{2,1,0:T(8,128)(2,1)} custom-call(s32[1,33]{1,0:T(1,128)} %bitcast.166, bf16[1,8192,512]{2,1,0:T(8,128)(2,1)} %dispatch.2.x_ref, bf16[32,512,512]{2,1,0:T(8,128)(2,1)} %down_ref.5), custom_call_target="tpu_custom_call" | custom-call | flops 100663296 | bytes 131072 | tf_op jit(solution)/shard_map/hidden_back/pallas_call | solution.py:486
  124.7 21.3 %all-gather.21.cloned.1.call-done = bf16[4096,256]{1,0:T(8,128)(2,1)} async-done(((bf16[1024,256]{1,0:T(8,128)(2,1)}), bf16[4096,256]{1,0:T(8,128)(2,1)}) %all-gather.21.cloned.1.call-update) | async-done | bytes 2097168 | tf_op jit(solution)/shard_map/all_gather | solution.py:1027
  152.4 24.0 %collective-permute-done.3 = bf16[1024,512]{0,1:T(8,128)(2,1)S(1)} collective-permute-done((bf16[1024,512]{0,1:T(8,128)(2,1)}, bf16[1024,512]{0,1:T(8,128)(2,1)S(1)}, u32[]{:S(2)}, u32[]{:S(2)}) %collective-permute-start.3) | collective-permute-done | bytes 1048608 | tf_op jit(solution)/shard_map/ppermute | solution.py:913
  191.0 13.2 %dispatch.3.x_ref = bf16[1,8192,512]{2,1,0:T(8,128)(2,1)} custom-call(s32[1,16,4,128]{3,2,1,0:T(4,128)S(1)} %bitcast.97, bf16[1,1024,512]{2,1,0:T(8,128)(2,1)S(1)} %copy.127.source_ref), custom_call_target="tpu_custom_call" | custom-call | flops 134217728 | bytes 131072 | tf_op jit(solution)/shard_map/dispatch/pallas_call | solution.py:336
  204.2 19.4 %gate_up.2 = bf16[1,8192,512]{2,1,0:T(8,128)(2,1)} custom-call(s32[1,33]{1,0:T(1,128)} %bitcast.167, bf16[1,8192,512]{2,1,0:T(8,128)(2,1)} %dispatch.3.x_ref, bf16[32,512,512]{2,1,0:T(8,128)(2,1)} %gate_ref.7, bf16[32,512,512]{2,1,0:T(8,128)(2,1)} %up_ref.7), custom_call_target="tpu_custom_call" | custom-call | flops 100663296 | bytes 131072 | tf_op jit(solution)/shard_map/gate_up/pallas_call | solution.py:458
  223.6 20.6 %gate_up.3 = bf16[1,8192,512]{2,1,0:T(8,128)(2,1)} custom-call(s32[1,33]{1,0:T(1,128)} %bitcast.168, bf16[1,8192,512]{2,1,0:T(8,128)(2,1)} %dispatch.3.x_ref, bf16[32,512,512]{2,1,0:T(8,128)(2,1)} %gate_ref.7, bf16[32,512,512]{2,1,0:T(8,128)(2,1)} %up_ref.7), custom_call_target="tpu_custom_call" | custom-call | flops 100663296 | bytes 131072 | tf_op jit(solution)/shard_map/gate_up/pallas_call | solution.py:458
  256.8 10.9 pick.1.scale_ref
  280.4 19.8 %collective-permute-done.6 = f32[1,8192]{1,0:T(1,128)S(1)} collective-permute-done((f32[1,8192]{1,0:T(1,128)S(1)}, f32[1,8192]{1,0:T(1,128)S(1)}, u32[]{:S(2)}, u32[]{:S(2)}) %collective-permute-start.6) | collective-permute-done | bytes 32800 | tf_op jit(solution)/shard_map/ppermute | solution.py:885
  309.6 81.3 %collective-permute-done.10 = bf16[1024,512]{0,1:T(8,128)(2,1)S(1)} collective-permute-done((bf16[1024,512]{0,1:T(8,128)(2,1)}, bf16[1024,512]{0,1:T(8,128)(2,1)S(1)}, u32[]{:S(2)}, u32[]{:S(2)}) %collective-permute-start.10) | collective-permute-done | bytes 1048608 | tf_op jit(solution)/shard_map/ppermute | solution.py:885
  418.5 82.9 %all-gather.13.cloned.1.call-done = bf16[32768,512]{1,0:T(8,128)(2,1)} async-done(((bf16[2048,512]{1,0:T(8,128)(2,1)}), bf16[32768,512]{1,0:T(8,128)(2,1)}) %all-gather.13.cloned.1.call-update) | async-done | bytes 33554448 | tf_op jit(solution)/shard_map/all_gather | solution.py:1086
  501.5 61.7 %all-gather.15.cloned.1.call-done = bf16[8192,512]{1,0:T(8,128)(2,1)} async-done(((bf16[2048,512]{1,0:T(8,128)(2,1)}), bf16[8192,512]{1,0:T(8,128)(2,1)}) %all-gather.15.cloned.1.call-update) | async-done | bytes 8388624 | tf_op jit(solution)/shard_map/all_gather | solution.py:1096
  566.5 87.6 %dispatch_turned.1 = (bf16[4,64,512,128]{3,2,1,0:T(8,128)(2,1)}, bf16[4,64,512,128]{3,2,1,0:T(8,128)(2,1)}) custom-call(s32[4,16,1,512]{3,2,1,0:T(1,128)S(1)} %reshape.280.token_ref, f32[4,16,1,512]{3,2,1,0:T(1,128)S(1)} %reshape.281.scale_ref, bf16[4,512,1024]{2,1,0:T(8,128)(2,1)S(1)} %bitcast.89, bf16[4,512,1024]{2,1,0:T(8,128)(2,1)} %bitcast.133), custom_call_target="tpu_custom_call" | custom-call | flops 1073741824 | bytes 1048576 | tf_op jit(solution)/shard_map/dispatch_turned/pallas_call | solution.py:367
  654.2 28.7 %expert_down.2.rest_2_ = f32[1,1024,512]{2,1,0:T(8,128)} custom-call(s32[1,33]{1,0:T(1,128)} %bitcast.169, s32[1]{0:T(128)} %constant.154.clone.1.base_ref, bf16[32,512,512]{2,1,0:T(8,128)(2,1)} %down_ref.5, s32[1,16,1,512]{3,2,1,0:T(1,128)} %bitcast.99, f32[1,16,1,512]{3,2,1,0:T(1,128)} %copy-done.27, bf16[1,8192,512]{2,1,0:T(8,128)(2,1)} %bitcast.122, ...), custom_call_target="tpu_custom_call" | custom-call | flops 234881024 | bytes 262144 | tf_op jit(solution)/shard_map/expert_down/pallas_call | solution.py:628
  682.9 42.6 %expert_back.2.rest_0_ = f32[1,1024,640]{2,1,0:T(8,128)} custom-call(s32[1,33]{1,0:T(1,128)} %bitcast.170, s32[2]{0:T(128)} %pad_add_fusion._, bf16[1,8192,512]{2,1,0:T(8,128)(2,1)} %bitcast.124, bf16[1,8192,512]{2,1,0:T(8,128)(2,1)} %bitcast.125, bf16[4,8192,512]{2,1,0:T(8,128)(2,1)} %bitcast.117, bf16[32,512,512]{2,1,0:T(8,128)(2,1)} %gate_ref.7, ...), custom_call_target="tpu_custom_call" | custom-call | flops 234881024 | bytes 262144 | tf_op jit(solution)/shard_map/expert_back/pallas_call | solution.py:564
  732.3 43.8 %expert_back.3 = f32[1,1024,640]{2,1,0:T(8,128)} custom-call(s32[1,33]{1,0:T(1,128)} %bitcast.171, s32[2]{0:T(128)} %pad_add_fusion.2._, bf16[4,8192,512]{2,1,0:T(8,128)(2,1)} %bitcast.112, bf16[4,8192,512]{2,1,0:T(8,128)(2,1)} %bitcast.113, bf16[4,8192,512]{2,1,0:T(8,128)(2,1)} %bitcast.118, bf16[32,512,512]{2,1,0:T(8,128)(2,1)} %gate_ref.7, ...), custom_call_target="tpu_custom_call" | custom-call | flops 234881024 | bytes 262144 | tf_op jit(solution)/shard_map/expert_back/pallas_call | solution.py:564
  787.1 98.9 %expert_gradients.3 = (f32[32,512,512]{2,1,0:T(8,128)}, f32[32,512,512]{2,1,0:T(8,128)}, f32[32,512,512]{2,1,0:T(8,128)}) custom-call(s32[4,33]{1,0:T(4,128)} %copy.133.offset_ref, bf16[4,1,64,128,512]{4,3,2,1,0:T(8,128)(2,1)} %bitcast.114, bf16[4,64,128,512]{3,2,1,0:T(8,128)(2,1)} %bitcast.119, bf16[4,64,512,128]{3,2,1,0:T(8,128)(2,1)} %get-tuple-element.97.rest_2_, ...), custom_call_target="tpu_custom_call" | custom-call | flops 603979776 | bytes 1835008 | tf_op jit(solution)/shard_map/expert_gradients/pallas_call | solution.py:802
  923.0 10.1 collective-permute-done.14
  934.5 7.5 attend_back.1
  961.6 42.1 %expert_gradients.4 = (f32[32,512,512]{2,1,0:T(8,128)}, f32[32,512,512]{2,1,0:T(8,128)}, f32[32,512,512]{2,1,0:T(8,128)}) custom-call(s32[4,33]{1,0:T(4,128)} %copy.133.offset_ref, bf16[4,1,64,128,512]{4,3,2,1,0:T(8,128)(2,1)} %bitcast.126, bf16[4,64,128,512]{3,2,1,0:T(8,128)(2,1)} %bitcast.120, ...), custom_call_target="tpu_custom_call", output_to_operand_aliasing={{0}: (5, {}), {1}: (6, {}), {2}: (7, {})} | custom-call | flops 603979776 | bytes 1835008 | tf_op jit(solution)/shard_map/expert_gradients/pallas_call | solution.py:802
  1030.6 29.3 %expert_down.3 = f32[1,1024,512]{2,1,0:T(8,128)} custom-call(s32[1,33]{1,0:T(1,128)} %bitcast.172, s32[2]{0:T(128)} %pad_add_fusion.1.base_ref, bf16[32,512,512]{2,1,0:T(8,128)(2,1)} %down_ref.5, s32[1,16,1,512]{3,2,1,0:T(1,128)} %bitcast.102, f32[1,16,1,512]{3,2,1,0:T(1,128)} %copy-done.27, bf16[4,8192,512]{2,1,0:T(8,128)(2,1)} %bitcast.115, ...), custom_call_target="tpu_custom_call" | custom-call | flops 234881024 | bytes 262144 | tf_op jit(solution)/shard_map/expert_down/pallas_call | solution.py:628
  1090.8 64.1 %expert_gradients.5 = (f32[32,512,512]{2,1,0:T(8,128)}, f32[32,512,512]{2,1,0:T(8,128)}, f32[32,512,512]{2,1,0:T(8,128)}) custom-call(s32[4,33]{1,0:T(4,128)} %copy.133.offset_ref, bf16[4,1,64,128,512]{4,3,2,1,0:T(8,128)(2,1)} %bitcast.127, bf16[4,64,128,512]{3,2,1,0:T(8,128)(2,1)} %bitcast.121, ...), custom_call_target="tpu_custom_call", output_to_operand_aliasing={{0}: (5, {}), {1}: (6, {}), {2}: (7, {})} | custom-call | flops 603979776 | bytes 1835008 | tf_op jit(solution)/shard_map/expert_gradients/pallas_call | solution.py:802
  (358 shorter events, 287.9 us)
Async XLA Ops:
  14.3 87.7 %reduce-scatter.5.cloned.1.call-start = ((), (), s32[]{:S(2)}) async-start(), calls=%async_computation.4 | async-start | bytes 7864320 | tf_op jit(solution)/shard_map/reduce_scatter | solution.py:994
  42.2 81.3 %all-gather.11.cloned.1.call-start = ((), (), s32[]{:S(2)}) async-start(), calls=%async_computation.5 | async-start | bytes 4718592 | tf_op jit(solution)/shard_map/all_gather | solution.py:983
  43.0 103.0 %all-gather.21.cloned.1.call-start = ((), (), s32[]{:S(2)}) async-start(), calls=%async_computation.13 | async-start | bytes 2621440 | tf_op jit(solution)/shard_map/all_gather | solution.py:1027
  123.6 120.6 %reduce-scatter.9.cloned.1.call-start = ((), (), s32[]{:S(2)}) async-start(), calls=%async_computation.7 | async-start | bytes 10485760 | tf_op jit(solution)/shard_map/reduce_scatter | solution.py:1028
  124.2 294.4 %reduce-scatter.7.cloned.1.call-start = ((), (), s32[]{:S(2)}) async-start(), calls=%async_computation.6 | async-start | bytes 10485760 | tf_op jit(solution)/shard_map/reduce_scatter | solution.py:1058
  150.9 25.5 %collective-permute-start.3 = (bf16[1024,512]{0,1:T(8,128)(2,1)}, bf16[1024,512]{0,1:T(8,128)(2,1)S(1)}, u32[]{:S(2)}, u32[]{:S(2)}) collective-permute-start(bf16[1024,512]{0,1:T(8,128)(2,1)} %copy.125), channel_id=1, source_target_pairs={{0,1},{1,0},{2,3},{3,2},{4,5},{5,4},{6,7},{7,6},{8,9},{9,8},{10,11... | collective-permute-start | bytes 3145736 | tf_op jit(solution)/shard_map/ppermute | solution.py:913
  223.5 277.8 %all-gather.13.cloned.1.call-start = ((), (), s32[]{:S(2)}) async-start(), calls=%async_computation.8 | async-start | bytes 35651584 | tf_op jit(solution)/shard_map/all_gather | solution.py:1086
  244.2 257.3 %reduce-scatter.11.cloned.1.call-start = ((), (), s32[]{:S(2)}) async-start(), calls=%async_computation.9 | async-start | bytes 10485760 | tf_op jit(solution)/shard_map/reduce_scatter | solution.py:1058
  245.0 318.3 %all-gather.15.cloned.1.call-start = ((), (), s32[]{:S(2)}) async-start(), calls=%async_computation.10 | async-start | bytes 10485760 | tf_op jit(solution)/shard_map/all_gather | solution.py:1096
  249.3 58.0 %collective-permute-start.9 = (bf16[1024,512]{0,1:T(8,128)(2,1)}, bf16[1024,512]{0,1:T(8,128)(2,1)}, u32[]{:S(2)}, u32[]{:S(2)}) collective-permute-start(bf16[1024,512]{0,1:T(8,128)(2,1)} %get-tuple-element.214), channel_id=1, source_target_pairs={{0,24},{8,0},{16,8},{24,16},{1,25},{9,1},{17,9},{25,17},{2,26},{10... | collective-permute-start | bytes 3145736 | tf_op jit(solution)/shard_map/ppermute | solution.py:885
  267.8 32.4 %collective-permute-start.6 = (f32[1,8192]{1,0:T(1,128)S(1)}, f32[1,8192]{1,0:T(1,128)S(1)}, u32[]{:S(2)}, u32[]{:S(2)}) collective-permute-start(f32[1,8192]{1,0:T(1,128)S(1)} %bitcast.103), channel_id=1, source_target_pairs={{0,24},{8,0},{16,8},{24,16},{1,25},{9,1},{17,9},{25,17},{2,26},{10... | collective-permute-start | bytes 98312 | tf_op jit(solution)/shard_map/ppermute | solution.py:885
  271.2 32.6 %collective-permute-start.7 = (f32[1,8192]{1,0:T(1,128)S(1)}, f32[1,8192]{1,0:T(1,128)S(1)}, u32[]{:S(2)}, u32[]{:S(2)}) collective-permute-start(f32[1,8192]{1,0:T(1,128)S(1)} %bitcast.104), channel_id=1, source_target_pairs={{0,16},{8,24},{16,0},{24,8},{1,17},{9,25},{17,1},{25,9},{2,18},{10... | collective-permute-start | bytes 98312 | tf_op jit(solution)/shard_map/ppermute | solution.py:885
  271.2 32.6 %collective-permute-start.8 = (f32[1,8192]{1,0:T(1,128)S(1)}, f32[1,8192]{1,0:T(1,128)}, u32[]{:S(2)}, u32[]{:S(2)}) collective-permute-start(f32[1,8192]{1,0:T(1,128)S(1)} %bitcast.105), channel_id=1, source_target_pairs={{0,8},{8,16},{16,24},{24,0},{1,9},{9,17},{17,25},{25,1},{2,10},{10... | collective-permute-start | bytes 98312 | tf_op jit(solution)/shard_map/ppermute | solution.py:885
  272.3 118.5 %collective-permute-start.10 = (bf16[1024,512]{0,1:T(8,128)(2,1)}, bf16[1024,512]{0,1:T(8,128)(2,1)S(1)}, u32[]{:S(2)}, u32[]{:S(2)}) collective-permute-start(bf16[1024,512]{0,1:T(8,128)(2,1)} %get-tuple-element.214), channel_id=1, source_target_pairs={{0,16},{8,24},{16,0},{24,8},{1,17},{9,25},{17,1},{25,9},{2,18},{10... | collective-permute-start | bytes 3145736 | tf_op jit(solution)/shard_map/ppermute | solution.py:885
  300.2 92.4 %collective-permute-start.11 = (bf16[1024,512]{0,1:T(8,128)(2,1)}, bf16[1024,512]{0,1:T(8,128)(2,1)}, u32[]{:S(2)}, u32[]{:S(2)}) collective-permute-start(bf16[1024,512]{0,1:T(8,128)(2,1)} %get-tuple-element.214), channel_id=1, source_target_pairs={{0,8},{8,16},{16,24},{24,0},{1,9},{9,17},{17,25},{25,1},{2,10},{10... | collective-permute-start | bytes 3145736 | tf_op jit(solution)/shard_map/ppermute | solution.py:885
  501.4 230.1 %all-gather.17.cloned.1.call-start = ((), (), s32[]{:S(2)}) async-start(), calls=%async_computation.11 | async-start | bytes 35651584 | tf_op jit(solution)/shard_map/all_gather | solution.py:1117
  563.2 337.8 %all-gather.19.cloned.1.call-start = ((), (), s32[]{:S(2)}) async-start(), calls=%async_computation.12 | async-start | bytes 35651584 | tf_op jit(solution)/shard_map/all_gather | solution.py:1117
  731.5 278.7 %all-gather.23.cloned.1.call-start = ((), (), s32[]{:S(2)}) async-start(), calls=%async_computation.14 | async-start | bytes 7864320 | tf_op jit(solution)/shard_map/all_gather | solution.py:1225
  783.7 102.3 %collective-permute-start.12 = (bf16[1024,512]{0,1:T(8,128)(2,1)S(1)}, bf16[1024,512]{0,1:T(8,128)(2,1)}, u32[]{:S(2)}, u32[]{:S(2)}) collective-permute-start(bf16[1024,512]{0,1:T(8,128)(2,1)S(1)} %fusion.3), channel_id=1, source_target_pairs={{0,1},{1,0},{2,3},{3,2},{4,5},{5,4},{6,7},{7,6},{8,9},{9,8},{10,11... | collective-permute-start | bytes 3145736 | tf_op jit(solution)/shard_map/ppermute | solution.py:913
  921.5 25.5 %collective-permute-start.17 = (bf16[1056,512]{1,0:T(8,128)(2,1)}, bf16[1056,512]{1,0:T(8,128)(2,1)}, u32[]{:S(2)}, u32[]{:S(2)}) collective-permute-start(bf16[1056,512]{1,0:T(8,128)(2,1)} %pad_maximum_fusion.1), channel_id=1, source_target_pairs={{0,8},{8,0},{16,24},{24,16},{1,9},{9,1},{17,25},{25,17},{2,10},{10... | collective-permute-start | bytes 3244040 | tf_op jit(solution)/shard_map/ppermute | solution.py:855
  958.7 199.6 %all-reduce.3.cloned.1.call-start = ((), (), s32[]{:S(2)}) async-start(), calls=%async_computation.15 | async-start | bytes 6291456 | tf_op jit(solution)/shard_map/psum | solution.py:1231
  959.1 49.7 %collective-permute-start.18 = (bf16[1056,512]{1,0:T(8,128)(2,1)S(1)}, bf16[1056,512]{1,0:T(8,128)(2,1)S(1)}, u32[]{:S(2)}, u32[]{:S(2)}) collective-permute-start(bf16[1056,512]{1,0:T(8,128)(2,1)S(1)} %fusion.54), channel_id=1, source_target_pairs={{0,16},{8,24},{16,0},{24,8},{1,17},{9,25},{17,1},{25,9},{2,18},{10... | collective-permute-start | bytes 3244040 | tf_op jit(solution)/shard_map/ppermute | solution.py:855
  1028.8 36.9 %collective-permute-start.19 = (bf16[512,512]{0,1:T(8,128)(2,1)}, bf16[512,512]{0,1:T(8,128)(2,1)}, u32[]{:S(2)}, u32[]{:S(2)}) collective-permute-start(bf16[512,512]{0,1:T(8,128)(2,1)} %bitcast.51), channel_id=1, source_target_pairs={{0,1},{1,0},{2,3},{3,2},{4,5},{5,4},{6,7},{7,6},{8,9},{9,8},{10,11... | collective-permute-start | bytes 1572872 | tf_op jit(solution)/shard_map/ppermute | solution.py:923
  1077.4 78.7 %collective-permute-start.20 = (bf16[512,512]{0,1:T(8,128)(2,1)}, bf16[512,512]{0,1:T(8,128)(2,1)}, u32[]{:S(2)}, u32[]{:S(2)}) collective-permute-start(bf16[512,512]{0,1:T(8,128)(2,1)} %bitcast.54), channel_id=1, source_target_pairs={{0,1},{1,0},{2,3},{3,2},{4,5},{5,4},{6,7},{7,6},{8,9},{9,8},{10,11... | collective-permute-start | bytes 1572872 | tf_op jit(solution)/shard_map/ppermute | solution.py:923
  (88 other events, 1544.0 us)
Sparse Core Ops, SparseCore 0:
  14.4 11.4 sort.11.cloned.1.call-done
  45.4 75.1 all-gather.10
  244.3 257.0 all-gather.12
  563.4 168.0 all-gather.16
  732.9 168.0 all-gather.18
  (1 shorter events, 0.0 us)
Sparse Core Ops, SparseCore 1:
  42.3 59.7 reduce-scatter.4
  123.7 22.3 all-gather.20
  148.6 71.7 reduce-scatter.8
  223.6 99.7 reduce-scatter.6
  326.8 101.3 reduce-scatter.10
  501.5 61.7 all-gather.14
  958.8 46.2 all-gather.22
  1019.4 121.4 all-reduce.2
